TPU v7x, 256 devices: a whole 4x4x8 slice. The times are simulated.
256 devices in a mesh: phase: 16 (over x_hi, z), dp: 16 (over x_lo, y, core).
Axes of the slice: x: 4 (x_hi: 2, x_lo: 2; x = x_hi * 2 + x_lo), y: 4, z: 8, core: 2. Of those that a mesh axis runs over, the one named last changes fastest.
Arguments:
- hidden_flight: bfloat16 [16, 16, 48, 1536], P('phase', 'dp'), may hold values from -6 to 6
- latent_flight: bfloat16 [16, 16, 48, 64], P('phase', 'dp'), may hold values from -6 to 6
- key_cache: bfloat16 [16, 32, 256, 1536], P('phase', 'dp'), may hold values from -97 to 97
- value_cache: bfloat16 [16, 32, 256, 1536], P('phase', 'dp'), may hold values from -6 to 6
- text_keys: bfloat16 [16, 32, 256, 1536], P('phase', 'dp'), may hold values from -9 to 9
- text_values: bfloat16 [16, 32, 256, 1536], P('phase', 'dp'), may hold values from -6 to 6
- norm_gain: float32 [16, 1536], P('phase'), may hold values from 0.1 to 1.9
- w_qkv: bfloat16 [16, 1536, 4608], P('phase', 'dp'), may hold values from -0.15625 to 0.15625
- w_out: bfloat16 [16, 1536, 1536], P('phase', 'dp'), may hold values from -0.15625 to 0.15625
- embed_weight: bfloat16 [64, 1536], replicated, may hold values from -0.75 to 0.75
- embed_bias: float32 [1536], replicated, may hold values from -6 to 6
- head_weight: bfloat16 [1536, 64], replicated, may hold values from -0.21875 to 0.21875
- head_bias: float32 [64], replicated, may hold values from -6 to 6
- sigma_table: float32 [5], replicated, may hold values from 0 to 1, as said below
- step_index: int32 [32], P('dp'), may hold values from 0 to 3
- patch_lengths: int32 [32, 8], P('dp'), may hold values from 1 to 48, 256 in all within a row
Outputs:
- hidden_out: bfloat16 [16, 16, 48, 1536], P('phase', 'dp')
- latent_out: bfloat16 [16, 16, 48, 64], P('phase', 'dp')
- key_out: bfloat16 [16, 32, 256, 1536], P('phase', 'dp')
- value_out: bfloat16 [16, 32, 256, 1536], P('phase', 'dp')
Inputs may be any that keep to these rules, and one draw needn't show every extreme that they name: `patch_lengths`: the 8 lengths of one image sum to 256, and the longest of each image is exactly 48. `sigma_table`: entry 0 is 1, entry 4 is 0, and the entries fall from one to the next.
All inputs are finite; a program needn't handle non-finite values.
Results may differ from a plain program's by a relative error of at most 0.039.
Values may be sent and summed in bfloat16 or wider, within the bound.
No kernel may reach another device: no remote copies, remote signals or barrier semaphores. Data moves between devices by JAX's collectives and lax.ppermute only.
A program may use at most 128 MiB of HBM per device.

v0:
```python
import math

import jax
import jax.numpy as jnp
from jax import lax
from jax.sharding import PartitionSpec as P

HEAD_DIM = 128
TICKS = 3


epsilon = 1e-06


def shifted(value, axis, steps):
    count = lax.axis_size(axis)
    pairs = [(source, (source + steps) % count) for source in range(count)]
    return lax.ppermute(value, axis, pairs)


def normalize(row_block):
    widened = row_block.astype(jnp.float32)
    return widened * lax.rsqrt(jnp.mean(widened * widened, axis=-1, keepdims=True) + epsilon)


def place_rows(cached, fresh_rows, offset, inside):
    token_count = cached.shape[0]
    canvas = jnp.zeros((token_count + fresh_rows.shape[0], fresh_rows.shape[1]), fresh_rows.dtype)
    canvas = lax.dynamic_update_slice_in_dim(canvas, fresh_rows, offset, 0)
    return jnp.where(inside[:, None], canvas[:token_count], cached)


def attend(queries, key_rows, value_rows, allowed):
    row_count = queries.shape[0]
    inner_width = queries.shape[1]
    head_count = inner_width // HEAD_DIM
    query_heads = queries.reshape(row_count, head_count, HEAD_DIM)
    key_heads = key_rows.reshape(key_rows.shape[0], head_count, HEAD_DIM)
    value_heads = value_rows.reshape(value_rows.shape[0], head_count, HEAD_DIM)
    scores = jnp.einsum(
        "qhd,khd->hqk", query_heads, key_heads, preferred_element_type=jnp.float32
    ) * (1.0 / math.sqrt(HEAD_DIM))
    scores = jnp.where(allowed[None, None, :], scores, -jnp.inf)
    highest = jnp.max(scores, axis=-1, keepdims=True)
    raised = jnp.exp(scores - highest)
    attn_weights = (raised / jnp.sum(raised, axis=-1, keepdims=True)).astype(jnp.bfloat16)
    attended = jnp.einsum(
        "hqk,khd->qhd", attn_weights, value_heads, preferred_element_type=jnp.float32
    )
    return attended.reshape(row_count, inner_width).astype(jnp.bfloat16)


def shards(
    hidden_flight,
    latent_flight,
    key_cache,
    value_cache,
    text_keys,
    text_values,
    norm_gain,
    w_qkv,
    w_out,
    embed_weight,
    embed_bias,
    head_weight,
    head_bias,
    sigma_table,
    step_index,
    patch_lengths,
):
    sections = lax.axis_size("phase")
    section = lax.axis_index("phase")
    patches = patch_lengths.shape[1]
    hidden = hidden_flight[0, 0]
    latents = latent_flight[0, 0]
    keys_img = key_cache[0]
    values_img = value_cache[0]
    keys_txt = text_keys[0]
    values_txt = text_values[0]
    norm_scale = norm_gain[0]
    capacity = hidden.shape[0]
    inner_width = w_qkv.shape[2] // 3
    offsets = jnp.cumsum(patch_lengths, axis=1) - patch_lengths
    levels = jnp.arange(sigma_table.shape[0], dtype=jnp.int32)[None, :]
    sigma_now = jnp.sum(jnp.where(levels == step_index[:, None], sigma_table[None, :], 0.0), axis=1)
    sigma_next = jnp.sum(
        jnp.where(levels == step_index[:, None] + 1, sigma_table[None, :], 0.0), axis=1
    )
    sigma_jumps = sigma_next - sigma_now
    row_ids = jnp.arange(capacity, dtype=jnp.int32)
    token_ids = jnp.arange(keys_img.shape[1], dtype=jnp.int32)
    text_ok = jnp.ones((keys_txt.shape[1],), bool)
    first_proj = None
    qkv_full, out_full = (
        lax.all_gather(w_qkv, "dp", axis=1, tiled=True),
        lax.all_gather(w_out, "dp", axis=1, tiled=True),
    )
    qkv_full = qkv_full[0]
    out_full = out_full[0]
    for instant in range(TICKS):
        flight_slot = jnp.mod(instant - section, sections)
        picture = flight_slot // patches
        segment = flight_slot % patches
        length = lax.dynamic_slice(patch_lengths, (picture, segment), (1, 1))[0, 0]
        offset = lax.dynamic_slice(offsets, (picture, segment), (1, 1))[0, 0]
        live_rows = row_ids < length
        inside = (token_ids >= offset) & (token_ids < offset + length)
        normed = (normalize(hidden) * norm_scale).astype(jnp.bfloat16)
        projected = jnp.dot(normed, qkv_full, preferred_element_type=jnp.float32)
        projected = projected.astype(jnp.bfloat16)
        queries = projected[:, :inner_width]
        fresh_k = projected[:, inner_width : 2 * inner_width]
        fresh_v = projected[:, 2 * inner_width :]
        cached_k = lax.dynamic_index_in_dim(keys_img, picture, 0, keepdims=False)
        cached_v = lax.dynamic_index_in_dim(values_img, picture, 0, keepdims=False)
        text_k = lax.dynamic_index_in_dim(keys_txt, picture, 0, keepdims=False)
        text_v = lax.dynamic_index_in_dim(values_txt, picture, 0, keepdims=False)
        allowed = jnp.concatenate([text_ok, jnp.logical_not(inside), live_rows])
        attended = attend(
            queries,
            jnp.concatenate([text_k, cached_k, fresh_k], 0),
            jnp.concatenate([text_v, cached_v, fresh_v], 0),
            allowed,
        )
        summed = hidden.astype(jnp.float32) + jnp.dot(
            attended, out_full, preferred_element_type=jnp.float32
        )
        hidden_new = jnp.where(live_rows[:, None], summed, 0.0).astype(jnp.bfloat16)
        keys_img = lax.dynamic_update_index_in_dim(
            keys_img, place_rows(cached_k, fresh_k, offset, inside), picture, 0
        )
        values_img = lax.dynamic_update_index_in_dim(
            values_img, place_rows(cached_v, fresh_v, offset, inside), picture, 0
        )
        velocity = (
            jnp.dot(
                normalize(hidden_new).astype(jnp.bfloat16),
                head_weight,
                preferred_element_type=jnp.float32,
            )
            + head_bias
        )
        sigma_jump = lax.dynamic_index_in_dim(sigma_jumps, picture, 0, keepdims=False)
        stepped = jnp.where(
            live_rows[:, None], latents.astype(jnp.float32) + sigma_jump * velocity, 0.0
        ).astype(jnp.bfloat16)
        latents_new = jnp.where(section == sections - 1, stepped, latents)
        hidden, latents = shifted((hidden_new, latents_new), "phase", 1)
        arrival = (instant + 1) % sections
        arrival_len = patch_lengths[arrival // patches, arrival % patches]
        embedded = jnp.dot(latents, embed_weight, preferred_element_type=jnp.float32) + embed_bias
        embedded = jnp.where((row_ids < arrival_len)[:, None], embedded, 0.0).astype(jnp.bfloat16)
        hidden = jnp.where(section == 0, embedded, hidden)
    return (hidden[None, None], latents[None, None], keys_img[None], values_img[None])


def solution(mesh):
    placed = (
        P("phase", "dp", None, None),
        P("phase", "dp", None, None),
        P("phase", "dp", None, None),
        P("phase", "dp", None, None),
        P("phase", "dp", None, None),
        P("phase", "dp", None, None),
        P("phase", None),
        P("phase", "dp", None),
        P("phase", "dp", None),
        P(),
        P(),
        P(),
        P(),
        P(),
        P("dp"),
        P("dp", None),
    )
    return jax.shard_map(
        shards,
        mesh=mesh,
        in_specs=placed,
        out_specs=(
            P("phase", "dp", None, None),
            P("phase", "dp", None, None),
            P("phase", "dp", None, None),
            P("phase", "dp", None, None),
        ),
        check_vma=False,
    )
```

profile of v0, /device:TPU:24, one launch (start us, length us, event | category | flops | bytes accessed | tf_op | source)
XLA Modules:
  0.0 251.6 jit_solution(14716112577258381966)
XLA Ops:
  20.5 2.6 %copy.72 = bf16[1,2,256,1536]{2,3,1,0:T(8,128)(2,1)} copy(bf16[1,2,256,1536]{3,2,1,0:T(8,128)(2,1)} %param.19) | data formatting | bytes 3145728 | tf_op args[3]
  27.0 3.3 %constant_dynamic-slice_fusion.1 = (bf16[1,1,256,1536]{3,2,1,0:T(8,128)(2,1)}, bf16[1,1,256,1536]{3,2,1,0:T(8,128)(2,1)}, bf16[1,1,256,1536]{3,2,1,0:T(8,128)(2,1)}) fusion(bf16[1,2,256,1536]{3,2,1,0:T(8,128)(2,1)} %param.20, s32[]{:T(128)S(6)} %select_n.198, s32[]{:T(128)S(6)} %select_n.203, s32[]{:T(128)S(6)} %select_n.208), kind=kLoop, calls=%fused_computation.188 | loop fusion | bytes 4718604 | tf_op jit(solution)/shard_map/jit(dynamic_index_in_dim)/dynamic_slice | solution.py:116
  32.7 2.3 copy.78
  37.1 2.4 copy.79
  39.4 3.4 %constant_dynamic-slice_fusion.3 = (bf16[1,1,256,1536]{3,2,1,0:T(8,128)(2,1)}, bf16[1,1,256,1536]{3,2,1,0:T(8,128)(2,1)}, bf16[1,1,256,1536]{3,2,1,0:T(8,128)(2,1)}) fusion(bf16[1,2,256,1536]{3,2,1,0:T(8,128)(2,1)} %param.21, s32[]{:T(128)S(6)} %select_n.198, s32[]{:T(128)S(6)} %select_n.203, s32[]{:T(128)S(6)} %select_n.208), kind=kLoop, calls=%fused_computation.190 | loop fusion | bytes 4718604 | tf_op jit(solution)/shard_map/jit(dynamic_index_in_dim)/dynamic_slice | solution.py:117
  58.7 2.4 copy.86
  61.1 2.3 copy.117
  63.4 2.3 copy.104
  65.7 2.4 copy.118
  68.1 2.3 copy.99
  80.3 14.1 %all-gather.3.cloned.1.call-done = bf16[1,1536,4608]{2,1,0:T(8,128)(2,1)} async-done(((bf16[1,96,4608]{2,1,0:T(8,128)(2,1)}), bf16[1,1536,4608]{2,1,0:T(8,128)(2,1)}) %all-gather.3.cloned.1.call-update) | async-done | bytes 14155792 | tf_op jit(solution)/shard_map/all_gather | solution.py:95
  94.4 7.6 %fusion.9 = bf16[48,4608]{1,0:T(8,128)(2,1)S(1)} fusion(bf16[1,1536,4608]{2,1,0:T(8,128)(2,1)} %all-gather.3.cloned.1.call-done, bf16[1,1,48,1536]{3,2,1,0:T(8,128)(2,1)S(1)} %copy-done.10, f32[1536]{0:T(1024)S(1)} %reduce, f32[48]{0:T(128)S(1)} %add_rsqrt_fusion.5), kind=kOutput, calls=%fused_computation.9 | convolution fusion | flops 679993344 | bytes 14751936 | tf_op jit(solution)/shard_map/dot_general | solution.py:109
  110.9 4.8 %dynamic_update_slice.39 = bf16[304,1536]{0,1:T(8,128)(2,1)} dynamic-update-slice(bf16[304,1536]{0,1:T(8,128)(2,1)} %broadcast.164.clone.1, bf16[48,1536]{0,1:T(8,128)(2,1)} %copy.85, s32[]{:T(128)S(6)} %select_n.219, s32[]{:T(128)} %constant.143.clone.1) | dynamic-update-slice | bytes 294916 | tf_op jit(solution)/shard_map/dynamic_update_slice | solution.py:29
  116.8 4.8 %dynamic_update_slice.41 = bf16[304,1536]{0,1:T(8,128)(2,1)} dynamic-update-slice(bf16[304,1536]{0,1:T(8,128)(2,1)} %broadcast.164.clone, bf16[48,1536]{0,1:T(8,128)(2,1)} %copy.91, s32[]{:T(128)S(6)} %select_n.219, s32[]{:T(128)} %constant.143.clone.1) | dynamic-update-slice | bytes 294916 | tf_op jit(solution)/shard_map/dynamic_update_slice | solution.py:29
  121.6 2.3 fusion.147
  125.0 3.5 %fusion.252 = (f32[12,48]{1,0:T(8,128)S(1)}, f32[12,48,560]{2,1,0:T(8,128)}) fusion(bf16[48,12,128]{2,0,1:T(8,128)(2,1)} %bitcast.239, bf16[256,12,128]{2,0,1:T(8,128)(2,1)} %copy.79, bf16[256,12,128]{2,0,1:T(8,128)(2,1)} %copy.78, pred[560]{0:T(1024)(128)(4,1)S(1)} %get-tuple-element.57, bf16[6,12,8,128]{3,2,1,0:T(8,128)(2,1)} %get-tuple-element.39), kind=kOutput, calls=%fused_computation.255 | convolution fusion | flops 89027120 | bytes 3160880 | tf_op jit(solution)/shard_map/sub | solution.py:45
  128.5 3.1 %fusion.120 = bf16[12,6,8,128]{3,2,1,0:T(8,128)(2,1)} fusion(bf16[48,12,128]{2,0,1:T(8,128)(2,1)} %bitcast.238, bf16[256,12,128]{2,0,1:T(8,128)(2,1)} %copy.74, bf16[256,12,128]{2,0,1:T(8,128)(2,1)} %copy.73, f32[12,48,560]{2,1,0:T(8,128)} %get-tuple-element.63, f32[12,48]{1,0:T(8,128)S(1)} %get-tuple-element.62), kind=kOutput, calls=%fused_computation.93 | convolution fusion | flops 88455168 | bytes 3160320 | tf_op jit(solution)/shard_map/hqk,khd->qhd/dot_general | solution.py:47
  131.6 5.7 %all-gather.5.cloned.1.call-done = bf16[1,1536,1536]{2,1,0:T(8,128)(2,1)} async-done(((bf16[1,96,1536]{2,1,0:T(8,128)(2,1)}), bf16[1,1536,1536]{2,1,0:T(8,128)(2,1)}) %all-gather.5.cloned.1.call-update) | async-done | bytes 4718608 | tf_op jit(solution)/shard_map/all_gather | solution.py:96
  137.2 4.2 %fusion.152 = (f32[48]{0:T(128)S(1)}, bf16[48,1536]{1,0:T(8,128)(2,1)}) fusion(bf16[1,1536,1536]{2,1,0:T(8,128)(2,1)} %all-gather.5.cloned.1.call-done, bf16[12,6,8,128]{3,2,1,0:T(8,128)(2,1)} %fusion.120, bf16[1,1,48,1536]{3,2,1,0:T(8,128)(2,1)S(1)} %copy-done.10, pred[48]{0:T(512)(128)(4,1)S(1)} %iota_compare_fusion.2), kind=kOutput, calls=%fused_computation.136 | convolution fusion | flops 227008464 | bytes 5161200 | tf_op jit(solution)/shard_map/dot_general | solution.py:125
  143.2 2.3 fusion.135
  148.0 2.4 copy.93
  153.6 7.6 %fusion.12 = bf16[48,4608]{1,0:T(8,128)(2,1)S(1)} fusion(bf16[1,1536,4608]{2,1,0:T(8,128)(2,1)} %all-gather.3.cloned.1.call-done, f32[48,1536]{1,0:T(8,128)S(1)} %get-tuple-element.67, f32[1536]{0:T(1024)S(1)} %reduce, f32[48]{0:T(128)S(1)} %add_rsqrt_fusion.3), kind=kOutput, calls=%fused_computation.10 | convolution fusion | flops 679919616 | bytes 14899392 | tf_op jit(solution)/shard_map/dot_general | solution.py:109
  162.8 4.1 %fusion.257 = (f32[12,48]{1,0:T(8,128)}, f32[12,48,560]{2,1,0:T(8,128)}) fusion(bf16[48,12,128]{2,0,1:T(8,128)(2,1)} %get-tuple-element.81, bf16[256,12,128]{2,0,1:T(8,128)(2,1)} %copy.93, bf16[256,12,128]{2,0,1:T(8,128)(2,1)} %copy.92, pred[560]{0:T(1024)(128)(4,1)S(1)} %get-tuple-element.56, bf16[6,12,8,128]{3,2,1,0:T(8,128)(2,1)} %get-tuple-element.34), kind=kOutput, calls=%fused_computation.256 | convolution fusion | flops 89027120 | bytes 3160880 | tf_op jit(solution)/shard_map/sub | solution.py:45
  173.7 3.0 %collective-permute-start.2 = (bf16[48,64]{1,0:T(8,128)(2,1)S(1)}, bf16[48,64]{1,0:T(8,128)(2,1)S(1)}, u32[]{:S(2)}, u32[]{:S(2)}) collective-permute-start(bf16[48,64]{1,0:T(8,128)(2,1)S(1)} %fusion.199), channel_id=1, source_target_pairs={{0,16},{16,32},{32,48},{48,64},{64,80},{80,96},{96,112},{112,128},... | collective-permute-start | bytes 18440 | tf_op jit(solution)/shard_map/ppermute | solution.py:18
  179.7 5.5 %dynamic_update_slice.43 = bf16[304,1536]{0,1:T(8,128)(2,1)} dynamic-update-slice(bf16[304,1536]{0,1:T(8,128)(2,1)} %broadcast.164.clone.3, bf16[48,1536]{0,1:T(8,128)(2,1)} %copy.98, s32[]{:T(128)S(6)} %select_n.228, s32[]{:T(128)} %constant.143.clone.1) | dynamic-update-slice | bytes 294916 | tf_op jit(solution)/shard_map/dynamic_update_slice | solution.py:29
  186.3 5.3 %dynamic_update_slice.45 = bf16[304,1536]{0,1:T(8,128)(2,1)} dynamic-update-slice(bf16[304,1536]{0,1:T(8,128)(2,1)} %broadcast.164.clone.2, bf16[48,1536]{0,1:T(8,128)(2,1)} %copy.103, s32[]{:T(128)S(6)} %select_n.228, s32[]{:T(128)} %constant.143.clone.1) | dynamic-update-slice | bytes 294916 | tf_op jit(solution)/shard_map/dynamic_update_slice | solution.py:29
  201.1 7.7 %fusion.15 = bf16[48,4608]{1,0:T(8,128)(2,1)S(1)} fusion(bf16[1,1536,4608]{2,1,0:T(8,128)(2,1)} %all-gather.3.cloned.1.call-done, f32[48,1536]{1,0:T(8,128)S(1)} %get-tuple-element.73, f32[48]{0:T(128)S(1)} %add_rsqrt_fusion.1, f32[1536]{0:T(1024)S(1)} %reduce), kind=kOutput, calls=%fused_computation.11 | convolution fusion | flops 679919616 | bytes 14899392 | tf_op jit(solution)/shard_map/dot_general | solution.py:109
  212.1 3.5 %fusion.262 = (f32[12,48]{1,0:T(8,128)S(1)}, f32[12,48,560]{2,1,0:T(8,128)}) fusion(bf16[48,12,128]{2,0,1:T(8,128)(2,1)} %bitcast.241, bf16[256,12,128]{2,0,1:T(8,128)(2,1)} %copy.105, bf16[256,12,128]{2,0,1:T(8,128)(2,1)} %copy.104, pred[560]{0:T(1024)(128)(4,1)S(1)} %get-tuple-element.55, bf16[6,12,8,128]{3,2,1,0:T(8,128)(2,1)S(1)} %get-tuple-element.30), kind=kOutput, calls=%fused_computation.257 | convolution fusion | flops 89027120 | bytes 3160880 | tf_op jit(solution)/shard_map/sub | solution.py:45
  224.1 5.5 %dynamic_update_slice.47 = bf16[304,1536]{0,1:T(8,128)(2,1)} dynamic-update-slice(bf16[304,1536]{0,1:T(8,128)(2,1)} %broadcast.164.clone.5, bf16[48,1536]{0,1:T(8,128)(2,1)} %copy.109, s32[]{:T(128)S(6)} %select_n.237, s32[]{:T(128)} %constant.143.clone.1) | dynamic-update-slice | bytes 294916 | tf_op jit(solution)/shard_map/dynamic_update_slice | solution.py:29
  230.7 5.4 %dynamic_update_slice.49 = bf16[304,1536]{0,1:T(8,128)(2,1)} dynamic-update-slice(bf16[304,1536]{0,1:T(8,128)(2,1)} %broadcast.164.clone.4, bf16[48,1536]{0,1:T(8,128)(2,1)} %copy.110, s32[]{:T(128)S(6)} %select_n.237, s32[]{:T(128)} %constant.143.clone.1) | dynamic-update-slice | bytes 294916 | tf_op jit(solution)/shard_map/dynamic_update_slice | solution.py:29
  236.1 2.9 %fusion.137 = (bf16[1,2,256,1536]{2,3,1,0:T(8,128)(2,1)}, bf16[1,2,256,1536]{2,3,1,0:T(8,128)(2,1)}) fusion(bf16[1,2,256,1536]{2,3,1,0:T(8,128)(2,1)} %copy.199, s32[]{:T(128)S(6)} %select_n.198, bf16[304,1536]{0,1:T(8,128)(2,1)} %dynamic_update_slice.49, pred[256]{0:T(512)(128)(4,1)S(1)} %get-tuple-element.15, bf16[2,256,1536]{1,2,0:T(8,128)(2,1)S(1)} %copy-done.4, ...), kind=kLoop, calls=%fused_computation.108 | loop fusion | flops 786432 | bytes 4718852 | tf_op jit(solution)/shard_map/jit(dynamic_update_index_in_dim)/dynamic_update_slice | solution.py:132
  239.0 2.7 %copy.111 = bf16[1,2,256,1536]{3,2,1,0:T(8,128)(2,1)} copy(bf16[1,2,256,1536]{2,3,1,0:T(8,128)(2,1)} %get-tuple-element.51) | data formatting | bytes 3145728
  (168 shorter events, 93.9 us)
Async XLA Ops:
  7.2 145.8 %copy-start = (bf16[64,1536]{1,0:T(8,128)(2,1)S(1)}, bf16[64,1536]{1,0:T(8,128)(2,1)}, u32[]{:S(2)}) copy-start(bf16[64,1536]{1,0:T(8,128)(2,1)} %param.25) | copy-start | bytes 589828
  7.2 87.2 %all-gather.3.cloned.1.call-start = ((), (), s32[]{:S(2)}) async-start(), calls=%async_computation | async-start | bytes 15040512 | tf_op jit(solution)/shard_map/all_gather | solution.py:95
  7.9 129.3 %all-gather.5.cloned.1.call-start = ((), (), s32[]{:S(2)}) async-start(), calls=%async_computation.1 | async-start | bytes 5013504 | tf_op jit(solution)/shard_map/all_gather | solution.py:96
  65.7 5.9 %copy-start.14 = (f32[1,1536]{1,0:T(1,128)S(1)}, f32[1,1536]{1,0:T(1,128)}, u32[]{:S(2)}) copy-start(f32[1,1536]{1,0:T(1,128)} %param.22) | copy-start | bytes 18436
  65.7 6.0 %copy-start.15 = (s32[2]{0:T(128)S(1)}, s32[2]{0:T(128)}, u32[]{:S(2)}) copy-start(s32[2]{0:T(128)} %param.30) | copy-start | bytes 28
  65.7 6.0 %copy-start.16 = (f32[5]{0:T(128)S(1)}, f32[5]{0:T(128)}, u32[]{:S(2)}) copy-start(f32[5]{0:T(128)} %param.29) | copy-start | bytes 64
  65.7 14.4 %copy-start.10 = (bf16[1,1,48,1536]{3,2,1,0:T(8,128)(2,1)S(1)}, bf16[1,1,48,1536]{3,2,1,0:T(8,128)(2,1)}, u32[]{:S(2)}) copy-start(bf16[1,1,48,1536]{3,2,1,0:T(8,128)(2,1)} %param.16) | copy-start | bytes 442372
  124.0 23.1 %copy-start.1 = (bf16[2,256,1536]{1,2,0:T(8,128)(2,1)}, bf16[2,256,1536]{1,2,0:T(8,128)(2,1)S(1)}, u32[]{:S(2)}) copy-start(bf16[2,256,1536]{1,2,0:T(8,128)(2,1)S(1)} %get-tuple-element.61) | copy-start | bytes 4718596
  131.5 11.6 %copy-start.20 = (bf16[1,1,48,64]{3,2,1,0:T(8,128)(2,1)S(1)}, bf16[1,1,48,64]{3,2,1,0:T(8,128)(2,1)}, u32[]{:S(2)}) copy-start(bf16[1,1,48,64]{3,2,1,0:T(8,128)(2,1)} %param.17) | copy-start | bytes 18436
  131.6 11.6 %copy-start.28 = (f32[64]{0:T(128)S(1)}, f32[64]{0:T(128)}, u32[]{:S(2)}) copy-start(f32[64]{0:T(128)} %param.28) | copy-start | bytes 772
  137.2 5.9 %copy-start.17 = (bf16[1536,64]{0,1:T(8,128)(2,1)S(1)}, bf16[1536,64]{0,1:T(8,128)(2,1)}, u32[]{:S(2)}) copy-start(bf16[1536,64]{0,1:T(8,128)(2,1)} %param.27) | copy-start | bytes 589828
  141.4 11.6 %collective-permute-start.1 = (bf16[48,1536]{1,0:T(8,128)(2,1)}, bf16[48,1536]{1,0:T(8,128)(2,1)S(1)}, u32[]{:S(2)}, u32[]{:S(2)}) collective-permute-start(bf16[48,1536]{1,0:T(8,128)(2,1)} %get-tuple-element.65), channel_id=1, source_target_pairs={{0,16},{16,32},{32,48},{48,64},{64,80},{80,96},{96,112},{112,128},... | collective-permute-start | bytes 442376 | tf_op jit(solution)/shard_map/ppermute | solution.py:18
  145.5 7.5 %collective-permute-start = (bf16[48,64]{1,0:T(8,128)(2,1)}, bf16[48,64]{1,0:T(8,128)(2,1)S(1)}, u32[]{:S(2)}, u32[]{:S(2)}) collective-permute-start(bf16[48,64]{1,0:T(8,128)(2,1)} %fusion.135), channel_id=1, source_target_pairs={{0,16},{16,32},{32,48},{48,64},{64,80},{80,96},{96,112},{112,128},... | collective-permute-start | bytes 18440 | tf_op jit(solution)/shard_map/ppermute | solution.py:18
  148.0 2.4 copy-start.6
  148.0 5.0 %copy-start.25 = (f32[1536]{0:T(1024)S(1)}, f32[1536]{0:T(1024)}, u32[]{:S(2)}) copy-start(f32[1536]{0:T(1024)} %param.26) | copy-start | bytes 18436
  162.8 4.1 %copy-start.12 = (bf16[256,12,128]{2,0,1:T(8,128)(2,1)S(1)}, bf16[256,12,128]{2,0,1:T(8,128)(2,1)}, u32[]{:S(2)}) copy-start(bf16[256,12,128]{2,0,1:T(8,128)(2,1)} %copy.86) | copy-start | bytes 2359300
  162.8 6.4 %slice-start = ((s8[4718592]{0:T(1024)(128)(4,1)}), s8[524288]{0:T(1024)(128)(4,1)S(1)}, s32[]{:S(2)}) async-start(s8[4718592]{0:T(1024)(128)(4,1)} %bitcast.218), calls=%async_computation.2 | async-start | bytes 1048576
  167.0 2.9 %slice-start.1 = ((s8[4718592]{0:T(1024)(128)(4,1)}), s8[4194304]{0:T(1024)(128)(4,1)S(1)}, s32[]{:S(2)}) async-start(s8[4718592]{0:T(1024)(128)(4,1)} %bitcast.218), calls=%async_computation.3 | async-start | bytes 8388608
  169.9 6.8 %copy-start.13 = (bf16[48,1536]{1,0:T(8,128)(2,1)S(1)}, bf16[48,1536]{1,0:T(8,128)(2,1)}, u32[]{:S(2)}) copy-start(bf16[48,1536]{1,0:T(8,128)(2,1)} %get-tuple-element.35) | copy-start | bytes 442372
  171.6 29.2 %collective-permute-start.3 = (bf16[48,1536]{1,0:T(8,128)(2,1)}, bf16[48,1536]{1,0:T(8,128)(2,1)}, u32[]{:S(2)}, u32[]{:S(2)}) collective-permute-start(bf16[48,1536]{1,0:T(8,128)(2,1)} %get-tuple-element.71), channel_id=1, source_target_pairs={{0,16},{16,32},{32,48},{48,64},{64,80},{80,96},{96,112},{112,128},... | collective-permute-start | bytes 442376 | tf_op jit(solution)/shard_map/ppermute | solution.py:18
  173.7 27.0 %collective-permute-start.2 = (bf16[48,64]{1,0:T(8,128)(2,1)S(1)}, bf16[48,64]{1,0:T(8,128)(2,1)S(1)}, u32[]{:S(2)}, u32[]{:S(2)}) collective-permute-start(bf16[48,64]{1,0:T(8,128)(2,1)S(1)} %fusion.199), channel_id=1, source_target_pairs={{0,16},{16,32},{32,48},{48,64},{64,80},{80,96},{96,112},{112,128},... | collective-permute-start | bytes 18440 | tf_op jit(solution)/shard_map/ppermute | solution.py:18
  179.7 11.9 %copy-start.2 = (bf16[2,256,1536]{1,2,0:T(8,128)(2,1)S(1)}, bf16[2,256,1536]{1,2,0:T(8,128)(2,1)}, u32[]{:S(2)}) copy-start(bf16[2,256,1536]{1,2,0:T(8,128)(2,1)} %copy-done.1) | copy-start | bytes 4718596
  198.4 2.4 copy-start.26
  198.4 2.4 copy-start.31
  200.8 8.0 %copy-start.21 = (bf16[48,64]{1,0:T(8,128)(2,1)}, bf16[48,64]{1,0:T(8,128)(2,1)S(1)}, u32[]{:S(2)}) copy-start(bf16[48,64]{1,0:T(8,128)(2,1)S(1)} %collective-permute-done.2) | copy-start | bytes 18436
  212.1 3.5 %copy-start.11 = (bf16[256,12,128]{2,0,1:T(8,128)(2,1)S(1)}, bf16[256,12,128]{2,0,1:T(8,128)(2,1)}, u32[]{:S(2)}) copy-start(bf16[256,12,128]{2,0,1:T(8,128)(2,1)} %copy.99) | copy-start | bytes 2359300
  212.1 5.8 %slice-start.2 = ((s8[4718592]{0:T(1024)(128)(4,1)}), s8[524288]{0:T(1024)(128)(4,1)S(1)}, s32[]{:S(2)}) async-start(s8[4718592]{0:T(1024)(128)(4,1)} %bitcast.220), calls=%async_computation.4 | async-start | bytes 1048576
  215.6 2.9 %slice-start.3 = ((s8[4718592]{0:T(1024)(128)(4,1)}), s8[4194304]{0:T(1024)(128)(4,1)S(1)}, s32[]{:S(2)}) async-start(s8[4718592]{0:T(1024)(128)(4,1)} %bitcast.220), calls=%async_computation.5 | async-start | bytes 8388608
  219.5 23.7 %collective-permute-start.5 = (bf16[48,1536]{1,0:T(8,128)(2,1)S(1)}, bf16[48,1536]{1,0:T(8,128)(2,1)}, u32[]{:S(2)}, u32[]{:S(2)}) collective-permute-start(bf16[48,1536]{1,0:T(8,128)(2,1)S(1)} %get-tuple-element.77), channel_id=1, source_target_pairs={{0,16},{16,32},{32,48},{48,64},{64,80},{80,96},{96,112},{112,128},... | collective-permute-start | bytes 442376 | tf_op jit(solution)/shard_map/ppermute | solution.py:18
  220.9 22.3 %collective-permute-start.4 = (bf16[48,64]{1,0:T(8,128)(2,1)S(1)}, bf16[48,64]{1,0:T(8,128)(2,1)S(1)}, u32[]{:S(2)}, u32[]{:S(2)}) collective-permute-start(bf16[48,64]{1,0:T(8,128)(2,1)S(1)} %fusion.200), channel_id=1, source_target_pairs={{0,16},{16,32},{32,48},{48,64},{64,80},{80,96},{96,112},{112,128},... | collective-permute-start | bytes 18440 | tf_op jit(solution)/shard_map/ppermute | solution.py:18
  224.1 12.0 %copy-start.4 = (bf16[2,256,1536]{1,2,0:T(8,128)(2,1)S(1)}, bf16[2,256,1536]{1,2,0:T(8,128)(2,1)}, u32[]{:S(2)}) copy-start(bf16[2,256,1536]{1,2,0:T(8,128)(2,1)} %copy-done.3) | copy-start | bytes 4718596
  239.0 2.7 %copy-start.7 = (bf16[1,2,256,1536]{2,3,1,0:T(8,128)(2,1)S(1)}, bf16[1,2,256,1536]{2,3,1,0:T(8,128)(2,1)}, u32[]{:S(2)}) copy-start(bf16[1,2,256,1536]{2,3,1,0:T(8,128)(2,1)} %get-tuple-element.50) | copy-start | bytes 4718596
  (12 other events, 19.0 us)
Sparse Core Ops, SparseCore 0:
  9.9 84.4 all-gather.2
  96.2 40.9 all-gather.4
where the time goes:
time: 256 us; the launch traced here: 252 us
  local copies, waits for them, and re-layouts  125 us (49%)
  matrix products  55 us (21%)
  between operations  24.1 us (9%)
  waiting for transfers between devices  22.5 us (9%)
  other arithmetic  16.3 us (6%)
  starting transfers between devices  9.14 us (4%)
    dynamic_update_slice x6, local copies, waits for them, and re-layouts, place_rows(): canvas = lax.dynamic_update_slice_in_dim(canvas, fresh_rows, offset, 0)  31.3 us
    unnamed x87, local copies, waits for them, and re-layouts  30.3 us
    dot_general x3, matrix products, shards(): projected = jnp.dot(normed, qkv_full, preferred_element_type=jnp.float32)  22.9 us
    concatenate x8, local copies, waits for them, and re-layouts, shards(): jnp.concatenate([text_k, cached_k, fresh_k], 0)  15.2 us
    concatenate x9, local copies, waits for them, and re-layouts, shards(): jnp.concatenate([text_v, cached_v, fresh_v], 0)  14.7 us
    all_gather x1, waiting for transfers between devices, shards(): lax.all_gather(w_qkv, 'dp', axis=1, tiled=True)  14.1 us
    sub x3, matrix products, attend(): raised = jnp.exp(scores - highest)  11.1 us
    ppermute x6, starting transfers between devices, shifted(): return lax.ppermute(value, axis, pairs)  9.06 us
  transfers between devices with their start and end apart: 8, of which 3 were waited for; matrix products, arithmetic and copies ran while one was open for 60% of the time, Pallas kernels for 0%

commit v1 on v0

v1 whole, which is shorter than its diff:
```python
import functools
import math

import jax
import jax.numpy as jnp
from jax import lax
from jax.experimental import pallas as pl
from jax.experimental.pallas import tpu as pltpu
from jax.sharding import PartitionSpec as P

HEAD_DIM = 128
TICKS = 3
WINDOW = 64
TILE = 16
GRANT = 12 * 1024 * 1024

epsilon = 1e-06

X, Y, C = 2, 4, 2


def spot(x, y, core):
    return ((x % X) * Y + (y % Y)) * C + core


def moved(value, dx, dy, dc):
    pairs = [
        (spot(x, y, c), spot(x + dx, y + dy, (c + dc) % C))
        for x in range(X)
        for y in range(Y)
        for c in range(C)
    ]
    return lax.ppermute(value, "dp", pairs)


def shifted(value):
    count = lax.axis_size("phase")
    pairs = [(source, (source + 1) % count) for source in range(count)]
    return lax.ppermute(value, "phase", pairs)


def joined(*values):
    return lax.optimization_barrier(values)


NEAR = [
    (0, 0, 0, 16),
    (0, -1, 0, 8),
    (0, -1, 8, 8),
    (0, 1, 0, 8),
    (0, 1, 8, 8),
    (1, 0, 0, 8),
    (1, 0, 8, 8),
]
MIDDLE = [(0, 2, 0, 8), (0, 2, 8, 8), (1, -1, 0, 8), (1, 1, 0, 8), (1, 2, 0, 8)]
LAST = [(1, -1, 8, 8), (1, 1, 8, 8), (1, 2, 8, 8)]


def in_hbm(array):
    return pltpu.with_memory_space_constraint(array, pltpu.HBM)


def pair(piece):
    return moved(piece, 0, 0, 1)


def places(rows, group):
    device = lax.axis_index("dp")
    core = lax.rem(device, C)
    y = lax.rem(device // C, Y)
    x = device // (C * Y)
    found = []
    for dx, dy, dc, part, count in group:
        source = (lax.rem(x + dx, X) * Y + lax.rem(y + dy + Y, Y)) * C + lax.rem(core + dc, C)
        found.append((pl.multiple_of(source * rows + part * rows // 16, TILE), count * rows // 16))
    return found


def both(group):
    return [(dx, dy, dc, part, count) for dc in range(C) for dx, dy, part, count in group]


def normalize(widened):
    return widened * lax.rsqrt(jnp.mean(widened * widened, axis=-1, keepdims=True) + epsilon)


def batch_of(tick, section, sections, lengths_ref):
    patches = lengths_ref.shape[1]
    slot = lax.rem(tick - section + sections, sections)
    picture = slot // patches
    segment = lax.rem(slot, patches)
    length = lengths_ref[picture, segment]
    offset = jnp.int32(0)
    for m in range(patches - 1):
        offset = offset + jnp.where(m < segment, lengths_ref[picture, m], 0)
    return picture, length, offset


def embedded_rows(latents, embed_w_ref, embed_b_ref, live):
    rows = jnp.dot(latents, embed_w_ref[...], preferred_element_type=jnp.float32) + embed_b_ref[...][None]
    row_ids = lax.broadcasted_iota(jnp.int32, rows.shape, 0)
    return jnp.where(row_ids < live, rows, 0.0).astype(jnp.bfloat16)


def attend(proj, image_k, image_v, text_k, text_v, attended):
    width = attended.shape[1]
    scale = 1.0 / math.sqrt(HEAD_DIM)
    across = (((1,), (1,)), ((), ()))
    for head in range(width // HEAD_DIM):
        cols = slice(head * HEAD_DIM, (head + 1) * HEAD_DIM)
        queries = proj[:, cols]
        on_text = lax.dot_general(queries, text_k[:, cols], across, preferred_element_type=jnp.float32)
        on_image = lax.dot_general(queries, image_k[:, cols], across, preferred_element_type=jnp.float32)
        highest = jnp.maximum(
            jnp.max(on_text, axis=-1, keepdims=True), jnp.max(on_image, axis=-1, keepdims=True)
        )
        on_text = jnp.exp((on_text - highest) * scale)
        on_image = jnp.exp((on_image - highest) * scale)
        total = jnp.sum(on_text, axis=-1, keepdims=True) + jnp.sum(on_image, axis=-1, keepdims=True)
        mixed = jnp.dot(
            on_text.astype(jnp.bfloat16), text_v[:, cols], preferred_element_type=jnp.float32
        ) + jnp.dot(on_image.astype(jnp.bfloat16), image_v[:, cols], preferred_element_type=jnp.float32)
        attended[:, cols] = (mixed / total).astype(jnp.bfloat16)


def weight_copies(pieces, weights, rows, group, sems):
    return [
        pltpu.make_async_copy(piece, weights.at[pl.ds(start, count), :], sems.at[at])
        for at, (piece, (start, count)) in enumerate(zip(pieces, places(rows, group)))
    ]


def run_copies(copies):
    for copy in copies:
        copy.start()
    for copy in copies:
        copy.wait()


def own_kernel(qkv, out, low, high, whole, sems):
    half, width = low.shape[0], qkv.shape[1]
    copies = []
    for at, (target, start) in enumerate(((low, 0), (high, half), (whole, 0))):
        rows = pl.ds(start, target.shape[0])
        copies += [
            pltpu.make_async_copy(qkv.at[rows, :], target.at[:, pl.ds(0, width)], sems.at[2 * at]),
            pltpu.make_async_copy(
                out.at[rows, :], target.at[:, pl.ds(width, out.shape[1])], sems.at[2 * at + 1]
            ),
        ]
    run_copies(copies)


def load_kernel(rows, group, copied, first, *refs):
    if not first:
        refs = refs[1:]
    count = len(group)
    pieces, sources, refs = refs[:count], refs[count : count + copied], refs[count + copied :]
    weights, targets, (sems, copy_sems) = refs[0], refs[1 : 1 + copied], refs[1 + copied :]
    run_copies(
        weight_copies(pieces, weights, rows, group, sems)
        + [
            pltpu.make_async_copy(source, target, copy_sems.at[at])
            for at, (source, target) in enumerate(zip(sources, targets))
        ]
    )


def tick_kernel(tick, sections, first, rows, *refs):
    lengths, steps, sigmas = refs[:3]
    gain, embed_w, embed_b, head_w, head_b = refs[3:8]
    text_k, text_v, keys_in, values_in = refs[8:12]
    rest = refs[12:]
    if first:
        hidden_in, latents_in, _ = rest[:3]
        pieces = rest[3 : 3 + C * len(LAST)]
        keys, values, weights, sent, *scratch = rest[3 + C * len(LAST) :]
    else:
        received, weights = rest[:2]
        keys, values, sent, *scratch = rest[2:]
    hidden, image_k, image_v, txt_k, txt_v, proj, attended, cache_sem, back_sem, *weight_sem = scratch
    width = hidden.shape[1]
    section = lax.axis_index("phase")
    picture, length, offset = batch_of(tick, section, sections, lengths)
    base = pl.multiple_of(jnp.minimum((offset // TILE) * TILE, image_k.shape[0] - WINDOW), TILE)

    loads = [
        pltpu.make_async_copy(source.at[picture], target, cache_sem.at[at])
        for at, (source, target) in enumerate(
            [(keys_in, image_k), (values_in, image_v), (text_k, txt_k), (text_v, txt_v)]
        )
    ]
    weight_loads = []
    if first:
        weight_loads = weight_copies(pieces, weights, rows, both(LAST), weight_sem[0])
    for load in weight_loads + loads:
        load.start()

    if first:
        hidden[...] = hidden_in[...]
    else:
        hidden[...] = received[:, :width]

        @pl.when(section == 0)
        def _():
            hidden[...] = embedded_rows(
                received[:, width : width + embed_w.shape[0]], embed_w, embed_b, lengths[0, tick]
            )

    normed = (normalize(hidden[...].astype(jnp.float32)) * gain[...]).astype(jnp.bfloat16)
    for load in weight_loads:
        load.wait()
    for block in range(3):
        cols = slice(block * width, (block + 1) * width)
        proj[:, cols] = jnp.dot(normed, weights[:, cols], preferred_element_type=jnp.float32).astype(
            jnp.bfloat16
        )
    for load in loads:
        load.wait()

    token = lax.broadcasted_iota(jnp.int32, (WINDOW, proj.shape[0]), 0) + base - offset
    place = (token == lax.broadcasted_iota(jnp.int32, token.shape, 1)) & (token < length)
    place = place.astype(jnp.bfloat16)
    token = lax.broadcasted_iota(jnp.int32, (WINDOW, width), 0) + base - offset
    inside = (token >= 0) & (token < length)
    for block, cache in ((1, image_k), (2, image_v)):
        fresh = jnp.dot(
            place, proj[:, block * width : (block + 1) * width], preferred_element_type=jnp.float32
        )
        old = cache[pl.ds(base, WINDOW), :].astype(jnp.float32)
        cache[pl.ds(base, WINDOW), :] = jnp.where(inside, fresh, old).astype(jnp.bfloat16)
    backs = [
        pltpu.make_async_copy(
            source.at[pl.ds(base, WINDOW), :],
            target.at[picture, pl.ds(base, WINDOW), :],
            back_sem.at[at],
        )
        for at, (source, target) in enumerate([(image_k, keys), (image_v, values)])
    ]
    for back in backs:
        back.start()

    attend(proj, image_k, image_v, txt_k, txt_v, attended)

    summed = hidden[...].astype(jnp.float32) + jnp.dot(
        attended[...], weights[:, 3 * width :], preferred_element_type=jnp.float32
    )
    row_ids = lax.broadcasted_iota(jnp.int32, summed.shape, 0)
    hidden_new = jnp.where(row_ids < length, summed, 0.0).astype(jnp.bfloat16)
    sent[:, :width] = hidden_new
    channels = embed_w.shape[0]
    latents = latents_in[...] if first else received[:, width : width + channels]
    sent[:, width:] = jnp.concatenate(
        [latents, jnp.zeros((latents.shape[0], sent.shape[1] - width - channels), latents.dtype)], axis=1
    )

    @pl.when(section == sections - 1)
    def _():
        velocity = (
            lax.dot_general(
                normalize(hidden_new.astype(jnp.float32)).astype(jnp.bfloat16),
                head_w[...],
                (((1,), (1,)), ((), ())),
                preferred_element_type=jnp.float32,
            )
            + head_b[...][None]
        )
        step = steps[picture]
        jump = sigmas[step + 1] - sigmas[step]
        stepped = latents.astype(jnp.float32) + jump * velocity
        row_ids = lax.broadcasted_iota(jnp.int32, stepped.shape, 0)
        stepped = jnp.where(row_ids < length, stepped, 0.0).astype(jnp.bfloat16)
        sent[:, width:] = jnp.concatenate(
            [stepped, jnp.zeros((latents.shape[0], sent.shape[1] - width - channels), latents.dtype)],
            axis=1,
        )

    for back in backs:
        back.wait()


def final_kernel(tick, lengths, embed_w, embed_b, received, hidden, latents):
    width = hidden.shape[1]
    arrived = received[:, width : width + latents.shape[1]]
    hidden[...] = received[:, :width]
    latents[...] = arrived

    @pl.when(lax.axis_index("phase") == 0)
    def _():
        hidden[...] = embedded_rows(arrived, embed_w, embed_b, lengths[0, tick])


def shards(
    hidden_flight,
    latent_flight,
    key_cache,
    value_cache,
    text_keys,
    text_values,
    norm_gain,
    w_qkv,
    w_out,
    embed_weight,
    embed_bias,
    head_weight,
    head_bias,
    sigma_table,
    step_index,
    patch_lengths,
):
    sections = lax.axis_size("phase")
    hidden = hidden_flight[0, 0]
    latents = latent_flight[0, 0]
    keys, values = key_cache[0], value_cache[0]
    rows, width = hidden.shape
    wide = width + HEAD_DIM
    tokens = keys.shape[1]
    part = w_qkv.shape[1]
    full = part * lax.axis_size("dp")
    smem = pl.BlockSpec(memory_space=pltpu.SMEM)
    vmem = pl.BlockSpec(memory_space=pltpu.VMEM)
    hbm = pl.BlockSpec(memory_space=pl.ANY)
    scalars = [patch_lengths, step_index, sigma_table]
    small = [norm_gain, embed_weight, embed_bias, head_weight.T, head_bias]
    texts = [text_keys[0], text_values[0]]
    params = pltpu.CompilerParams(vmem_limit_bytes=GRANT)
    small_params = pltpu.CompilerParams(vmem_limit_bytes=GRANT // 8)

    full = part * lax.axis_size("dp")
    total = w_qkv.shape[2] + w_out.shape[2]
    halves = [jax.ShapeDtypeStruct((part // 2, total), jnp.bfloat16)] * 2
    low, high, whole = pl.pallas_call(
        own_kernel,
        out_shape=halves + [jax.ShapeDtypeStruct((part, total), jnp.bfloat16)],
        in_specs=[hbm] * 2,
        out_specs=[hbm] * 3,
        scratch_shapes=[pltpu.SemaphoreType.DMA((6,))],
        compiler_params=small_params,
        name="own",
    )(in_hbm(w_qkv[0]), in_hbm(w_out[0]))

    def loaded(weights, pieces, group, copied, name):
        first = weights is None
        if not first:
            weights = pltpu.with_memory_space_constraint(weights, pltpu.VMEM)
        return pl.pallas_call(
            functools.partial(load_kernel, part, group, len(copied), first),
            out_shape=[pltpu.VMEM((full, total), jnp.bfloat16)]
            + [jax.ShapeDtypeStruct(array.shape, array.dtype) for array in copied],
            in_specs=[vmem] * (not first) + [hbm] * (len(pieces) + len(copied)),
            out_specs=[vmem] + [hbm] * len(copied),
            scratch_shapes=[
                pltpu.SemaphoreType.DMA((len(pieces),)),
                pltpu.SemaphoreType.DMA((max(len(copied), 1),)),
            ],
            input_output_aliases={} if first else {0: 0},
            compiler_params=small_params,
            name=name,
        )(*([] if first else [weights]), *pieces, *[in_hbm(array) for array in copied])

    below_low, above_high, across_low = moved(low, 0, 1, 0), moved(high, 0, -1, 0), moved(low, 1, 0, 0)
    below_high, above_low = moved(high, 0, 1, 0), moved(low, 0, -1, 0)
    far_low, far_high = moved(below_low, 0, 1, 0), moved(above_high, 0, -1, 0)
    across_high = moved(joined(high, across_low)[0], 1, 0, 0)
    ready = joined(whole, below_low, above_high, across_low, below_high, below_high, above_low, across_high)
    whole_pair, below_low_pair, above_high_pair, across_low_pair, below_high_pair = [pair(piece) for piece in ready[:5]]
    far_low, far_high, onward_low, onward_high, *ready = joined(
        far_low, far_high, across_low, across_high, above_low, across_high, whole_pair, below_low_pair, above_high_pair, across_low_pair, below_high_pair
    )
    above_low_pair, across_high_pair = [pair(piece) for piece in ready[:2]]
    xu_low, xd_low, xf_low = moved(onward_low, 0, 1, 0), moved(onward_low, 0, -1, 0), moved(far_low, 1, 0, 0)
    xu_high, xd_high, xf_high = moved(onward_high, 0, 1, 0), moved(onward_high, 0, -1, 0), moved(far_high, 1, 0, 0)
    near = [whole, below_low, below_high, above_low, above_high, across_low, across_high]
    near += [whole_pair, below_low_pair, below_high_pair, above_low_pair, above_high_pair, across_low_pair, across_high_pair]
    weights, keys, values = loaded(None, near, both(NEAR), [keys, values], "near")
    low_set = [far_low, far_high, xu_low, xd_low, xf_low]
    keys, *low_set = joined(keys, *low_set)
    middle = low_set + [pair(piece) for piece in low_set]
    weights, latents = loaded(weights, middle, both(MIDDLE), [latents], "middle")
    latents, *last = joined(latents, xu_high, xd_high, xf_high)
    last += [pair(piece) for piece in last]

    for tick in range(TICKS):
        first = tick == 0
        weights = pltpu.with_memory_space_constraint(weights, pltpu.VMEM)
        if first:
            own = [hidden, latents, weights] + last
            own_specs = [vmem] * 3 + [hbm] * len(last)
        else:
            own = [received, weights]
            own_specs = [vmem] * 2
        shapes = [
            jax.ShapeDtypeStruct(keys.shape, keys.dtype),
            jax.ShapeDtypeStruct(values.shape, values.dtype),
        ]
        out_specs = [hbm, hbm]
        aliases = {10: 0, 11: 1}
        if first:
            shapes.append(pltpu.VMEM(weights.shape, weights.dtype))
            out_specs.append(vmem)
            aliases[14] = 2
        shapes.append(jax.ShapeDtypeStruct((rows, wide), jnp.bfloat16))
        out_specs.append(vmem)
        scratch = [
            pltpu.VMEM((rows, width), jnp.bfloat16),
            *[pltpu.VMEM((tokens, width), jnp.bfloat16)] * 4,
            pltpu.VMEM((rows, 3 * width), jnp.bfloat16),
            pltpu.VMEM((rows, width), jnp.bfloat16),
            pltpu.SemaphoreType.DMA((4,)),
            pltpu.SemaphoreType.DMA((2,)),
        ]
        if first:
            scratch.append(pltpu.SemaphoreType.DMA((len(last),)))
        results = pl.pallas_call(
            functools.partial(tick_kernel, tick, sections, first, part),
            out_shape=shapes,
            in_specs=[smem] * 3 + [vmem] * 5 + [hbm] * 4 + own_specs,
            out_specs=out_specs,
            scratch_shapes=scratch,
            input_output_aliases=aliases,
            compiler_params=params,
            name=f"tick{tick}",
        )(*scalars, *small, *texts, keys, values, *own)
        if first:
            keys, values, weights, sent = results
        else:
            keys, values, sent = results
        received = shifted(sent)

    hidden, latents = pl.pallas_call(
        functools.partial(final_kernel, TICKS),
        out_shape=[
            jax.ShapeDtypeStruct(hidden.shape, hidden.dtype),
            jax.ShapeDtypeStruct(latents.shape, latents.dtype),
        ],
        in_specs=[smem, vmem, vmem, vmem],
        out_specs=[vmem, vmem],
        compiler_params=params,
        name="final",
    )(patch_lengths, embed_weight, embed_bias, received)
    return (hidden[None, None], latents[None, None], keys[None], values[None])


def solution(mesh):
    placed = (
        P("phase", "dp", None, None),
        P("phase", "dp", None, None),
        P("phase", "dp", None, None),
        P("phase", "dp", None, None),
        P("phase", "dp", None, None),
        P("phase", "dp", None, None),
        P("phase", None),
        P("phase", "dp", None),
        P("phase", "dp", None),
        P(),
        P(),
        P(),
        P(),
        P(),
        P("dp"),
        P("dp", None),
    )
    return jax.shard_map(
        shards,
        mesh=mesh,
        in_specs=placed,
        out_specs=(
            P("phase", "dp", None, None),
            P("phase", "dp", None, None),
            P("phase", "dp", None, None),
            P("phase", "dp", None, None),
        ),
        check_vma=False,
    )
```

time: 256 us -> 237 us (0.926); the launches traced: 252 us -> 236 us
  Pallas kernels: 0 us -> 130 us
  local copies, waits for them, and re-layouts: 125 us -> 0.07 us
  waiting for transfers between devices: 22.5 us -> 80.2 us
  matrix products: 55 us -> 0 us
  between operations: 24.1 us -> 0.91 us
  starting transfers between devices: 9.14 us -> 25.5 us
  other arithmetic: 16.3 us -> 0 us
    pallas_call x0 -> x7, Pallas kernels: none -> 130 us  [the longest x2 101 us: loaded(): pl.pallas_call(functools.partial(load_kernel, part, group, len(copied), f...]
    ppermute x6 -> x32, waiting for transfers between devices: 1.4 us -> 80.2 us  [the longest x29 51 us: moved(): return lax.ppermute(value, 'dp', pairs)]
    dot_general x15 -> x0, matrix products: 43.9 us -> none  [the longest x3 22.9 us: shards(): projected = jnp.dot(normed, qkv_full, preferred_element_type=jnp.float32)]
    dynamic_update_slice x6 -> x0, local copies, waits for them, and re-layouts: 31.3 us -> none  [place_rows(): canvas = lax.dynamic_update_slice_in_dim(canvas, fresh_rows, offset, 0)]
    unnamed x87 -> x22, local copies, waits for them, and re-layouts: 30.3 us -> 0.07 us
    concatenate x17 -> x0, local copies, waits for them, and re-layouts: 29.9 us -> none  [the longest x8 15.2 us: shards(): jnp.concatenate([text_k, cached_k, fresh_k], 0)]
    all_gather x2 -> x0, waiting for transfers between devices: 19.7 us -> none  [the longest x1 14.1 us: shards(): lax.all_gather(w_qkv, 'dp', axis=1, tiled=True)]
    ppermute x6 -> x32, starting transfers between devices: 9.06 us -> 25.5 us  [the longest x29 22.5 us: moved(): return lax.ppermute(value, 'dp', pairs)]
  transfers between devices with their start and end apart: 8 -> 32, of which waited for: 3 -> 15; matrix products, arithmetic and copies ran while one was open for 60% -> 0% of each run, Pallas kernels for 0% -> 43%
where the time goes in v1:
time: 237 us; the launch traced here: 236 us
  Pallas kernels  130 us (55%)
  waiting for transfers between devices  80.2 us (34%)
  starting transfers between devices  25.5 us (11%)
    pallas_call x2, Pallas kernels, loaded(): pl.pallas_call(functools.partial(load_kernel, part, group, len(copied), f...  101 us
    ppermute x29, waiting for transfers between devices, moved(): return lax.ppermute(value, 'dp', pairs)  51 us
    ppermute x3, waiting for transfers between devices, shifted(): return lax.ppermute(value, 'phase', pairs)  29.2 us
    pallas_call x3, Pallas kernels, shards(): pl.pallas_call(functools.partial(tick_kernel, tick, sections, first, part...  25.5 us
    ppermute x29, starting transfers between devices, moved(): return lax.ppermute(value, 'dp', pairs)  22.5 us
  transfers between devices with their start and end apart: 32, of which 15 were waited for; matrix products, arithmetic and copies ran while one was open for 0% of the time, Pallas kernels for 43%

profile of v1, /device:TPU:24, one launch (start us, length us, event | category | flops | bytes accessed | tf_op | source)
XLA Modules:
  0.0 236.1 jit_solution(8150634502690948512)
XLA Ops:
  0.6 1.7 own.1
  2.4 1.6 collective-permute-start.4
  4.0 0.6 collective-permute-start
  4.5 1.5 collective-permute-start.2
  6.0 0.7 collective-permute-start.3
  6.7 2.5 %collective-permute-start.1 = (bf16[48,6144]{1,0:T(8,128)(2,1)S(1)}, bf16[48,6144]{1,0:T(8,128)(2,1)S(1)}, u32[]{:S(2)}, u32[]{:S(2)}) collective-permute-start(bf16[48,6144]{1,0:T(8,128)(2,1)S(1)} %get-tuple-element.49), channel_id=1, source_target_pairs={{0,2},{1,3},{2,4},{3,5},{4,6},{5,7},{6,0},{7,1},{8,10},{9,11},{10,... | collective-permute-start | bytes 1769480 | tf_op jit(solution)/shard_map/ppermute | solution.py:33
  9.2 8.3 %collective-permute-done.4.refs_5_ = bf16[48,6144]{1,0:T(8,128)(2,1)S(1)} collective-permute-done((bf16[48,6144]{1,0:T(8,128)(2,1)S(1)}, bf16[48,6144]{1,0:T(8,128)(2,1)S(1)}, u32[]{:S(2)}, u32[]{:S(2)}) %collective-permute-start.4) | collective-permute-done | bytes 589856 | tf_op jit(solution)/shard_map/ppermute | solution.py:33
  17.5 1.5 collective-permute-start.5
  19.0 13.6 %collective-permute-done.3.refs_4_ = bf16[48,6144]{1,0:T(8,128)(2,1)S(1)} collective-permute-done((bf16[48,6144]{1,0:T(8,128)(2,1)S(1)}, bf16[48,6144]{1,0:T(8,128)(2,1)S(1)}, u32[]{:S(2)}, u32[]{:S(2)}) %collective-permute-start.3) | collective-permute-done | bytes 589856 | tf_op jit(solution)/shard_map/ppermute | solution.py:33
  33.1 2.7 %collective-permute-start.9 = (bf16[48,6144]{1,0:T(8,128)(2,1)S(1)}, bf16[48,6144]{1,0:T(8,128)(2,1)S(1)}, u32[]{:S(2)}, u32[]{:S(2)}) collective-permute-start(bf16[48,6144]{1,0:T(8,128)(2,1)S(1)} %collective-permute-done.refs_1_), channel_id=1, source_target_pairs={{0,2},{1,3},{2,4},{3,5},{4,6},{5,7},{6,0},{7,1},{8,10},{9,11},{10,... | collective-permute-start | bytes 1769480 | tf_op jit(solution)/shard_map/ppermute | solution.py:33
  36.6 10.6 %collective-permute-done.10.refs_2_ = bf16[48,6144]{1,0:T(8,128)(2,1)S(1)} collective-permute-done((bf16[48,6144]{1,0:T(8,128)(2,1)S(1)}, bf16[48,6144]{1,0:T(8,128)(2,1)S(1)}, u32[]{:S(2)}, u32[]{:S(2)}) %collective-permute-start.10) | collective-permute-done | bytes 589856 | tf_op jit(solution)/shard_map/ppermute | solution.py:33
  47.6 1.5 collective-permute-done.7.refs_8_
  49.1 0.8 collective-permute-done.8.refs_9_
  50.5 2.1 collective-permute-start.15
  52.8 98.7 %near.1 = (bf16[1536,6144]{1,0:T(8,128)(2,1)S(1)}, bf16[2,256,1536]{2,1,0:T(8,128)(2,1)}, bf16[2,256,1536]{2,1,0:T(8,128)(2,1)}) custom-call(bf16[96,6144]{1,0:T(8,128)(2,1)S(1)} %get-tuple-element.50.refs_0_, bf16[48,6144]{1,0:T(8,128)(2,1)S(1)} %collective-permute-done.refs_1_, bf16[48,6144]{1,0:T(8,128)(2,1)S(1)} %collective-permute-done.1.refs_2_, ...), custom_call_target="tpu_custom_call" | custom-call | tf_op jit(solution)/shard_map/near/pallas_call | solution.py:346
  153.0 0.8 collective-permute-done.18.refs_6_
  153.8 3.1 %collective-permute-start.23 = (bf16[48,6144]{1,0:T(8,128)(2,1)S(1)}, bf16[48,6144]{1,0:T(8,128)(2,1)S(1)}, u32[]{:S(2)}, u32[]{:S(2)}) collective-permute-start(bf16[48,6144]{1,0:T(8,128)(2,1)S(1)} %collective-permute-done.5.refs_6_), channel_id=1, source_target_pairs={{0,2},{1,3},{2,4},{3,5},{4,6},{5,7},{6,0},{7,1},{8,10},{9,11},{10,... | collective-permute-start | bytes 1769480 | tf_op jit(solution)/shard_map/ppermute | solution.py:33
  156.9 2.1 collective-permute-start.25
  159.1 2.1 middle.1
  161.3 8.5 %collective-permute-done.23.refs_15_ = bf16[48,6144]{1,0:T(8,128)(2,1)S(1)} collective-permute-done((bf16[48,6144]{1,0:T(8,128)(2,1)S(1)}, bf16[48,6144]{1,0:T(8,128)(2,1)S(1)}, u32[]{:S(2)}, u32[]{:S(2)}) %collective-permute-start.23) | collective-permute-done | bytes 589856 | tf_op jit(solution)/shard_map/ppermute | solution.py:33
  169.8 3.4 %collective-permute-done.24.refs_16_ = bf16[48,6144]{1,0:T(8,128)(2,1)S(1)} collective-permute-done((bf16[48,6144]{1,0:T(8,128)(2,1)S(1)}, bf16[48,6144]{1,0:T(8,128)(2,1)S(1)}, u32[]{:S(2)}, u32[]{:S(2)}) %collective-permute-start.24) | collective-permute-done | bytes 589856 | tf_op jit(solution)/shard_map/ppermute | solution.py:33
  173.7 1.5 collective-permute-done.26.refs_18_
  175.2 0.8 collective-permute-done.27.refs_19_
  176.1 0.8 collective-permute-done.28.refs_20_
  177.0 8.5 %tick0.1 = (bf16[2,256,1536]{2,1,0:T(8,128)(2,1)}, bf16[2,256,1536]{2,1,0:T(8,128)(2,1)}, bf16[1536,6144]{1,0:T(8,128)(2,1)S(1)}, bf16[48,1664]{1,0:T(8,128)(2,1)S(1)}) custom-call(s32[2,8]{1,0:T(2,128)S(1)} %copy-done.7, s32[2]{0:T(128)S(1)} %copy-done.8, f32[5]{0:T(128)S(1)} %copy-done.9, ...), custom_call_target="tpu_custom_call", output_to_operand_aliasing={{0}: (10, {}), {1}: (11, {}), {2}: (14, {})} | custom-call | tf_op jit(solution)/shard_map/tick0/pallas_call | solution.py:414
  185.5 2.8 %collective-permute-start.29 = (bf16[48,1664]{1,0:T(8,128)(2,1)S(1)}, bf16[48,1664]{1,0:T(8,128)(2,1)S(1)}, u32[]{:S(2)}, u32[]{:S(2)}) collective-permute-start(bf16[48,1664]{1,0:T(8,128)(2,1)S(1)} %get-tuple-element.78), channel_id=1, source_target_pairs={{0,16},{16,32},{32,48},{48,64},{64,80},{80,96},{96,112},{112,128},... | collective-permute-start | bytes 479240 | tf_op jit(solution)/shard_map/ppermute | solution.py:39
  188.4 11.1 %collective-permute-done.29.refs_12_ = bf16[48,1664]{1,0:T(8,128)(2,1)S(1)} collective-permute-done((bf16[48,1664]{1,0:T(8,128)(2,1)S(1)}, bf16[48,1664]{1,0:T(8,128)(2,1)S(1)}, u32[]{:S(2)}, u32[]{:S(2)}) %collective-permute-start.29) | collective-permute-done | bytes 159776 | tf_op jit(solution)/shard_map/ppermute | solution.py:39
  199.4 8.6 %tick1.1 = (bf16[2,256,1536]{2,1,0:T(8,128)(2,1)}, bf16[2,256,1536]{2,1,0:T(8,128)(2,1)}, bf16[48,1664]{1,0:T(8,128)(2,1)S(1)}) custom-call(s32[2,8]{1,0:T(2,128)S(1)} %copy-done.7, s32[2]{0:T(128)S(1)} %copy-done.8, f32[5]{0:T(128)S(1)} %copy-done.9, f32[1,1536]{1,0:T(1,128)S(1)} %copy-done.6, ...), custom_call_target="tpu_custom_call", output_to_operand_aliasing={{0}: (10, {}), {1}: (11, {})} | custom-call | tf_op jit(solution)/shard_map/tick1/pallas_call | solution.py:414
  208.1 9.2 %collective-permute-done.30.refs_12_ = bf16[48,1664]{1,0:T(8,128)(2,1)S(1)} collective-permute-done((bf16[48,1664]{1,0:T(8,128)(2,1)S(1)}, bf16[48,1664]{1,0:T(8,128)(2,1)S(1)}, u32[]{:S(2)}, u32[]{:S(2)}) %collective-permute-start.30) | collective-permute-done | bytes 159776 | tf_op jit(solution)/shard_map/ppermute | solution.py:39
  217.4 8.4 %tick2.1 = (bf16[2,256,1536]{2,1,0:T(8,128)(2,1)}, bf16[2,256,1536]{2,1,0:T(8,128)(2,1)}, bf16[48,1664]{1,0:T(8,128)(2,1)S(1)}) custom-call(s32[2,8]{1,0:T(2,128)S(1)} %copy-done.7, s32[2]{0:T(128)S(1)} %copy-done.8, f32[5]{0:T(128)S(1)} %copy-done.9, f32[1,1536]{1,0:T(1,128)S(1)} %copy-done.6, ...), custom_call_target="tpu_custom_call", output_to_operand_aliasing={{0}: (10, {}), {1}: (11, {})} | custom-call | tf_op jit(solution)/shard_map/tick2/pallas_call | solution.py:414
  225.9 8.9 %collective-permute-done.31.received = bf16[48,1664]{1,0:T(8,128)(2,1)S(1)} collective-permute-done((bf16[48,1664]{1,0:T(8,128)(2,1)S(1)}, bf16[48,1664]{1,0:T(8,128)(2,1)S(1)}, u32[]{:S(2)}, u32[]{:S(2)}) %collective-permute-start.31) | collective-permute-done | bytes 159776 | tf_op jit(solution)/shard_map/ppermute | solution.py:39
  234.7 1.4 final.1
  (61 shorter events, 4.7 us)
Async XLA Ops:
  2.4 15.2 %collective-permute-start.4 = (bf16[48,6144]{1,0:T(8,128)(2,1)S(1)}, bf16[48,6144]{1,0:T(8,128)(2,1)S(1)}, u32[]{:S(2)}, u32[]{:S(2)}) collective-permute-start(bf16[48,6144]{1,0:T(8,128)(2,1)S(1)} %get-tuple-element.47), channel_id=1, source_target_pairs={{0,8},{1,9},{2,10},{3,11},{4,12},{5,13},{6,14},{7,15},{8,0},{9,1},... | collective-permute-start | bytes 1769480 | tf_op jit(solution)/shard_map/ppermute | solution.py:33
  4.0 29.2 %collective-permute-start = (bf16[48,6144]{1,0:T(8,128)(2,1)S(1)}, bf16[48,6144]{1,0:T(8,128)(2,1)S(1)}, u32[]{:S(2)}, u32[]{:S(2)}) collective-permute-start(bf16[48,6144]{1,0:T(8,128)(2,1)S(1)} %get-tuple-element.47), channel_id=1, source_target_pairs={{0,2},{1,3},{2,4},{3,5},{4,6},{5,7},{6,0},{7,1},{8,10},{9,11},{10,... | collective-permute-start | bytes 1769480 | tf_op jit(solution)/shard_map/ppermute | solution.py:33
  4.5 31.3 %collective-permute-start.2 = (bf16[48,6144]{1,0:T(8,128)(2,1)S(1)}, bf16[48,6144]{1,0:T(8,128)(2,1)S(1)}, u32[]{:S(2)}, u32[]{:S(2)}) collective-permute-start(bf16[48,6144]{1,0:T(8,128)(2,1)S(1)} %get-tuple-element.47), channel_id=1, source_target_pairs={{0,6},{1,7},{2,0},{3,1},{4,2},{5,3},{6,4},{7,5},{8,14},{9,15},{10,... | collective-permute-start | bytes 1769480 | tf_op jit(solution)/shard_map/ppermute | solution.py:33
  6.0 26.6 %collective-permute-start.3 = (bf16[48,6144]{1,0:T(8,128)(2,1)S(1)}, bf16[48,6144]{1,0:T(8,128)(2,1)S(1)}, u32[]{:S(2)}, u32[]{:S(2)}) collective-permute-start(bf16[48,6144]{1,0:T(8,128)(2,1)S(1)} %get-tuple-element.49), channel_id=1, source_target_pairs={{0,6},{1,7},{2,0},{3,1},{4,2},{5,3},{6,4},{7,5},{8,14},{9,15},{10,... | collective-permute-start | bytes 1769480 | tf_op jit(solution)/shard_map/ppermute | solution.py:33
  6.7 29.1 %collective-permute-start.1 = (bf16[48,6144]{1,0:T(8,128)(2,1)S(1)}, bf16[48,6144]{1,0:T(8,128)(2,1)S(1)}, u32[]{:S(2)}, u32[]{:S(2)}) collective-permute-start(bf16[48,6144]{1,0:T(8,128)(2,1)S(1)} %get-tuple-element.49), channel_id=1, source_target_pairs={{0,2},{1,3},{2,4},{3,5},{4,6},{5,7},{6,0},{7,1},{8,10},{9,11},{10,... | collective-permute-start | bytes 1769480 | tf_op jit(solution)/shard_map/ppermute | solution.py:33
  17.5 18.3 %collective-permute-start.5 = (bf16[48,6144]{1,0:T(8,128)(2,1)S(1)}, bf16[48,6144]{1,0:T(8,128)(2,1)S(1)}, u32[]{:S(2)}, u32[]{:S(2)}) collective-permute-start(bf16[48,6144]{1,0:T(8,128)(2,1)S(1)} %get-tuple-element.49), channel_id=1, source_target_pairs={{0,8},{1,9},{2,10},{3,11},{4,12},{5,13},{6,14},{7,15},{8,0},{9,1},... | collective-permute-start | bytes 1769480 | tf_op jit(solution)/shard_map/ppermute | solution.py:33
  32.6 14.5 %collective-permute-start.10 = (bf16[48,6144]{1,0:T(8,128)(2,1)S(1)}, bf16[48,6144]{1,0:T(8,128)(2,1)S(1)}, u32[]{:S(2)}, u32[]{:S(2)}) collective-permute-start(bf16[48,6144]{1,0:T(8,128)(2,1)S(1)} %collective-permute-done.3.refs_4_), channel_id=1, source_target_pairs={{0,6},{1,7},{2,0},{3,1},{4,2},{5,3},{6,4},{7,5},{8,14},{9,15},{10,... | collective-permute-start | bytes 1769480 | tf_op jit(solution)/shard_map/ppermute | solution.py:33
  33.1 14.0 %collective-permute-start.9 = (bf16[48,6144]{1,0:T(8,128)(2,1)S(1)}, bf16[48,6144]{1,0:T(8,128)(2,1)S(1)}, u32[]{:S(2)}, u32[]{:S(2)}) collective-permute-start(bf16[48,6144]{1,0:T(8,128)(2,1)S(1)} %collective-permute-done.refs_1_), channel_id=1, source_target_pairs={{0,2},{1,3},{2,4},{3,5},{4,6},{5,7},{6,0},{7,1},{8,10},{9,11},{10,... | collective-permute-start | bytes 1769480 | tf_op jit(solution)/shard_map/ppermute | solution.py:33
  35.9 14.1 %collective-permute-start.6 = (bf16[96,6144]{1,0:T(8,128)(2,1)S(1)}, bf16[96,6144]{1,0:T(8,128)(2,1)S(1)}, u32[]{:S(2)}, u32[]{:S(2)}) collective-permute-start(bf16[96,6144]{1,0:T(8,128)(2,1)S(1)} %get-tuple-element.50.refs_0_), channel_id=1, source_target_pairs={{0,1},{1,0},{2,3},{3,2},{4,5},{5,4},{6,7},{7,6},{8,9},{9,8},{10,11... | collective-permute-start | bytes 3538952 | tf_op jit(solution)/shard_map/ppermute | solution.py:33
  36.0 11.7 %collective-permute-start.11 = (bf16[48,6144]{1,0:T(8,128)(2,1)S(1)}, bf16[48,6144]{1,0:T(8,128)(2,1)S(1)}, u32[]{:S(2)}, u32[]{:S(2)}) collective-permute-start(bf16[48,6144]{1,0:T(8,128)(2,1)S(1)} %collective-permute-done.3.refs_4_), channel_id=1, source_target_pairs={{0,1},{1,0},{2,3},{3,2},{4,5},{5,4},{6,7},{7,6},{8,9},{9,8},{10,11... | collective-permute-start | bytes 1769480 | tf_op jit(solution)/shard_map/ppermute | solution.py:33
  36.5 11.2 %collective-permute-start.12 = (bf16[48,6144]{1,0:T(8,128)(2,1)S(1)}, bf16[48,6144]{1,0:T(8,128)(2,1)S(1)}, u32[]{:S(2)}, u32[]{:S(2)}) collective-permute-start(bf16[48,6144]{1,0:T(8,128)(2,1)S(1)} %collective-permute-done.4.refs_5_), channel_id=1, source_target_pairs={{0,1},{1,0},{2,3},{3,2},{4,5},{5,4},{6,7},{7,6},{8,9},{9,8},{10,11... | collective-permute-start | bytes 1769480 | tf_op jit(solution)/shard_map/ppermute | solution.py:33
  47.1 2.0 collective-permute-start.7
  47.1 2.8 %collective-permute-start.8 = (bf16[48,6144]{1,0:T(8,128)(2,1)S(1)}, bf16[48,6144]{1,0:T(8,128)(2,1)S(1)}, u32[]{:S(2)}, u32[]{:S(2)}) collective-permute-start(bf16[48,6144]{1,0:T(8,128)(2,1)S(1)} %collective-permute-done.1.refs_2_), channel_id=1, source_target_pairs={{0,1},{1,0},{2,3},{3,2},{4,5},{5,4},{6,7},{7,6},{8,9},{9,8},{10,11... | collective-permute-start | bytes 1769480 | tf_op jit(solution)/shard_map/ppermute | solution.py:33
  50.0 2.6 %collective-permute-start.13 = (bf16[48,6144]{1,0:T(8,128)(2,1)S(1)}, bf16[48,6144]{1,0:T(8,128)(2,1)S(1)}, u32[]{:S(2)}, u32[]{:S(2)}) collective-permute-start(bf16[48,6144]{1,0:T(8,128)(2,1)S(1)} %collective-permute-done.2.refs_3_), channel_id=1, source_target_pairs={{0,1},{1,0},{2,3},{3,2},{4,5},{5,4},{6,7},{7,6},{8,9},{9,8},{10,11... | collective-permute-start | bytes 1769480 | tf_op jit(solution)/shard_map/ppermute | solution.py:33
  50.1 2.7 %collective-permute-start.14 = (bf16[48,6144]{1,0:T(8,128)(2,1)S(1)}, bf16[48,6144]{1,0:T(8,128)(2,1)S(1)}, u32[]{:S(2)}, u32[]{:S(2)}) collective-permute-start(bf16[48,6144]{1,0:T(8,128)(2,1)S(1)} %collective-permute-done.5.refs_6_), channel_id=1, source_target_pairs={{0,1},{1,0},{2,3},{3,2},{4,5},{5,4},{6,7},{7,6},{8,9},{9,8},{10,11... | collective-permute-start | bytes 1769480 | tf_op jit(solution)/shard_map/ppermute | solution.py:33
  50.5 101.1 %collective-permute-start.15 = (bf16[48,6144]{1,0:T(8,128)(2,1)S(1)}, bf16[48,6144]{1,0:T(8,128)(2,1)S(1)}, u32[]{:S(2)}, u32[]{:S(2)}) collective-permute-start(bf16[48,6144]{1,0:T(8,128)(2,1)S(1)} %collective-permute-done.4.refs_5_), channel_id=1, source_target_pairs={{0,2},{1,3},{2,4},{3,5},{4,6},{5,7},{6,0},{7,1},{8,10},{9,11},{10,... | collective-permute-start | bytes 1769480 | tf_op jit(solution)/shard_map/ppermute | solution.py:33
  52.6 98.9 %collective-permute-start.16 = (bf16[48,6144]{1,0:T(8,128)(2,1)S(1)}, bf16[48,6144]{1,0:T(8,128)(2,1)S(1)}, u32[]{:S(2)}, u32[]{:S(2)}) collective-permute-start(bf16[48,6144]{1,0:T(8,128)(2,1)S(1)} %collective-permute-done.4.refs_5_), channel_id=1, source_target_pairs={{0,6},{1,7},{2,0},{3,1},{4,2},{5,3},{6,4},{7,5},{8,14},{9,15},{10,... | collective-permute-start | bytes 1769480 | tf_op jit(solution)/shard_map/ppermute | solution.py:33
  52.6 99.0 %collective-permute-start.17 = (bf16[48,6144]{1,0:T(8,128)(2,1)S(1)}, bf16[48,6144]{1,0:T(8,128)(2,1)S(1)}, u32[]{:S(2)}, u32[]{:S(2)}) collective-permute-start(bf16[48,6144]{1,0:T(8,128)(2,1)S(1)} %collective-permute-done.9.refs_1_), channel_id=1, source_target_pairs={{0,8},{1,9},{2,10},{3,11},{4,12},{5,13},{6,14},{7,15},{8,0},{9,1},... | collective-permute-start | bytes 1769480 | tf_op jit(solution)/shard_map/ppermute | solution.py:33
  151.6 2.3 collective-permute-start.18
  152.0 4.9 %collective-permute-start.19 = (bf16[48,6144]{1,0:T(8,128)(2,1)S(1)}, bf16[48,6144]{1,0:T(8,128)(2,1)S(1)}, u32[]{:S(2)}, u32[]{:S(2)}) collective-permute-start(bf16[48,6144]{1,0:T(8,128)(2,1)S(1)} %collective-permute-done.10.refs_2_), channel_id=1, source_target_pairs={{0,1},{1,0},{2,3},{3,2},{4,5},{5,4},{6,7},{7,6},{8,9},{9,8},{10,11... | collective-permute-start | bytes 1769480 | tf_op jit(solution)/shard_map/ppermute | solution.py:33
  152.3 4.6 %collective-permute-start.20 = (bf16[48,6144]{1,0:T(8,128)(2,1)S(1)}, bf16[48,6144]{1,0:T(8,128)(2,1)S(1)}, u32[]{:S(2)}, u32[]{:S(2)}) collective-permute-start(bf16[48,6144]{1,0:T(8,128)(2,1)S(1)} %collective-permute-done.15.refs_3_), channel_id=1, source_target_pairs={{0,1},{1,0},{2,3},{3,2},{4,5},{5,4},{6,7},{7,6},{8,9},{9,8},{10,11... | collective-permute-start | bytes 1769480 | tf_op jit(solution)/shard_map/ppermute | solution.py:33
  152.5 6.5 %collective-permute-start.21 = (bf16[48,6144]{1,0:T(8,128)(2,1)S(1)}, bf16[48,6144]{1,0:T(8,128)(2,1)S(1)}, u32[]{:S(2)}, u32[]{:S(2)}) collective-permute-start(bf16[48,6144]{1,0:T(8,128)(2,1)S(1)} %collective-permute-done.16.refs_4_), channel_id=1, source_target_pairs={{0,1},{1,0},{2,3},{3,2},{4,5},{5,4},{6,7},{7,6},{8,9},{9,8},{10,11... | collective-permute-start | bytes 1769480 | tf_op jit(solution)/shard_map/ppermute | solution.py:33
  152.9 6.1 %collective-permute-start.22 = (bf16[48,6144]{1,0:T(8,128)(2,1)S(1)}, bf16[48,6144]{1,0:T(8,128)(2,1)S(1)}, u32[]{:S(2)}, u32[]{:S(2)}) collective-permute-start(bf16[48,6144]{1,0:T(8,128)(2,1)S(1)} %collective-permute-done.17.refs_5_), channel_id=1, source_target_pairs={{0,1},{1,0},{2,3},{3,2},{4,5},{5,4},{6,7},{7,6},{8,9},{9,8},{10,11... | collective-permute-start | bytes 1769480 | tf_op jit(solution)/shard_map/ppermute | solution.py:33
  153.8 16.0 %collective-permute-start.23 = (bf16[48,6144]{1,0:T(8,128)(2,1)S(1)}, bf16[48,6144]{1,0:T(8,128)(2,1)S(1)}, u32[]{:S(2)}, u32[]{:S(2)}) collective-permute-start(bf16[48,6144]{1,0:T(8,128)(2,1)S(1)} %collective-permute-done.5.refs_6_), channel_id=1, source_target_pairs={{0,2},{1,3},{2,4},{3,5},{4,6},{5,7},{6,0},{7,1},{8,10},{9,11},{10,... | collective-permute-start | bytes 1769480 | tf_op jit(solution)/shard_map/ppermute | solution.py:33
  156.9 16.3 %collective-permute-start.24 = (bf16[48,6144]{1,0:T(8,128)(2,1)S(1)}, bf16[48,6144]{1,0:T(8,128)(2,1)S(1)}, u32[]{:S(2)}, u32[]{:S(2)}) collective-permute-start(bf16[48,6144]{1,0:T(8,128)(2,1)S(1)} %collective-permute-done.5.refs_6_), channel_id=1, source_target_pairs={{0,6},{1,7},{2,0},{3,1},{4,2},{5,3},{6,4},{7,5},{8,14},{9,15},{10,... | collective-permute-start | bytes 1769480 | tf_op jit(solution)/shard_map/ppermute | solution.py:33
  156.9 16.3 %collective-permute-start.25 = (bf16[48,6144]{1,0:T(8,128)(2,1)S(1)}, bf16[48,6144]{1,0:T(8,128)(2,1)S(1)}, u32[]{:S(2)}, u32[]{:S(2)}) collective-permute-start(bf16[48,6144]{1,0:T(8,128)(2,1)S(1)} %collective-permute-done.10.refs_2_), channel_id=1, source_target_pairs={{0,8},{1,9},{2,10},{3,11},{4,12},{5,13},{6,14},{7,15},{8,0},{9,1},... | collective-permute-start | bytes 1769480 | tf_op jit(solution)/shard_map/ppermute | solution.py:33
  173.2 2.0 collective-permute-start.26
  173.2 2.8 %collective-permute-start.27 = (bf16[48,6144]{1,0:T(8,128)(2,1)S(1)}, bf16[48,6144]{1,0:T(8,128)(2,1)S(1)}, u32[]{:S(2)}, u32[]{:S(2)}) collective-permute-start(bf16[48,6144]{1,0:T(8,128)(2,1)S(1)} %collective-permute-done.24.refs_16_), channel_id=1, source_target_pairs={{0,1},{1,0},{2,3},{3,2},{4,5},{5,4},{6,7},{7,6},{8,9},{9,8},{10,11... | collective-permute-start | bytes 1769480 | tf_op jit(solution)/shard_map/ppermute | solution.py:33
  173.7 3.2 %collective-permute-start.28 = (bf16[48,6144]{1,0:T(8,128)(2,1)S(1)}, bf16[48,6144]{1,0:T(8,128)(2,1)S(1)}, u32[]{:S(2)}, u32[]{:S(2)}) collective-permute-start(bf16[48,6144]{1,0:T(8,128)(2,1)S(1)} %collective-permute-done.25.refs_17_), channel_id=1, source_target_pairs={{0,1},{1,0},{2,3},{3,2},{4,5},{5,4},{6,7},{7,6},{8,9},{9,8},{10,11... | collective-permute-start | bytes 1769480 | tf_op jit(solution)/shard_map/ppermute | solution.py:33
  185.5 13.9 %collective-permute-start.29 = (bf16[48,1664]{1,0:T(8,128)(2,1)S(1)}, bf16[48,1664]{1,0:T(8,128)(2,1)S(1)}, u32[]{:S(2)}, u32[]{:S(2)}) collective-permute-start(bf16[48,1664]{1,0:T(8,128)(2,1)S(1)} %get-tuple-element.78), channel_id=1, source_target_pairs={{0,16},{16,32},{32,48},{48,64},{64,80},{80,96},{96,112},{112,128},... | collective-permute-start | bytes 479240 | tf_op jit(solution)/shard_map/ppermute | solution.py:39
  208.0 9.3 %collective-permute-start.30 = (bf16[48,1664]{1,0:T(8,128)(2,1)S(1)}, bf16[48,1664]{1,0:T(8,128)(2,1)S(1)}, u32[]{:S(2)}, u32[]{:S(2)}) collective-permute-start(bf16[48,1664]{1,0:T(8,128)(2,1)S(1)} %get-tuple-element.82), channel_id=1, source_target_pairs={{0,16},{16,32},{32,48},{48,64},{64,80},{80,96},{96,112},{112,128},... | collective-permute-start | bytes 479240 | tf_op jit(solution)/shard_map/ppermute | solution.py:39
  225.8 9.0 %collective-permute-start.31 = (bf16[48,1664]{1,0:T(8,128)(2,1)S(1)}, bf16[48,1664]{1,0:T(8,128)(2,1)S(1)}, u32[]{:S(2)}, u32[]{:S(2)}) collective-permute-start(bf16[48,1664]{1,0:T(8,128)(2,1)S(1)} %get-tuple-element.83), channel_id=1, source_target_pairs={{0,16},{16,32},{32,48},{48,64},{64,80},{80,96},{96,112},{112,128},... | collective-permute-start | bytes 479240 | tf_op jit(solution)/shard_map/ppermute | solution.py:39
  (11 other events, 196.9 us)

commit v2 on v1

--- a/solution.py
+++ b/solution.py
@@ -156,14 +156,23 @@
         refs = refs[1:]
     count = len(group)
     pieces, sources, refs = refs[:count], refs[count : count + copied], refs[count + copied :]
-    weights, targets, (sems, copy_sems) = refs[0], refs[1 : 1 + copied], refs[1 + copied :]
-    run_copies(
-        weight_copies(pieces, weights, rows, group, sems)
-        + [
-            pltpu.make_async_copy(source, target, copy_sems.at[at])
-            for at, (source, target) in enumerate(zip(sources, targets))
-        ]
-    )
+    weights, targets, (sems, copy_sems, *stages) = refs[0], refs[1 : 1 + copied], refs[1 + copied :]
+    inward = [
+        pltpu.make_async_copy(source, stage, copy_sems.at[at, 0])
+        for at, (source, stage) in enumerate(zip(sources, stages))
+    ]
+    outward = [
+        pltpu.make_async_copy(stage, target, copy_sems.at[at, 1])
+        for at, (stage, target) in enumerate(zip(stages, targets))
+    ]
+    copies = weight_copies(pieces, weights, rows, group, sems)
+    for copy in inward + copies:
+        copy.start()
+    for copy, onward in zip(inward, outward):
+        copy.wait()
+        onward.start()
+    for copy in copies + outward:
+        copy.wait()
 
 
 def tick_kernel(tick, sections, first, rows, *refs):
@@ -324,7 +333,7 @@
     small = [norm_gain, embed_weight, embed_bias, head_weight.T, head_bias]
     texts = [text_keys[0], text_values[0]]
     params = pltpu.CompilerParams(vmem_limit_bytes=GRANT)
-    small_params = pltpu.CompilerParams(vmem_limit_bytes=GRANT // 8)
+    small_params = pltpu.CompilerParams(vmem_limit_bytes=GRANT // 2)
 
     full = part * lax.axis_size("dp")
     total = w_qkv.shape[2] + w_out.shape[2]
@@ -351,7 +360,8 @@
             out_specs=[vmem] + [hbm] * len(copied),
             scratch_shapes=[
                 pltpu.SemaphoreType.DMA((len(pieces),)),
-                pltpu.SemaphoreType.DMA((max(len(copied), 1),)),
+                pltpu.SemaphoreType.DMA((max(len(copied), 1), 2)),
+                *[pltpu.VMEM(array.shape, array.dtype) for array in copied],
             ],
             input_output_aliases={} if first else {0: 0},
             compiler_params=small_params,

time: 237 us -> 151 us (0.64)
  Pallas kernels: 130 us -> 34.2 us
  waiting for transfers between devices: 80.2 us -> 94.5 us
  starting transfers between devices: 25.5 us -> 21.6 us
    pallas_call x2, Pallas kernels: 101 us -> 5.48 us  [loaded(): pl.pallas_call(functools.partial(load_kernel, part, group, len(copied), f...]
    ppermute x29, waiting for transfers between devices: 51 us -> 65.6 us  [moved(): return lax.ppermute(value, 'dp', pairs)]
    ppermute x29, starting transfers between devices: 22.5 us -> 19.1 us  [moved(): return lax.ppermute(value, 'dp', pairs)]
  transfers between devices with their start and end apart: 32 -> 32, of which waited for: 15 -> 19; matrix products, arithmetic and copies ran while one was open for 0% -> 0% of each run, Pallas kernels for 43% -> 4%
where the time goes in v2:
time: 151 us
  waiting for transfers between devices  94.5 us (63%)
  Pallas kernels  34.2 us (23%)
  starting transfers between devices  21.6 us (14%)
    ppermute x29, waiting for transfers between devices, moved(): return lax.ppermute(value, 'dp', pairs)  65.6 us
    ppermute x3, waiting for transfers between devices, shifted(): return lax.ppermute(value, 'phase', pairs)  28.9 us
    pallas_call x3, Pallas kernels, shards(): pl.pallas_call(functools.partial(tick_kernel, tick, sections, first, part...  25.5 us
    ppermute x29, starting transfers between devices, moved(): return lax.ppermute(value, 'dp', pairs)  19.1 us
    pallas_call x2, Pallas kernels, loaded(): pl.pallas_call(functools.partial(load_kernel, part, group, len(copied), f...  5.48 us
  transfers between devices with their start and end apart: 32, of which 19 were waited for; matrix products, arithmetic and copies ran while one was open for 0% of the time, Pallas kernels for 4%

profile of v2, /device:TPU:24, one launch (start us, length us, event | category | flops | bytes accessed | tf_op | source)
XLA Modules:
  0.0 151.1 jit_solution(6287061636133513959)
XLA Ops:
  0.6 1.7 %own.1 = (bf16[48,6144]{1,0:T(8,128)(2,1)S(1)}, bf16[48,6144]{1,0:T(8,128)(2,1)S(1)}, bf16[96,6144]{1,0:T(8,128)(2,1)S(1)}) custom-call(bf16[96,4608]{1,0:T(8,128)(2,1)} %bitcast.27, bf16[96,1536]{1,0:T(8,128)(2,1)} %bitcast.28), custom_call_target="tpu_custom_call" | custom-call | tf_op jit(solution)/shard_map/own/pallas_call | solution.py:341
  2.4 1.6 %collective-permute-start.4 = (bf16[48,6144]{1,0:T(8,128)(2,1)S(1)}, bf16[48,6144]{1,0:T(8,128)(2,1)S(1)}, u32[]{:S(2)}, u32[]{:S(2)}) collective-permute-start(bf16[48,6144]{1,0:T(8,128)(2,1)S(1)} %get-tuple-element.47), channel_id=1, source_target_pairs={{0,8},{1,9},{2,10},{3,11},{4,12},{5,13},{6,14},{7,15},{8,0},{9,1},... | collective-permute-start | bytes 1769480 | tf_op jit(solution)/shard_map/ppermute | solution.py:33
  4.5 1.5 collective-permute-start.2
  6.7 2.5 %collective-permute-start.1 = (bf16[48,6144]{1,0:T(8,128)(2,1)S(1)}, bf16[48,6144]{1,0:T(8,128)(2,1)S(1)}, u32[]{:S(2)}, u32[]{:S(2)}) collective-permute-start(bf16[48,6144]{1,0:T(8,128)(2,1)S(1)} %get-tuple-element.49), channel_id=1, source_target_pairs={{0,2},{1,3},{2,4},{3,5},{4,6},{5,7},{6,0},{7,1},{8,10},{9,11},{10,... | collective-permute-start | bytes 1769480 | tf_op jit(solution)/shard_map/ppermute | solution.py:33
  9.2 8.3 %collective-permute-done.4.refs_5_ = bf16[48,6144]{1,0:T(8,128)(2,1)S(1)} collective-permute-done((bf16[48,6144]{1,0:T(8,128)(2,1)S(1)}, bf16[48,6144]{1,0:T(8,128)(2,1)S(1)}, u32[]{:S(2)}, u32[]{:S(2)}) %collective-permute-start.4) | collective-permute-done | bytes 589856 | tf_op jit(solution)/shard_map/ppermute | solution.py:33
  17.5 1.5 collective-permute-start.5
  19.0 13.6 %collective-permute-done.3.refs_4_ = bf16[48,6144]{1,0:T(8,128)(2,1)S(1)} collective-permute-done((bf16[48,6144]{1,0:T(8,128)(2,1)S(1)}, bf16[48,6144]{1,0:T(8,128)(2,1)S(1)}, u32[]{:S(2)}, u32[]{:S(2)}) %collective-permute-start.3) | collective-permute-done | bytes 589856 | tf_op jit(solution)/shard_map/ppermute | solution.py:33
  33.1 2.7 %collective-permute-start.9 = (bf16[48,6144]{1,0:T(8,128)(2,1)S(1)}, bf16[48,6144]{1,0:T(8,128)(2,1)S(1)}, u32[]{:S(2)}, u32[]{:S(2)}) collective-permute-start(bf16[48,6144]{1,0:T(8,128)(2,1)S(1)} %collective-permute-done.refs_1_), channel_id=1, source_target_pairs={{0,2},{1,3},{2,4},{3,5},{4,6},{5,7},{6,0},{7,1},{8,10},{9,11},{10,... | collective-permute-start | bytes 1769480 | tf_op jit(solution)/shard_map/ppermute | solution.py:33
  36.6 10.6 %collective-permute-done.10.refs_2_ = bf16[48,6144]{1,0:T(8,128)(2,1)S(1)} collective-permute-done((bf16[48,6144]{1,0:T(8,128)(2,1)S(1)}, bf16[48,6144]{1,0:T(8,128)(2,1)S(1)}, u32[]{:S(2)}, u32[]{:S(2)}) %collective-permute-start.10) | collective-permute-done | bytes 589856 | tf_op jit(solution)/shard_map/ppermute | solution.py:33
  47.6 1.5 collective-permute-done.7.refs_8_
  49.1 0.8 collective-permute-done.8.refs_9_
  50.5 2.1 %collective-permute-start.15 = (bf16[48,6144]{1,0:T(8,128)(2,1)S(1)}, bf16[48,6144]{1,0:T(8,128)(2,1)S(1)}, u32[]{:S(2)}, u32[]{:S(2)}) collective-permute-start(bf16[48,6144]{1,0:T(8,128)(2,1)S(1)} %collective-permute-done.4.refs_5_), channel_id=1, source_target_pairs={{0,2},{1,3},{2,4},{3,5},{4,6},{5,7},{6,0},{7,1},{8,10},{9,11},{10,... | collective-permute-start | bytes 1769480 | tf_op jit(solution)/shard_map/ppermute | solution.py:33
  52.8 4.0 %near.1 = (bf16[1536,6144]{1,0:T(8,128)(2,1)S(1)}, bf16[2,256,1536]{2,1,0:T(8,128)(2,1)}, bf16[2,256,1536]{2,1,0:T(8,128)(2,1)}) custom-call(bf16[96,6144]{1,0:T(8,128)(2,1)S(1)} %get-tuple-element.50.refs_0_, bf16[48,6144]{1,0:T(8,128)(2,1)S(1)} %collective-permute-done.refs_1_, bf16[48,6144]{1,0:T(8,128)(2,1)S(1)} %collective-permute-done.1.refs_2_, ...), custom_call_target="tpu_custom_call" | custom-call | tf_op jit(solution)/shard_map/near/pallas_call | solution.py:355
  56.8 9.0 %collective-permute-done.15.refs_3_ = bf16[48,6144]{1,0:T(8,128)(2,1)S(1)} collective-permute-done((bf16[48,6144]{1,0:T(8,128)(2,1)S(1)}, bf16[48,6144]{1,0:T(8,128)(2,1)S(1)}, u32[]{:S(2)}, u32[]{:S(2)}) %collective-permute-start.15) | collective-permute-done | bytes 589856 | tf_op jit(solution)/shard_map/ppermute | solution.py:33
  65.9 3.0 %collective-permute-done.16.refs_4_ = bf16[48,6144]{1,0:T(8,128)(2,1)S(1)} collective-permute-done((bf16[48,6144]{1,0:T(8,128)(2,1)S(1)}, bf16[48,6144]{1,0:T(8,128)(2,1)S(1)}, u32[]{:S(2)}, u32[]{:S(2)}) %collective-permute-start.16) | collective-permute-done | bytes 589856 | tf_op jit(solution)/shard_map/ppermute | solution.py:33
  69.9 1.0 collective-permute-done.18.refs_6_
  70.9 1.7 %collective-permute-start.23 = (bf16[48,6144]{1,0:T(8,128)(2,1)S(1)}, bf16[48,6144]{1,0:T(8,128)(2,1)S(1)}, u32[]{:S(2)}, u32[]{:S(2)}) collective-permute-start(bf16[48,6144]{1,0:T(8,128)(2,1)S(1)} %collective-permute-done.5.refs_6_), channel_id=1, source_target_pairs={{0,2},{1,3},{2,4},{3,5},{4,6},{5,7},{6,0},{7,1},{8,10},{9,11},{10,... | collective-permute-start | bytes 1769480 | tf_op jit(solution)/shard_map/ppermute | solution.py:33
  73.4 0.8 collective-permute-done.22.refs_10_
  74.4 1.5 middle.1
  75.9 10.4 %collective-permute-done.23.refs_15_ = bf16[48,6144]{1,0:T(8,128)(2,1)S(1)} collective-permute-done((bf16[48,6144]{1,0:T(8,128)(2,1)S(1)}, bf16[48,6144]{1,0:T(8,128)(2,1)S(1)}, u32[]{:S(2)}, u32[]{:S(2)}) %collective-permute-start.23) | collective-permute-done | bytes 589856 | tf_op jit(solution)/shard_map/ppermute | solution.py:33
  86.3 2.7 %collective-permute-done.24.refs_16_ = bf16[48,6144]{1,0:T(8,128)(2,1)S(1)} collective-permute-done((bf16[48,6144]{1,0:T(8,128)(2,1)S(1)}, bf16[48,6144]{1,0:T(8,128)(2,1)S(1)}, u32[]{:S(2)}, u32[]{:S(2)}) %collective-permute-start.24) | collective-permute-done | bytes 589856 | tf_op jit(solution)/shard_map/ppermute | solution.py:33
  89.5 1.5 collective-permute-done.26.refs_18_
  91.0 0.8 collective-permute-done.27.refs_19_
  91.8 0.8 collective-permute-done.28.refs_20_
  92.7 8.5 %tick0.1 = (bf16[2,256,1536]{2,1,0:T(8,128)(2,1)}, bf16[2,256,1536]{2,1,0:T(8,128)(2,1)}, bf16[1536,6144]{1,0:T(8,128)(2,1)S(1)}, bf16[48,1664]{1,0:T(8,128)(2,1)S(1)}) custom-call(s32[2,8]{1,0:T(2,128)S(1)} %copy-done.7, s32[2]{0:T(128)S(1)} %copy-done.8, f32[5]{0:T(128)S(1)} %copy-done.9, ...), custom_call_target="tpu_custom_call", output_to_operand_aliasing={{0}: (10, {}), {1}: (11, {}), {2}: (14, {})} | custom-call | tf_op jit(solution)/shard_map/tick0/pallas_call | solution.py:424
  101.3 2.3 %collective-permute-start.29 = (bf16[48,1664]{1,0:T(8,128)(2,1)S(1)}, bf16[48,1664]{1,0:T(8,128)(2,1)S(1)}, u32[]{:S(2)}, u32[]{:S(2)}) collective-permute-start(bf16[48,1664]{1,0:T(8,128)(2,1)S(1)} %get-tuple-element.78), channel_id=1, source_target_pairs={{0,16},{16,32},{32,48},{48,64},{64,80},{80,96},{96,112},{112,128},... | collective-permute-start | bytes 479240 | tf_op jit(solution)/shard_map/ppermute | solution.py:39
  103.6 10.8 %collective-permute-done.29.refs_12_ = bf16[48,1664]{1,0:T(8,128)(2,1)S(1)} collective-permute-done((bf16[48,1664]{1,0:T(8,128)(2,1)S(1)}, bf16[48,1664]{1,0:T(8,128)(2,1)S(1)}, u32[]{:S(2)}, u32[]{:S(2)}) %collective-permute-start.29) | collective-permute-done | bytes 159776 | tf_op jit(solution)/shard_map/ppermute | solution.py:39
  114.4 8.6 %tick1.1 = (bf16[2,256,1536]{2,1,0:T(8,128)(2,1)}, bf16[2,256,1536]{2,1,0:T(8,128)(2,1)}, bf16[48,1664]{1,0:T(8,128)(2,1)S(1)}) custom-call(s32[2,8]{1,0:T(2,128)S(1)} %copy-done.7, s32[2]{0:T(128)S(1)} %copy-done.8, f32[5]{0:T(128)S(1)} %copy-done.9, f32[1,1536]{1,0:T(1,128)S(1)} %copy-done.6, ...), custom_call_target="tpu_custom_call", output_to_operand_aliasing={{0}: (10, {}), {1}: (11, {})} | custom-call | tf_op jit(solution)/shard_map/tick1/pallas_call | solution.py:424
  123.1 9.2 %collective-permute-done.30.refs_12_ = bf16[48,1664]{1,0:T(8,128)(2,1)S(1)} collective-permute-done((bf16[48,1664]{1,0:T(8,128)(2,1)S(1)}, bf16[48,1664]{1,0:T(8,128)(2,1)S(1)}, u32[]{:S(2)}, u32[]{:S(2)}) %collective-permute-start.30) | collective-permute-done | bytes 159776 | tf_op jit(solution)/shard_map/ppermute | solution.py:39
  132.3 8.4 %tick2.1 = (bf16[2,256,1536]{2,1,0:T(8,128)(2,1)}, bf16[2,256,1536]{2,1,0:T(8,128)(2,1)}, bf16[48,1664]{1,0:T(8,128)(2,1)S(1)}) custom-call(s32[2,8]{1,0:T(2,128)S(1)} %copy-done.7, s32[2]{0:T(128)S(1)} %copy-done.8, f32[5]{0:T(128)S(1)} %copy-done.9, f32[1,1536]{1,0:T(1,128)S(1)} %copy-done.6, ...), custom_call_target="tpu_custom_call", output_to_operand_aliasing={{0}: (10, {}), {1}: (11, {})} | custom-call | tf_op jit(solution)/shard_map/tick2/pallas_call | solution.py:424
  140.8 8.9 %collective-permute-done.31.received = bf16[48,1664]{1,0:T(8,128)(2,1)S(1)} collective-permute-done((bf16[48,1664]{1,0:T(8,128)(2,1)S(1)}, bf16[48,1664]{1,0:T(8,128)(2,1)S(1)}, u32[]{:S(2)}, u32[]{:S(2)}) %collective-permute-start.31) | collective-permute-done | bytes 159776 | tf_op jit(solution)/shard_map/ppermute | solution.py:39
  149.7 1.4 final.1
  (61 shorter events, 6.3 us)
Async XLA Ops:
  2.4 15.2 %collective-permute-start.4 = (bf16[48,6144]{1,0:T(8,128)(2,1)S(1)}, bf16[48,6144]{1,0:T(8,128)(2,1)S(1)}, u32[]{:S(2)}, u32[]{:S(2)}) collective-permute-start(bf16[48,6144]{1,0:T(8,128)(2,1)S(1)} %get-tuple-element.47), channel_id=1, source_target_pairs={{0,8},{1,9},{2,10},{3,11},{4,12},{5,13},{6,14},{7,15},{8,0},{9,1},... | collective-permute-start | bytes 1769480 | tf_op jit(solution)/shard_map/ppermute | solution.py:33
  4.0 29.2 %collective-permute-start = (bf16[48,6144]{1,0:T(8,128)(2,1)S(1)}, bf16[48,6144]{1,0:T(8,128)(2,1)S(1)}, u32[]{:S(2)}, u32[]{:S(2)}) collective-permute-start(bf16[48,6144]{1,0:T(8,128)(2,1)S(1)} %get-tuple-element.47), channel_id=1, source_target_pairs={{0,2},{1,3},{2,4},{3,5},{4,6},{5,7},{6,0},{7,1},{8,10},{9,11},{10,... | collective-permute-start | bytes 1769480 | tf_op jit(solution)/shard_map/ppermute | solution.py:33
  4.5 31.3 %collective-permute-start.2 = (bf16[48,6144]{1,0:T(8,128)(2,1)S(1)}, bf16[48,6144]{1,0:T(8,128)(2,1)S(1)}, u32[]{:S(2)}, u32[]{:S(2)}) collective-permute-start(bf16[48,6144]{1,0:T(8,128)(2,1)S(1)} %get-tuple-element.47), channel_id=1, source_target_pairs={{0,6},{1,7},{2,0},{3,1},{4,2},{5,3},{6,4},{7,5},{8,14},{9,15},{10,... | collective-permute-start | bytes 1769480 | tf_op jit(solution)/shard_map/ppermute | solution.py:33
  6.0 26.6 %collective-permute-start.3 = (bf16[48,6144]{1,0:T(8,128)(2,1)S(1)}, bf16[48,6144]{1,0:T(8,128)(2,1)S(1)}, u32[]{:S(2)}, u32[]{:S(2)}) collective-permute-start(bf16[48,6144]{1,0:T(8,128)(2,1)S(1)} %get-tuple-element.49), channel_id=1, source_target_pairs={{0,6},{1,7},{2,0},{3,1},{4,2},{5,3},{6,4},{7,5},{8,14},{9,15},{10,... | collective-permute-start | bytes 1769480 | tf_op jit(solution)/shard_map/ppermute | solution.py:33
  6.7 29.1 %collective-permute-start.1 = (bf16[48,6144]{1,0:T(8,128)(2,1)S(1)}, bf16[48,6144]{1,0:T(8,128)(2,1)S(1)}, u32[]{:S(2)}, u32[]{:S(2)}) collective-permute-start(bf16[48,6144]{1,0:T(8,128)(2,1)S(1)} %get-tuple-element.49), channel_id=1, source_target_pairs={{0,2},{1,3},{2,4},{3,5},{4,6},{5,7},{6,0},{7,1},{8,10},{9,11},{10,... | collective-permute-start | bytes 1769480 | tf_op jit(solution)/shard_map/ppermute | solution.py:33
  17.5 18.3 %collective-permute-start.5 = (bf16[48,6144]{1,0:T(8,128)(2,1)S(1)}, bf16[48,6144]{1,0:T(8,128)(2,1)S(1)}, u32[]{:S(2)}, u32[]{:S(2)}) collective-permute-start(bf16[48,6144]{1,0:T(8,128)(2,1)S(1)} %get-tuple-element.49), channel_id=1, source_target_pairs={{0,8},{1,9},{2,10},{3,11},{4,12},{5,13},{6,14},{7,15},{8,0},{9,1},... | collective-permute-start | bytes 1769480 | tf_op jit(solution)/shard_map/ppermute | solution.py:33
  32.6 14.5 %collective-permute-start.10 = (bf16[48,6144]{1,0:T(8,128)(2,1)S(1)}, bf16[48,6144]{1,0:T(8,128)(2,1)S(1)}, u32[]{:S(2)}, u32[]{:S(2)}) collective-permute-start(bf16[48,6144]{1,0:T(8,128)(2,1)S(1)} %collective-permute-done.3.refs_4_), channel_id=1, source_target_pairs={{0,6},{1,7},{2,0},{3,1},{4,2},{5,3},{6,4},{7,5},{8,14},{9,15},{10,... | collective-permute-start | bytes 1769480 | tf_op jit(solution)/shard_map/ppermute | solution.py:33
  33.1 14.0 %collective-permute-start.9 = (bf16[48,6144]{1,0:T(8,128)(2,1)S(1)}, bf16[48,6144]{1,0:T(8,128)(2,1)S(1)}, u32[]{:S(2)}, u32[]{:S(2)}) collective-permute-start(bf16[48,6144]{1,0:T(8,128)(2,1)S(1)} %collective-permute-done.refs_1_), channel_id=1, source_target_pairs={{0,2},{1,3},{2,4},{3,5},{4,6},{5,7},{6,0},{7,1},{8,10},{9,11},{10,... | collective-permute-start | bytes 1769480 | tf_op jit(solution)/shard_map/ppermute | solution.py:33
  35.9 14.1 %collective-permute-start.6 = (bf16[96,6144]{1,0:T(8,128)(2,1)S(1)}, bf16[96,6144]{1,0:T(8,128)(2,1)S(1)}, u32[]{:S(2)}, u32[]{:S(2)}) collective-permute-start(bf16[96,6144]{1,0:T(8,128)(2,1)S(1)} %get-tuple-element.50.refs_0_), channel_id=1, source_target_pairs={{0,1},{1,0},{2,3},{3,2},{4,5},{5,4},{6,7},{7,6},{8,9},{9,8},{10,11... | collective-permute-start | bytes 3538952 | tf_op jit(solution)/shard_map/ppermute | solution.py:33
  36.0 11.7 %collective-permute-start.11 = (bf16[48,6144]{1,0:T(8,128)(2,1)S(1)}, bf16[48,6144]{1,0:T(8,128)(2,1)S(1)}, u32[]{:S(2)}, u32[]{:S(2)}) collective-permute-start(bf16[48,6144]{1,0:T(8,128)(2,1)S(1)} %collective-permute-done.3.refs_4_), channel_id=1, source_target_pairs={{0,1},{1,0},{2,3},{3,2},{4,5},{5,4},{6,7},{7,6},{8,9},{9,8},{10,11... | collective-permute-start | bytes 1769480 | tf_op jit(solution)/shard_map/ppermute | solution.py:33
  36.5 11.2 %collective-permute-start.12 = (bf16[48,6144]{1,0:T(8,128)(2,1)S(1)}, bf16[48,6144]{1,0:T(8,128)(2,1)S(1)}, u32[]{:S(2)}, u32[]{:S(2)}) collective-permute-start(bf16[48,6144]{1,0:T(8,128)(2,1)S(1)} %collective-permute-done.4.refs_5_), channel_id=1, source_target_pairs={{0,1},{1,0},{2,3},{3,2},{4,5},{5,4},{6,7},{7,6},{8,9},{9,8},{10,11... | collective-permute-start | bytes 1769480 | tf_op jit(solution)/shard_map/ppermute | solution.py:33
  47.1 2.0 %collective-permute-start.7 = (bf16[48,6144]{1,0:T(8,128)(2,1)S(1)}, bf16[48,6144]{1,0:T(8,128)(2,1)S(1)}, u32[]{:S(2)}, u32[]{:S(2)}) collective-permute-start(bf16[48,6144]{1,0:T(8,128)(2,1)S(1)} %collective-permute-done.refs_1_), channel_id=1, source_target_pairs={{0,1},{1,0},{2,3},{3,2},{4,5},{5,4},{6,7},{7,6},{8,9},{9,8},{10,11... | collective-permute-start | bytes 1769480 | tf_op jit(solution)/shard_map/ppermute | solution.py:33
  47.1 2.8 %collective-permute-start.8 = (bf16[48,6144]{1,0:T(8,128)(2,1)S(1)}, bf16[48,6144]{1,0:T(8,128)(2,1)S(1)}, u32[]{:S(2)}, u32[]{:S(2)}) collective-permute-start(bf16[48,6144]{1,0:T(8,128)(2,1)S(1)} %collective-permute-done.1.refs_2_), channel_id=1, source_target_pairs={{0,1},{1,0},{2,3},{3,2},{4,5},{5,4},{6,7},{7,6},{8,9},{9,8},{10,11... | collective-permute-start | bytes 1769480 | tf_op jit(solution)/shard_map/ppermute | solution.py:33
  50.0 2.6 %collective-permute-start.13 = (bf16[48,6144]{1,0:T(8,128)(2,1)S(1)}, bf16[48,6144]{1,0:T(8,128)(2,1)S(1)}, u32[]{:S(2)}, u32[]{:S(2)}) collective-permute-start(bf16[48,6144]{1,0:T(8,128)(2,1)S(1)} %collective-permute-done.2.refs_3_), channel_id=1, source_target_pairs={{0,1},{1,0},{2,3},{3,2},{4,5},{5,4},{6,7},{7,6},{8,9},{9,8},{10,11... | collective-permute-start | bytes 1769480 | tf_op jit(solution)/shard_map/ppermute | solution.py:33
  50.1 2.7 %collective-permute-start.14 = (bf16[48,6144]{1,0:T(8,128)(2,1)S(1)}, bf16[48,6144]{1,0:T(8,128)(2,1)S(1)}, u32[]{:S(2)}, u32[]{:S(2)}) collective-permute-start(bf16[48,6144]{1,0:T(8,128)(2,1)S(1)} %collective-permute-done.5.refs_6_), channel_id=1, source_target_pairs={{0,1},{1,0},{2,3},{3,2},{4,5},{5,4},{6,7},{7,6},{8,9},{9,8},{10,11... | collective-permute-start | bytes 1769480 | tf_op jit(solution)/shard_map/ppermute | solution.py:33
  50.5 15.4 %collective-permute-start.15 = (bf16[48,6144]{1,0:T(8,128)(2,1)S(1)}, bf16[48,6144]{1,0:T(8,128)(2,1)S(1)}, u32[]{:S(2)}, u32[]{:S(2)}) collective-permute-start(bf16[48,6144]{1,0:T(8,128)(2,1)S(1)} %collective-permute-done.4.refs_5_), channel_id=1, source_target_pairs={{0,2},{1,3},{2,4},{3,5},{4,6},{5,7},{6,0},{7,1},{8,10},{9,11},{10,... | collective-permute-start | bytes 1769480 | tf_op jit(solution)/shard_map/ppermute | solution.py:33
  52.6 16.3 %collective-permute-start.16 = (bf16[48,6144]{1,0:T(8,128)(2,1)S(1)}, bf16[48,6144]{1,0:T(8,128)(2,1)S(1)}, u32[]{:S(2)}, u32[]{:S(2)}) collective-permute-start(bf16[48,6144]{1,0:T(8,128)(2,1)S(1)} %collective-permute-done.4.refs_5_), channel_id=1, source_target_pairs={{0,6},{1,7},{2,0},{3,1},{4,2},{5,3},{6,4},{7,5},{8,14},{9,15},{10,... | collective-permute-start | bytes 1769480 | tf_op jit(solution)/shard_map/ppermute | solution.py:33
  52.6 16.3 %collective-permute-start.17 = (bf16[48,6144]{1,0:T(8,128)(2,1)S(1)}, bf16[48,6144]{1,0:T(8,128)(2,1)S(1)}, u32[]{:S(2)}, u32[]{:S(2)}) collective-permute-start(bf16[48,6144]{1,0:T(8,128)(2,1)S(1)} %collective-permute-done.9.refs_1_), channel_id=1, source_target_pairs={{0,8},{1,9},{2,10},{3,11},{4,12},{5,13},{6,14},{7,15},{8,0},{9,1},... | collective-permute-start | bytes 1769480 | tf_op jit(solution)/shard_map/ppermute | solution.py:33
  68.9 2.0 %collective-permute-start.18 = (bf16[48,6144]{1,0:T(8,128)(2,1)S(1)}, bf16[48,6144]{1,0:T(8,128)(2,1)S(1)}, u32[]{:S(2)}, u32[]{:S(2)}) collective-permute-start(bf16[48,6144]{1,0:T(8,128)(2,1)S(1)} %collective-permute-done.9.refs_1_), channel_id=1, source_target_pairs={{0,1},{1,0},{2,3},{3,2},{4,5},{5,4},{6,7},{7,6},{8,9},{9,8},{10,11... | collective-permute-start | bytes 1769480 | tf_op jit(solution)/shard_map/ppermute | solution.py:33
  68.9 3.7 %collective-permute-start.19 = (bf16[48,6144]{1,0:T(8,128)(2,1)S(1)}, bf16[48,6144]{1,0:T(8,128)(2,1)S(1)}, u32[]{:S(2)}, u32[]{:S(2)}) collective-permute-start(bf16[48,6144]{1,0:T(8,128)(2,1)S(1)} %collective-permute-done.10.refs_2_), channel_id=1, source_target_pairs={{0,1},{1,0},{2,3},{3,2},{4,5},{5,4},{6,7},{7,6},{8,9},{9,8},{10,11... | collective-permute-start | bytes 1769480 | tf_op jit(solution)/shard_map/ppermute | solution.py:33
  69.4 3.5 %collective-permute-start.20 = (bf16[48,6144]{1,0:T(8,128)(2,1)S(1)}, bf16[48,6144]{1,0:T(8,128)(2,1)S(1)}, u32[]{:S(2)}, u32[]{:S(2)}) collective-permute-start(bf16[48,6144]{1,0:T(8,128)(2,1)S(1)} %collective-permute-done.15.refs_3_), channel_id=1, source_target_pairs={{0,1},{1,0},{2,3},{3,2},{4,5},{5,4},{6,7},{7,6},{8,9},{9,8},{10,11... | collective-permute-start | bytes 1769480 | tf_op jit(solution)/shard_map/ppermute | solution.py:33
  69.4 4.0 %collective-permute-start.21 = (bf16[48,6144]{1,0:T(8,128)(2,1)S(1)}, bf16[48,6144]{1,0:T(8,128)(2,1)S(1)}, u32[]{:S(2)}, u32[]{:S(2)}) collective-permute-start(bf16[48,6144]{1,0:T(8,128)(2,1)S(1)} %collective-permute-done.16.refs_4_), channel_id=1, source_target_pairs={{0,1},{1,0},{2,3},{3,2},{4,5},{5,4},{6,7},{7,6},{8,9},{9,8},{10,11... | collective-permute-start | bytes 1769480 | tf_op jit(solution)/shard_map/ppermute | solution.py:33
  69.9 4.4 %collective-permute-start.22 = (bf16[48,6144]{1,0:T(8,128)(2,1)S(1)}, bf16[48,6144]{1,0:T(8,128)(2,1)S(1)}, u32[]{:S(2)}, u32[]{:S(2)}) collective-permute-start(bf16[48,6144]{1,0:T(8,128)(2,1)S(1)} %collective-permute-done.17.refs_5_), channel_id=1, source_target_pairs={{0,1},{1,0},{2,3},{3,2},{4,5},{5,4},{6,7},{7,6},{8,9},{9,8},{10,11... | collective-permute-start | bytes 1769480 | tf_op jit(solution)/shard_map/ppermute | solution.py:33
  70.9 15.4 %collective-permute-start.23 = (bf16[48,6144]{1,0:T(8,128)(2,1)S(1)}, bf16[48,6144]{1,0:T(8,128)(2,1)S(1)}, u32[]{:S(2)}, u32[]{:S(2)}) collective-permute-start(bf16[48,6144]{1,0:T(8,128)(2,1)S(1)} %collective-permute-done.5.refs_6_), channel_id=1, source_target_pairs={{0,2},{1,3},{2,4},{3,5},{4,6},{5,7},{6,0},{7,1},{8,10},{9,11},{10,... | collective-permute-start | bytes 1769480 | tf_op jit(solution)/shard_map/ppermute | solution.py:33
  72.7 16.3 %collective-permute-start.24 = (bf16[48,6144]{1,0:T(8,128)(2,1)S(1)}, bf16[48,6144]{1,0:T(8,128)(2,1)S(1)}, u32[]{:S(2)}, u32[]{:S(2)}) collective-permute-start(bf16[48,6144]{1,0:T(8,128)(2,1)S(1)} %collective-permute-done.5.refs_6_), channel_id=1, source_target_pairs={{0,6},{1,7},{2,0},{3,1},{4,2},{5,3},{6,4},{7,5},{8,14},{9,15},{10,... | collective-permute-start | bytes 1769480 | tf_op jit(solution)/shard_map/ppermute | solution.py:33
  72.9 16.0 %collective-permute-start.25 = (bf16[48,6144]{1,0:T(8,128)(2,1)S(1)}, bf16[48,6144]{1,0:T(8,128)(2,1)S(1)}, u32[]{:S(2)}, u32[]{:S(2)}) collective-permute-start(bf16[48,6144]{1,0:T(8,128)(2,1)S(1)} %collective-permute-done.10.refs_2_), channel_id=1, source_target_pairs={{0,8},{1,9},{2,10},{3,11},{4,12},{5,13},{6,14},{7,15},{8,0},{9,1},... | collective-permute-start | bytes 1769480 | tf_op jit(solution)/shard_map/ppermute | solution.py:33
  89.0 2.0 %collective-permute-start.26 = (bf16[48,6144]{1,0:T(8,128)(2,1)S(1)}, bf16[48,6144]{1,0:T(8,128)(2,1)S(1)}, u32[]{:S(2)}, u32[]{:S(2)}) collective-permute-start(bf16[48,6144]{1,0:T(8,128)(2,1)S(1)} %collective-permute-done.23.refs_15_), channel_id=1, source_target_pairs={{0,1},{1,0},{2,3},{3,2},{4,5},{5,4},{6,7},{7,6},{8,9},{9,8},{10,11... | collective-permute-start | bytes 1769480 | tf_op jit(solution)/shard_map/ppermute | solution.py:33
  89.0 2.8 %collective-permute-start.27 = (bf16[48,6144]{1,0:T(8,128)(2,1)S(1)}, bf16[48,6144]{1,0:T(8,128)(2,1)S(1)}, u32[]{:S(2)}, u32[]{:S(2)}) collective-permute-start(bf16[48,6144]{1,0:T(8,128)(2,1)S(1)} %collective-permute-done.24.refs_16_), channel_id=1, source_target_pairs={{0,1},{1,0},{2,3},{3,2},{4,5},{5,4},{6,7},{7,6},{8,9},{9,8},{10,11... | collective-permute-start | bytes 1769480 | tf_op jit(solution)/shard_map/ppermute | solution.py:33
  89.5 3.2 %collective-permute-start.28 = (bf16[48,6144]{1,0:T(8,128)(2,1)S(1)}, bf16[48,6144]{1,0:T(8,128)(2,1)S(1)}, u32[]{:S(2)}, u32[]{:S(2)}) collective-permute-start(bf16[48,6144]{1,0:T(8,128)(2,1)S(1)} %collective-permute-done.25.refs_17_), channel_id=1, source_target_pairs={{0,1},{1,0},{2,3},{3,2},{4,5},{5,4},{6,7},{7,6},{8,9},{9,8},{10,11... | collective-permute-start | bytes 1769480 | tf_op jit(solution)/shard_map/ppermute | solution.py:33
  101.3 13.1 %collective-permute-start.29 = (bf16[48,1664]{1,0:T(8,128)(2,1)S(1)}, bf16[48,1664]{1,0:T(8,128)(2,1)S(1)}, u32[]{:S(2)}, u32[]{:S(2)}) collective-permute-start(bf16[48,1664]{1,0:T(8,128)(2,1)S(1)} %get-tuple-element.78), channel_id=1, source_target_pairs={{0,16},{16,32},{32,48},{48,64},{64,80},{80,96},{96,112},{112,128},... | collective-permute-start | bytes 479240 | tf_op jit(solution)/shard_map/ppermute | solution.py:39
  123.0 9.3 %collective-permute-start.30 = (bf16[48,1664]{1,0:T(8,128)(2,1)S(1)}, bf16[48,1664]{1,0:T(8,128)(2,1)S(1)}, u32[]{:S(2)}, u32[]{:S(2)}) collective-permute-start(bf16[48,1664]{1,0:T(8,128)(2,1)S(1)} %get-tuple-element.82), channel_id=1, source_target_pairs={{0,16},{16,32},{32,48},{48,64},{64,80},{80,96},{96,112},{112,128},... | collective-permute-start | bytes 479240 | tf_op jit(solution)/shard_map/ppermute | solution.py:39
  140.7 9.0 %collective-permute-start.31 = (bf16[48,1664]{1,0:T(8,128)(2,1)S(1)}, bf16[48,1664]{1,0:T(8,128)(2,1)S(1)}, u32[]{:S(2)}, u32[]{:S(2)}) collective-permute-start(bf16[48,1664]{1,0:T(8,128)(2,1)S(1)} %get-tuple-element.83), channel_id=1, source_target_pairs={{0,16},{16,32},{32,48},{48,64},{64,80},{80,96},{96,112},{112,128},... | collective-permute-start | bytes 479240 | tf_op jit(solution)/shard_map/ppermute | solution.py:39
  (11 other events, 202.1 us)

commit v3 on v2

--- a/solution.py
+++ b/solution.py
@@ -43,17 +43,26 @@
     return lax.optimization_barrier(values)
 
 
+LOW, HIGH = 0, 1
 NEAR = [
-    (0, 0, 0, 16),
-    (0, -1, 0, 8),
-    (0, -1, 8, 8),
-    (0, 1, 0, 8),
-    (0, 1, 8, 8),
-    (1, 0, 0, 8),
-    (1, 0, 8, 8),
+    [(0, 0, 0, LOW)],
+    [(0, 0, 0, HIGH)],
+    [(0, -1, 0, LOW)],
+    [(0, 1, 0, HIGH)],
+    [(1, 0, 0, LOW)],
+    [(1, 0, 0, HIGH)],
+    [(0, 2, 0, LOW)],
+    [(0, 2, 0, HIGH)],
 ]
-MIDDLE = [(0, 2, 0, 8), (0, 2, 8, 8), (1, -1, 0, 8), (1, 1, 0, 8), (1, 2, 0, 8)]
-LAST = [(1, -1, 8, 8), (1, 1, 8, 8), (1, 2, 8, 8)]
+FAR = [[(1, 2, 0, LOW), (1, 2, 0, HIGH)]]
+LAST = [
+    [(0, -1, 0, HIGH), (1, -1, 0, LOW), (1, -1, 0, HIGH)],
+    [(0, 1, 0, LOW), (1, 1, 0, LOW), (1, 1, 0, HIGH)],
+]
+
+
+def paired(pieces):
+    return [[(dx, dy, 1, half) for dx, dy, _, half in piece] for piece in pieces]
 
 
 def in_hbm(array):
@@ -64,20 +73,13 @@
     return moved(piece, 0, 0, 1)
 
 
-def places(rows, group):
+def place(rows, block):
+    dx, dy, dc, half = block
     device = lax.axis_index("dp")
-    core = lax.rem(device, C)
-    y = lax.rem(device // C, Y)
-    x = device // (C * Y)
-    found = []
-    for dx, dy, dc, part, count in group:
-        source = (lax.rem(x + dx, X) * Y + lax.rem(y + dy + Y, Y)) * C + lax.rem(core + dc, C)
-        found.append((pl.multiple_of(source * rows + part * rows // 16, TILE), count * rows // 16))
-    return found
-
-
-def both(group):
-    return [(dx, dy, dc, part, count) for dc in range(C) for dx, dy, part, count in group]
+    core = lax.rem(device % C + dc, C)
+    y = lax.rem((device // C) % Y + dy + Y, Y)
+    x = lax.rem(device // (C * Y) + dx, X)
+    return pl.multiple_of(((x * Y + y) * C + core) * rows + half * (rows // 2), TILE)
 
 
 def normalize(widened):
@@ -123,11 +125,19 @@
         attended[:, cols] = (mixed / total).astype(jnp.bfloat16)
 
 
-def weight_copies(pieces, weights, rows, group, sems):
-    return [
-        pltpu.make_async_copy(piece, weights.at[pl.ds(start, count), :], sems.at[at])
-        for at, (piece, (start, count)) in enumerate(zip(pieces, places(rows, group)))
-    ]
+def weight_copies(pieces, weights, rows, blocks, sems):
+    size = rows // 2
+    found = []
+    for piece, held in zip(pieces, blocks):
+        for at, block in enumerate(held):
+            found.append(
+                pltpu.make_async_copy(
+                    piece.at[pl.ds(at * size, size), :],
+                    weights.at[pl.ds(place(rows, block), size), :],
+                    sems.at[len(found)],
+                )
+            )
+    return found
 
 
 def run_copies(copies):
@@ -137,11 +147,11 @@
         copy.wait()
 
 
-def own_kernel(qkv, out, low, high, whole, sems):
+def own_kernel(qkv, out, low, high, sems):
     half, width = low.shape[0], qkv.shape[1]
     copies = []
-    for at, (target, start) in enumerate(((low, 0), (high, half), (whole, 0))):
-        rows = pl.ds(start, target.shape[0])
+    for at, target in enumerate((low, high)):
+        rows = pl.ds(at * half, half)
         copies += [
             pltpu.make_async_copy(qkv.at[rows, :], target.at[:, pl.ds(0, width)], sems.at[2 * at]),
             pltpu.make_async_copy(
@@ -151,12 +161,27 @@
     run_copies(copies)
 
 
-def load_kernel(rows, group, copied, first, *refs):
+def stack_kernel(stacks, count, *refs):
+    pieces, targets, sems = refs[:count], refs[count:-1], refs[-1]
+    size = pieces[0].shape[0]
+    copies = []
+    for target, held in zip(targets, stacks):
+        for at, piece in enumerate(held):
+            copies.append(
+                pltpu.make_async_copy(
+                    pieces[piece], target.at[pl.ds(at * size, size), :], sems.at[len(copies)]
+                )
+            )
+    run_copies(copies)
+
+
+def load_kernel(rows, first, blocks, count, copied, *refs):
     if not first:
         refs = refs[1:]
-    count = len(group)
     pieces, sources, refs = refs[:count], refs[count : count + copied], refs[count + copied :]
-    weights, targets, (sems, copy_sems, *stages) = refs[0], refs[1 : 1 + copied], refs[1 + copied :]
+    weights, targets, refs = refs[0], refs[1 : 1 + copied], refs[1 + copied :]
+    sems, copy_sems, stages = refs[0], refs[1], refs[2:]
+    copies = weight_copies(pieces, weights, rows, blocks, sems)
     inward = [
         pltpu.make_async_copy(source, stage, copy_sems.at[at, 0])
         for at, (source, stage) in enumerate(zip(sources, stages))
@@ -165,7 +190,6 @@
         pltpu.make_async_copy(stage, target, copy_sems.at[at, 1])
         for at, (stage, target) in enumerate(zip(stages, targets))
     ]
-    copies = weight_copies(pieces, weights, rows, group, sems)
     for copy in inward + copies:
         copy.start()
     for copy, onward in zip(inward, outward):
@@ -201,7 +225,7 @@
     ]
     weight_loads = []
     if first:
-        weight_loads = weight_copies(pieces, weights, rows, both(LAST), weight_sem[0])
+        weight_loads = weight_copies(pieces, weights, rows, LAST + paired(LAST), weight_sem[0])
     for load in weight_loads + loads:
         load.start()
 
@@ -337,30 +361,44 @@
 
     full = part * lax.axis_size("dp")
     total = w_qkv.shape[2] + w_out.shape[2]
-    halves = [jax.ShapeDtypeStruct((part // 2, total), jnp.bfloat16)] * 2
-    low, high, whole = pl.pallas_call(
+    half = jax.ShapeDtypeStruct((part // 2, total), jnp.bfloat16)
+    low, high = pl.pallas_call(
         own_kernel,
-        out_shape=halves + [jax.ShapeDtypeStruct((part, total), jnp.bfloat16)],
+        out_shape=[half] * 2,
         in_specs=[hbm] * 2,
-        out_specs=[hbm] * 3,
-        scratch_shapes=[pltpu.SemaphoreType.DMA((6,))],
+        out_specs=[hbm] * 2,
+        scratch_shapes=[pltpu.SemaphoreType.DMA((4,))],
         compiler_params=small_params,
         name="own",
     )(in_hbm(w_qkv[0]), in_hbm(w_out[0]))
 
-    def loaded(weights, pieces, group, copied, name):
+    def stacked(pieces, stacks):
+        return pl.pallas_call(
+            functools.partial(stack_kernel, stacks, len(pieces)),
+            out_shape=[
+                jax.ShapeDtypeStruct((len(held) * (part // 2), total), jnp.bfloat16) for held in stacks
+            ],
+            in_specs=[hbm] * len(pieces),
+            out_specs=[hbm] * len(stacks),
+            scratch_shapes=[pltpu.SemaphoreType.DMA((sum(len(held) for held in stacks),))],
+            compiler_params=small_params,
+            name="stack",
+        )(*pieces)
+
+    def loaded(name, weights, pieces, blocks, copied):
         first = weights is None
         if not first:
             weights = pltpu.with_memory_space_constraint(weights, pltpu.VMEM)
+        shapes = [pltpu.VMEM((full, total), jnp.bfloat16)]
+        shapes += [jax.ShapeDtypeStruct(array.shape, array.dtype) for array in copied]
         return pl.pallas_call(
-            functools.partial(load_kernel, part, group, len(copied), first),
-            out_shape=[pltpu.VMEM((full, total), jnp.bfloat16)]
-            + [jax.ShapeDtypeStruct(array.shape, array.dtype) for array in copied],
+            functools.partial(load_kernel, part, first, blocks, len(pieces), len(copied)),
+            out_shape=shapes,
             in_specs=[vmem] * (not first) + [hbm] * (len(pieces) + len(copied)),
-            out_specs=[vmem] + [hbm] * len(copied),
+            out_specs=[vmem] + [hbm] * (len(shapes) - 1),
             scratch_shapes=[
-                pltpu.SemaphoreType.DMA((len(pieces),)),
-                pltpu.SemaphoreType.DMA((max(len(copied), 1), 2)),
+                pltpu.SemaphoreType.DMA((sum(len(held) for held in blocks),)),
+                pltpu.SemaphoreType.DMA((len(copied), 2)),
                 *[pltpu.VMEM(array.shape, array.dtype) for array in copied],
             ],
             input_output_aliases={} if first else {0: 0},
@@ -368,26 +406,25 @@
             name=name,
         )(*([] if first else [weights]), *pieces, *[in_hbm(array) for array in copied])
 
-    below_low, above_high, across_low = moved(low, 0, 1, 0), moved(high, 0, -1, 0), moved(low, 1, 0, 0)
-    below_high, above_low = moved(high, 0, 1, 0), moved(low, 0, -1, 0)
+    below_low, above_high = moved(low, 0, 1, 0), moved(high, 0, -1, 0)
+    across_low, across_high = moved(low, 1, 0, 0), moved(high, 1, 0, 0)
     far_low, far_high = moved(below_low, 0, 1, 0), moved(above_high, 0, -1, 0)
-    across_high = moved(joined(high, across_low)[0], 1, 0, 0)
-    ready = joined(whole, below_low, above_high, across_low, below_high, below_high, above_low, across_high)
-    whole_pair, below_low_pair, above_high_pair, across_low_pair, below_high_pair = [pair(piece) for piece in ready[:5]]
-    far_low, far_high, onward_low, onward_high, *ready = joined(
-        far_low, far_high, across_low, across_high, above_low, across_high, whole_pair, below_low_pair, above_high_pair, across_low_pair, below_high_pair
+    near = [low, high, below_low, above_high, across_low, across_high, far_low, far_high]
+    near_pair, up, down, far = stacked(near, [list(range(8)), [1, 4, 5], [0, 4, 5], [6, 7]])
+    near_pair = pair(near_pair)
+    up, down, far = moved(up, 0, 1, 0), moved(down, 0, -1, 0), moved(far, 1, 0, 0)
+    weights, keys, values = loaded(
+        "near",
+        None,
+        [*near, near_pair],
+        NEAR + [[block for piece in paired(NEAR) for block in piece]],
+        [keys, values],
     )
-    above_low_pair, across_high_pair = [pair(piece) for piece in ready[:2]]
-    xu_low, xd_low, xf_low = moved(onward_low, 0, 1, 0), moved(onward_low, 0, -1, 0), moved(far_low, 1, 0, 0)
-    xu_high, xd_high, xf_high = moved(onward_high, 0, 1, 0), moved(onward_high, 0, -1, 0), moved(far_high, 1, 0, 0)
-    near = [whole, below_low, below_high, above_low, above_high, across_low, across_high]
-    near += [whole_pair, below_low_pair, below_high_pair, above_low_pair, above_high_pair, across_low_pair, across_high_pair]
-    weights, keys, values = loaded(None, near, both(NEAR), [keys, values], "near")
-    low_set = [far_low, far_high, xu_low, xd_low, xf_low]
-    keys, *low_set = joined(keys, *low_set)
-    middle = low_set + [pair(piece) for piece in low_set]
-    weights, latents = loaded(weights, middle, both(MIDDLE), [latents], "middle")
-    latents, *last = joined(latents, xu_high, xd_high, xf_high)
+    keys, far = joined(keys, far)
+    far_pair = pair(far)
+    up, down, far_pair = joined(up, down, far_pair)
+    weights, latents = loaded("far", weights, [far, far_pair], FAR + paired(FAR), [latents])
+    last = [up, down]
     last += [pair(piece) for piece in last]
 
     for tick in range(TICKS):
@@ -420,7 +457,7 @@
             pltpu.SemaphoreType.DMA((2,)),
         ]
         if first:
-            scratch.append(pltpu.SemaphoreType.DMA((len(last),)))
+            scratch.append(pltpu.SemaphoreType.DMA((2 * sum(len(held) for held in LAST),)))
         results = pl.pallas_call(
             functools.partial(tick_kernel, tick, sections, first, part),
             out_shape=shapes,

time: 151 us -> 145 us (0.960)
  starting transfers between devices: 21.6 us -> 13.8 us
  Pallas kernels: 34.2 us -> 36 us
    ppermute x29 -> x13, starting transfers between devices: 19.1 us -> 11.7 us  [moved(): return lax.ppermute(value, 'dp', pairs)]
    pallas_call x3 -> x4, Pallas kernels: 7.22 us -> 8.32 us  [the longest x2 4.95 us: loaded(): pl.pallas_call(functools.partial(load_kernel, part, first, blocks, len(pi...]
    ppermute x29 -> x13, waiting for transfers between devices: 65.6 us -> 64.9 us  [moved(): return lax.ppermute(value, 'dp', pairs)]
  transfers between devices with their start and end apart: 32 -> 16, of which waited for: 19 -> 14; matrix products, arithmetic and copies ran while one was open for 0% -> 0% of each run, Pallas kernels for 4% -> 3%
where the time goes in v3:
time: 145 us
  waiting for transfers between devices  93.8 us (65%)
  Pallas kernels  36 us (25%)
  starting transfers between devices  13.8 us (10%)
    ppermute x13, waiting for transfers between devices, moved(): return lax.ppermute(value, 'dp', pairs)  64.9 us
    ppermute x3, waiting for transfers between devices, shifted(): return lax.ppermute(value, 'phase', pairs)  28.9 us
    pallas_call x3, Pallas kernels, shards(): pl.pallas_call(functools.partial(tick_kernel, tick, sections, first, part...  26.3 us
    ppermute x13, starting transfers between devices, moved(): return lax.ppermute(value, 'dp', pairs)  11.7 us
    pallas_call x2, Pallas kernels, loaded(): pl.pallas_call(functools.partial(load_kernel, part, first, blocks, len(pi...  4.95 us
  transfers between devices with their start and end apart: 16, of which 14 were waited for; matrix products, arithmetic and copies ran while one was open for 0% of the time, Pallas kernels for 3%

profile of v3, /device:TPU:24, one launch (start us, length us, event | category | flops | bytes accessed | tf_op | source)
XLA Modules:
  0.0 144.5 jit_solution(14293561689270148160)
XLA Ops:
  0.6 1.3 own.1
  1.9 2.0 %collective-permute-start = (bf16[48,6144]{1,0:T(8,128)(2,1)S(1)}, bf16[48,6144]{1,0:T(8,128)(2,1)S(1)}, u32[]{:S(2)}, u32[]{:S(2)}) collective-permute-start(bf16[48,6144]{1,0:T(8,128)(2,1)S(1)} %get-tuple-element.32.refs_0_), channel_id=1, source_target_pairs={{0,2},{1,3},{2,4},{3,5},{4,6},{5,7},{6,0},{7,1},{8,10},{9,11},{10,... | collective-permute-start | bytes 1769480 | tf_op jit(solution)/shard_map/ppermute | solution.py:33
  4.0 1.5 %collective-permute-start.2 = (bf16[48,6144]{1,0:T(8,128)(2,1)S(1)}, bf16[48,6144]{1,0:T(8,128)(2,1)S(1)}, u32[]{:S(2)}, u32[]{:S(2)}) collective-permute-start(bf16[48,6144]{1,0:T(8,128)(2,1)S(1)} %get-tuple-element.32.refs_0_), channel_id=1, source_target_pairs={{0,8},{1,9},{2,10},{3,11},{4,12},{5,13},{6,14},{7,15},{8,0},{9,1},... | collective-permute-start | bytes 1769480 | tf_op jit(solution)/shard_map/ppermute | solution.py:33
  5.5 0.5 collective-permute-start.3
  6.1 11.0 %collective-permute-done.refs_2_ = bf16[48,6144]{1,0:T(8,128)(2,1)S(1)} collective-permute-done((bf16[48,6144]{1,0:T(8,128)(2,1)S(1)}, bf16[48,6144]{1,0:T(8,128)(2,1)S(1)}, u32[]{:S(2)}, u32[]{:S(2)}) %collective-permute-start) | collective-permute-done | bytes 589856 | tf_op jit(solution)/shard_map/ppermute | solution.py:33
  17.1 1.5 %collective-permute-start.4 = (bf16[48,6144]{1,0:T(8,128)(2,1)S(1)}, bf16[48,6144]{1,0:T(8,128)(2,1)S(1)}, u32[]{:S(2)}, u32[]{:S(2)}) collective-permute-start(bf16[48,6144]{1,0:T(8,128)(2,1)S(1)} %collective-permute-done.refs_2_), channel_id=1, source_target_pairs={{0,2},{1,3},{2,4},{3,5},{4,6},{5,7},{6,0},{7,1},{8,10},{9,11},{10,... | collective-permute-start | bytes 1769480 | tf_op jit(solution)/shard_map/ppermute | solution.py:33
  18.6 0.5 collective-permute-start.5
  19.1 1.2 collective-permute-done.2.refs_4_
  20.3 10.9 %collective-permute-done.3.refs_5_ = bf16[48,6144]{1,0:T(8,128)(2,1)S(1)} collective-permute-done((bf16[48,6144]{1,0:T(8,128)(2,1)S(1)}, bf16[48,6144]{1,0:T(8,128)(2,1)S(1)}, u32[]{:S(2)}, u32[]{:S(2)}) %collective-permute-start.3) | collective-permute-done | bytes 589856 | tf_op jit(solution)/shard_map/ppermute | solution.py:33
  31.3 1.2 collective-permute-done.5.refs_7_
  32.5 2.1 %stack.1 = (bf16[384,6144]{1,0:T(8,128)(2,1)S(1)}, bf16[144,6144]{1,0:T(8,128)(2,1)S(1)}, bf16[144,6144]{1,0:T(8,128)(2,1)S(1)}, bf16[96,6144]{1,0:T(8,128)(2,1)S(1)}) custom-call(bf16[48,6144]{1,0:T(8,128)(2,1)S(1)} %get-tuple-element.32.refs_0_, bf16[48,6144]{1,0:T(8,128)(2,1)S(1)} %get-tuple-element.33.refs_1_, ...), custom_call_target="tpu_custom_call" | custom-call | tf_op jit(solution)/shard_map/stack/pallas_call | solution.py:376
  34.6 0.1 collective-permute-start.6
  34.7 2.9 %collective-permute-start.7 = (bf16[96,6144]{1,0:T(8,128)(2,1)S(1)}, bf16[96,6144]{1,0:T(8,128)(2,1)S(1)}, u32[]{:S(2)}, u32[]{:S(2)}) collective-permute-start(bf16[96,6144]{1,0:T(8,128)(2,1)S(1)} %get-tuple-element.36), channel_id=1, source_target_pairs={{0,8},{1,9},{2,10},{3,11},{4,12},{5,13},{6,14},{7,15},{8,0},{9,1},... | collective-permute-start | bytes 3538952 | tf_op jit(solution)/shard_map/ppermute | solution.py:33
  37.5 0.3 collective-permute-start.8
  37.8 1.7 %collective-permute-start.9 = (bf16[144,6144]{1,0:T(8,128)(2,1)S(1)}, bf16[144,6144]{1,0:T(8,128)(2,1)S(1)}, u32[]{:S(2)}, u32[]{:S(2)}) collective-permute-start(bf16[144,6144]{1,0:T(8,128)(2,1)S(1)} %get-tuple-element.42), channel_id=1, source_target_pairs={{0,6},{1,7},{2,0},{3,1},{4,2},{5,3},{6,4},{7,5},{8,14},{9,15},{10,... | collective-permute-start | bytes 5308424 | tf_op jit(solution)/shard_map/ppermute | solution.py:33
  39.6 3.0 %collective-permute-done.6.refs_8_ = bf16[384,6144]{1,0:T(8,128)(2,1)S(1)} collective-permute-done((bf16[384,6144]{1,0:T(8,128)(2,1)S(1)}, bf16[384,6144]{1,0:T(8,128)(2,1)S(1)}, u32[]{:S(2)}, u32[]{:S(2)}) %collective-permute-start.6) | collective-permute-done | bytes 4718624 | tf_op jit(solution)/shard_map/ppermute | solution.py:33
  42.6 4.0 %near.1 = (bf16[1536,6144]{1,0:T(8,128)(2,1)S(1)}, bf16[2,256,1536]{2,1,0:T(8,128)(2,1)}, bf16[2,256,1536]{2,1,0:T(8,128)(2,1)}) custom-call(bf16[48,6144]{1,0:T(8,128)(2,1)S(1)} %get-tuple-element.32.refs_0_, bf16[48,6144]{1,0:T(8,128)(2,1)S(1)} %get-tuple-element.33.refs_1_, bf16[48,6144]{1,0:T(8,128)(2,1)S(1)} %collective-permute-done.refs_2_, ...), custom_call_target="tpu_custom_call" | custom-call | tf_op jit(solution)/shard_map/near/pallas_call | solution.py:394
  46.6 17.5 %collective-permute-done.7.refs_1_ = bf16[96,6144]{1,0:T(8,128)(2,1)S(1)} collective-permute-done((bf16[96,6144]{1,0:T(8,128)(2,1)S(1)}, bf16[96,6144]{1,0:T(8,128)(2,1)S(1)}, u32[]{:S(2)}, u32[]{:S(2)}) %collective-permute-start.7) | collective-permute-done | bytes 1179680 | tf_op jit(solution)/shard_map/ppermute | solution.py:33
  64.1 14.1 %collective-permute-done.8.refs_15_ = bf16[144,6144]{1,0:T(8,128)(2,1)S(1)} collective-permute-done((bf16[144,6144]{1,0:T(8,128)(2,1)S(1)}, bf16[144,6144]{1,0:T(8,128)(2,1)S(1)}, u32[]{:S(2)}, u32[]{:S(2)}) %collective-permute-start.8) | collective-permute-done | bytes 1769504 | tf_op jit(solution)/shard_map/ppermute | solution.py:33
  78.2 1.2 collective-permute-done.9.refs_16_
  79.4 0.5 collective-permute-start.12
  80.0 0.9 far.1
  81.0 2.2 %collective-permute-done.11.refs_17_ = bf16[144,6144]{1,0:T(8,128)(2,1)S(1)} collective-permute-done((bf16[144,6144]{1,0:T(8,128)(2,1)S(1)}, bf16[144,6144]{1,0:T(8,128)(2,1)S(1)}, u32[]{:S(2)}, u32[]{:S(2)}) %collective-permute-start.11) | collective-permute-done | bytes 1769504 | tf_op jit(solution)/shard_map/ppermute | solution.py:33
  83.1 2.5 %collective-permute-done.12.refs_18_ = bf16[144,6144]{1,0:T(8,128)(2,1)S(1)} collective-permute-done((bf16[144,6144]{1,0:T(8,128)(2,1)S(1)}, bf16[144,6144]{1,0:T(8,128)(2,1)S(1)}, u32[]{:S(2)}, u32[]{:S(2)}) %collective-permute-start.12) | collective-permute-done | bytes 1769504 | tf_op jit(solution)/shard_map/ppermute | solution.py:33
  85.7 9.3 %tick0.1 = (bf16[2,256,1536]{2,1,0:T(8,128)(2,1)}, bf16[2,256,1536]{2,1,0:T(8,128)(2,1)}, bf16[1536,6144]{1,0:T(8,128)(2,1)S(1)}, bf16[48,1664]{1,0:T(8,128)(2,1)S(1)}) custom-call(s32[2,8]{1,0:T(2,128)S(1)} %copy-done.7, s32[2]{0:T(128)S(1)} %copy-done.8, f32[5]{0:T(128)S(1)} %copy-done.9, ...), custom_call_target="tpu_custom_call", output_to_operand_aliasing={{0}: (10, {}), {1}: (11, {}), {2}: (14, {})} | custom-call | tf_op jit(solution)/shard_map/tick0/pallas_call | solution.py:461
  95.0 2.0 %collective-permute-start.13 = (bf16[48,1664]{1,0:T(8,128)(2,1)S(1)}, bf16[48,1664]{1,0:T(8,128)(2,1)S(1)}, u32[]{:S(2)}, u32[]{:S(2)}) collective-permute-start(bf16[48,1664]{1,0:T(8,128)(2,1)S(1)} %get-tuple-element.50), channel_id=1, source_target_pairs={{0,16},{16,32},{32,48},{48,64},{64,80},{80,96},{96,112},{112,128},... | collective-permute-start | bytes 479240 | tf_op jit(solution)/shard_map/ppermute | solution.py:39
  97.0 10.8 %collective-permute-done.13.refs_12_ = bf16[48,1664]{1,0:T(8,128)(2,1)S(1)} collective-permute-done((bf16[48,1664]{1,0:T(8,128)(2,1)S(1)}, bf16[48,1664]{1,0:T(8,128)(2,1)S(1)}, u32[]{:S(2)}, u32[]{:S(2)}) %collective-permute-start.13) | collective-permute-done | bytes 159776 | tf_op jit(solution)/shard_map/ppermute | solution.py:39
  107.8 8.4 %tick1.1 = (bf16[2,256,1536]{2,1,0:T(8,128)(2,1)}, bf16[2,256,1536]{2,1,0:T(8,128)(2,1)}, bf16[48,1664]{1,0:T(8,128)(2,1)S(1)}) custom-call(s32[2,8]{1,0:T(2,128)S(1)} %copy-done.7, s32[2]{0:T(128)S(1)} %copy-done.8, f32[5]{0:T(128)S(1)} %copy-done.9, f32[1,1536]{1,0:T(1,128)S(1)} %copy-done.6, ...), custom_call_target="tpu_custom_call", output_to_operand_aliasing={{0}: (10, {}), {1}: (11, {})} | custom-call | tf_op jit(solution)/shard_map/tick1/pallas_call | solution.py:461
  116.3 9.2 %collective-permute-done.14.refs_12_ = bf16[48,1664]{1,0:T(8,128)(2,1)S(1)} collective-permute-done((bf16[48,1664]{1,0:T(8,128)(2,1)S(1)}, bf16[48,1664]{1,0:T(8,128)(2,1)S(1)}, u32[]{:S(2)}, u32[]{:S(2)}) %collective-permute-start.14) | collective-permute-done | bytes 159776 | tf_op jit(solution)/shard_map/ppermute | solution.py:39
  125.5 8.6 %tick2.1 = (bf16[2,256,1536]{2,1,0:T(8,128)(2,1)}, bf16[2,256,1536]{2,1,0:T(8,128)(2,1)}, bf16[48,1664]{1,0:T(8,128)(2,1)S(1)}) custom-call(s32[2,8]{1,0:T(2,128)S(1)} %copy-done.7, s32[2]{0:T(128)S(1)} %copy-done.8, f32[5]{0:T(128)S(1)} %copy-done.9, f32[1,1536]{1,0:T(1,128)S(1)} %copy-done.6, ...), custom_call_target="tpu_custom_call", output_to_operand_aliasing={{0}: (10, {}), {1}: (11, {})} | custom-call | tf_op jit(solution)/shard_map/tick2/pallas_call | solution.py:461
  134.2 8.9 %collective-permute-done.15.received = bf16[48,1664]{1,0:T(8,128)(2,1)S(1)} collective-permute-done((bf16[48,1664]{1,0:T(8,128)(2,1)S(1)}, bf16[48,1664]{1,0:T(8,128)(2,1)S(1)}, u32[]{:S(2)}, u32[]{:S(2)}) %collective-permute-start.15) | collective-permute-done | bytes 159776 | tf_op jit(solution)/shard_map/ppermute | solution.py:39
  143.1 1.4 final.1
  (30 shorter events, 0.4 us)
Async XLA Ops:
  1.9 15.1 %collective-permute-start = (bf16[48,6144]{1,0:T(8,128)(2,1)S(1)}, bf16[48,6144]{1,0:T(8,128)(2,1)S(1)}, u32[]{:S(2)}, u32[]{:S(2)}) collective-permute-start(bf16[48,6144]{1,0:T(8,128)(2,1)S(1)} %get-tuple-element.32.refs_0_), channel_id=1, source_target_pairs={{0,2},{1,3},{2,4},{3,5},{4,6},{5,7},{6,0},{7,1},{8,10},{9,11},{10,... | collective-permute-start | bytes 1769480 | tf_op jit(solution)/shard_map/ppermute | solution.py:33
  4.0 14.6 %collective-permute-start.1 = (bf16[48,6144]{1,0:T(8,128)(2,1)S(1)}, bf16[48,6144]{1,0:T(8,128)(2,1)S(1)}, u32[]{:S(2)}, u32[]{:S(2)}) collective-permute-start(bf16[48,6144]{1,0:T(8,128)(2,1)S(1)} %get-tuple-element.33.refs_1_), channel_id=1, source_target_pairs={{0,6},{1,7},{2,0},{3,1},{4,2},{5,3},{6,4},{7,5},{8,14},{9,15},{10,... | collective-permute-start | bytes 1769480 | tf_op jit(solution)/shard_map/ppermute | solution.py:33
  4.0 16.3 %collective-permute-start.2 = (bf16[48,6144]{1,0:T(8,128)(2,1)S(1)}, bf16[48,6144]{1,0:T(8,128)(2,1)S(1)}, u32[]{:S(2)}, u32[]{:S(2)}) collective-permute-start(bf16[48,6144]{1,0:T(8,128)(2,1)S(1)} %get-tuple-element.32.refs_0_), channel_id=1, source_target_pairs={{0,8},{1,9},{2,10},{3,11},{4,12},{5,13},{6,14},{7,15},{8,0},{9,1},... | collective-permute-start | bytes 1769480 | tf_op jit(solution)/shard_map/ppermute | solution.py:33
  5.5 25.7 %collective-permute-start.3 = (bf16[48,6144]{1,0:T(8,128)(2,1)S(1)}, bf16[48,6144]{1,0:T(8,128)(2,1)S(1)}, u32[]{:S(2)}, u32[]{:S(2)}) collective-permute-start(bf16[48,6144]{1,0:T(8,128)(2,1)S(1)} %get-tuple-element.33.refs_1_), channel_id=1, source_target_pairs={{0,8},{1,9},{2,10},{3,11},{4,12},{5,13},{6,14},{7,15},{8,0},{9,1},... | collective-permute-start | bytes 1769480 | tf_op jit(solution)/shard_map/ppermute | solution.py:33
  17.1 14.2 %collective-permute-start.4 = (bf16[48,6144]{1,0:T(8,128)(2,1)S(1)}, bf16[48,6144]{1,0:T(8,128)(2,1)S(1)}, u32[]{:S(2)}, u32[]{:S(2)}) collective-permute-start(bf16[48,6144]{1,0:T(8,128)(2,1)S(1)} %collective-permute-done.refs_2_), channel_id=1, source_target_pairs={{0,2},{1,3},{2,4},{3,5},{4,6},{5,7},{6,0},{7,1},{8,10},{9,11},{10,... | collective-permute-start | bytes 1769480 | tf_op jit(solution)/shard_map/ppermute | solution.py:33
  18.6 13.9 %collective-permute-start.5 = (bf16[48,6144]{1,0:T(8,128)(2,1)S(1)}, bf16[48,6144]{1,0:T(8,128)(2,1)S(1)}, u32[]{:S(2)}, u32[]{:S(2)}) collective-permute-start(bf16[48,6144]{1,0:T(8,128)(2,1)S(1)} %collective-permute-done.1.refs_3_), channel_id=1, source_target_pairs={{0,6},{1,7},{2,0},{3,1},{4,2},{5,3},{6,4},{7,5},{8,14},{9,15},{10,... | collective-permute-start | bytes 1769480 | tf_op jit(solution)/shard_map/ppermute | solution.py:33
  34.6 8.0 %collective-permute-start.6 = (bf16[384,6144]{1,0:T(8,128)(2,1)S(1)}, bf16[384,6144]{1,0:T(8,128)(2,1)S(1)}, u32[]{:S(2)}, u32[]{:S(2)}) collective-permute-start(bf16[384,6144]{1,0:T(8,128)(2,1)S(1)} %get-tuple-element.34), channel_id=1, source_target_pairs={{0,1},{1,0},{2,3},{3,2},{4,5},{5,4},{6,7},{7,6},{8,9},{9,8},{10,11... | collective-permute-start | bytes 14155784 | tf_op jit(solution)/shard_map/ppermute | solution.py:33
  34.7 29.4 %collective-permute-start.7 = (bf16[96,6144]{1,0:T(8,128)(2,1)S(1)}, bf16[96,6144]{1,0:T(8,128)(2,1)S(1)}, u32[]{:S(2)}, u32[]{:S(2)}) collective-permute-start(bf16[96,6144]{1,0:T(8,128)(2,1)S(1)} %get-tuple-element.36), channel_id=1, source_target_pairs={{0,8},{1,9},{2,10},{3,11},{4,12},{5,13},{6,14},{7,15},{8,0},{9,1},... | collective-permute-start | bytes 3538952 | tf_op jit(solution)/shard_map/ppermute | solution.py:33
  37.5 40.7 %collective-permute-start.8 = (bf16[144,6144]{1,0:T(8,128)(2,1)S(1)}, bf16[144,6144]{1,0:T(8,128)(2,1)S(1)}, u32[]{:S(2)}, u32[]{:S(2)}) collective-permute-start(bf16[144,6144]{1,0:T(8,128)(2,1)S(1)} %get-tuple-element.41), channel_id=1, source_target_pairs={{0,2},{1,3},{2,4},{3,5},{4,6},{5,7},{6,0},{7,1},{8,10},{9,11},{10,... | collective-permute-start | bytes 5308424 | tf_op jit(solution)/shard_map/ppermute | solution.py:33
  37.8 41.6 %collective-permute-start.9 = (bf16[144,6144]{1,0:T(8,128)(2,1)S(1)}, bf16[144,6144]{1,0:T(8,128)(2,1)S(1)}, u32[]{:S(2)}, u32[]{:S(2)}) collective-permute-start(bf16[144,6144]{1,0:T(8,128)(2,1)S(1)} %get-tuple-element.42), channel_id=1, source_target_pairs={{0,6},{1,7},{2,0},{3,1},{4,2},{5,3},{6,4},{7,5},{8,14},{9,15},{10,... | collective-permute-start | bytes 5308424 | tf_op jit(solution)/shard_map/ppermute | solution.py:33
  64.1 15.3 %collective-permute-start.10 = (bf16[96,6144]{1,0:T(8,128)(2,1)S(1)}, bf16[96,6144]{1,0:T(8,128)(2,1)S(1)}, u32[]{:S(2)}, u32[]{:S(2)}) collective-permute-start(bf16[96,6144]{1,0:T(8,128)(2,1)S(1)} %collective-permute-done.7.refs_1_), channel_id=1, source_target_pairs={{0,1},{1,0},{2,3},{3,2},{4,5},{5,4},{6,7},{7,6},{8,9},{9,8},{10,11... | collective-permute-start | bytes 3538952 | tf_op jit(solution)/shard_map/ppermute | solution.py:33
  79.4 3.7 %collective-permute-start.11 = (bf16[144,6144]{1,0:T(8,128)(2,1)S(1)}, bf16[144,6144]{1,0:T(8,128)(2,1)S(1)}, u32[]{:S(2)}, u32[]{:S(2)}) collective-permute-start(bf16[144,6144]{1,0:T(8,128)(2,1)S(1)} %collective-permute-done.8.refs_15_), channel_id=1, source_target_pairs={{0,1},{1,0},{2,3},{3,2},{4,5},{5,4},{6,7},{7,6},{8,9},{9,8},{10,11... | collective-permute-start | bytes 5308424 | tf_op jit(solution)/shard_map/ppermute | solution.py:33
  79.4 6.2 %collective-permute-start.12 = (bf16[144,6144]{1,0:T(8,128)(2,1)S(1)}, bf16[144,6144]{1,0:T(8,128)(2,1)S(1)}, u32[]{:S(2)}, u32[]{:S(2)}) collective-permute-start(bf16[144,6144]{1,0:T(8,128)(2,1)S(1)} %collective-permute-done.9.refs_16_), channel_id=1, source_target_pairs={{0,1},{1,0},{2,3},{3,2},{4,5},{5,4},{6,7},{7,6},{8,9},{9,8},{10,11... | collective-permute-start | bytes 5308424 | tf_op jit(solution)/shard_map/ppermute | solution.py:33
  79.9 5.7 %copy-start = (bf16[1,2,256,1536]{3,2,1,0:T(8,128)(2,1)S(1)}, bf16[1,2,256,1536]{3,2,1,0:T(8,128)(2,1)}, u32[]{:S(2)}) copy-start(bf16[1,2,256,1536]{3,2,1,0:T(8,128)(2,1)} %param.20) | copy-start | bytes 4718596
  79.9 5.7 %copy-start.1 = (bf16[1,2,256,1536]{3,2,1,0:T(8,128)(2,1)S(1)}, bf16[1,2,256,1536]{3,2,1,0:T(8,128)(2,1)}, u32[]{:S(2)}) copy-start(bf16[1,2,256,1536]{3,2,1,0:T(8,128)(2,1)} %param.21) | copy-start | bytes 4718596
  79.9 5.7 %copy-start.2 = (bf16[64,1536]{1,0:T(8,128)(2,1)S(1)}, bf16[64,1536]{1,0:T(8,128)(2,1)}, u32[]{:S(2)}) copy-start(bf16[64,1536]{1,0:T(8,128)(2,1)} %embed_w.1) | copy-start | bytes 589828
  79.9 5.7 %copy-start.3 = (bf16[1536,64]{0,1:T(8,128)(2,1)S(1)}, bf16[1536,64]{0,1:T(8,128)(2,1)}, u32[]{:S(2)}) copy-start(bf16[1536,64]{0,1:T(8,128)(2,1)} %param.27) | copy-start | bytes 589828
  79.9 5.7 %copy-start.4 = (bf16[1,1,48,1536]{3,2,1,0:T(8,128)(2,1)S(1)}, bf16[1,1,48,1536]{3,2,1,0:T(8,128)(2,1)}, u32[]{:S(2)}) copy-start(bf16[1,1,48,1536]{3,2,1,0:T(8,128)(2,1)} %param.16) | copy-start | bytes 442372
  80.0 5.7 %copy-start.5 = (f32[1536]{0:T(1024)S(1)}, f32[1536]{0:T(1024)}, u32[]{:S(2)}) copy-start(f32[1536]{0:T(1024)} %embed_b.1) | copy-start | bytes 18436
  80.0 5.7 %copy-start.6 = (f32[1,1536]{1,0:T(1,128)S(1)}, f32[1,1536]{1,0:T(1,128)}, u32[]{:S(2)}) copy-start(f32[1,1536]{1,0:T(1,128)} %refs_3_.5) | copy-start | bytes 18436
  80.0 5.7 %copy-start.7 = (s32[2,8]{1,0:T(2,128)S(1)}, s32[2,8]{1,0:T(2,128)}, u32[]{:S(2)}) copy-start(s32[2,8]{1,0:T(2,128)} %lengths.1) | copy-start | bytes 196
  80.0 5.7 %copy-start.8 = (s32[2]{0:T(128)S(1)}, s32[2]{0:T(128)}, u32[]{:S(2)}) copy-start(s32[2]{0:T(128)} %refs_1_.5) | copy-start | bytes 28
  80.0 5.7 %copy-start.9 = (f32[5]{0:T(128)S(1)}, f32[5]{0:T(128)}, u32[]{:S(2)}) copy-start(f32[5]{0:T(128)} %refs_2_.5) | copy-start | bytes 64
  80.0 5.7 %copy-start.10 = (f32[64]{0:T(128)S(1)}, f32[64]{0:T(128)}, u32[]{:S(2)}) copy-start(f32[64]{0:T(128)} %refs_7_.5) | copy-start | bytes 772
  95.0 12.8 %collective-permute-start.13 = (bf16[48,1664]{1,0:T(8,128)(2,1)S(1)}, bf16[48,1664]{1,0:T(8,128)(2,1)S(1)}, u32[]{:S(2)}, u32[]{:S(2)}) collective-permute-start(bf16[48,1664]{1,0:T(8,128)(2,1)S(1)} %get-tuple-element.50), channel_id=1, source_target_pairs={{0,16},{16,32},{32,48},{48,64},{64,80},{80,96},{96,112},{112,128},... | collective-permute-start | bytes 479240 | tf_op jit(solution)/shard_map/ppermute | solution.py:39
  116.2 9.3 %collective-permute-start.14 = (bf16[48,1664]{1,0:T(8,128)(2,1)S(1)}, bf16[48,1664]{1,0:T(8,128)(2,1)S(1)}, u32[]{:S(2)}, u32[]{:S(2)}) collective-permute-start(bf16[48,1664]{1,0:T(8,128)(2,1)S(1)} %get-tuple-element.54), channel_id=1, source_target_pairs={{0,16},{16,32},{32,48},{48,64},{64,80},{80,96},{96,112},{112,128},... | collective-permute-start | bytes 479240 | tf_op jit(solution)/shard_map/ppermute | solution.py:39
  134.2 9.0 %collective-permute-start.15 = (bf16[48,1664]{1,0:T(8,128)(2,1)S(1)}, bf16[48,1664]{1,0:T(8,128)(2,1)S(1)}, u32[]{:S(2)}, u32[]{:S(2)}) collective-permute-start(bf16[48,1664]{1,0:T(8,128)(2,1)S(1)} %get-tuple-element.55), channel_id=1, source_target_pairs={{0,16},{16,32},{32,48},{48,64},{64,80},{80,96},{96,112},{112,128},... | collective-permute-start | bytes 479240 | tf_op jit(solution)/shard_map/ppermute | solution.py:39

commit v4 on v3

--- a/solution.py
+++ b/solution.py
@@ -104,25 +104,28 @@
     return jnp.where(row_ids < live, rows, 0.0).astype(jnp.bfloat16)
 
 
-def attend(proj, image_k, image_v, text_k, text_v, attended):
+def attend(proj, image_k, image_v, text_k, text_v, attended, scores):
     width = attended.shape[1]
+    tokens = text_k.shape[0]
     scale = 1.0 / math.sqrt(HEAD_DIM)
     across = (((1,), (1,)), ((), ()))
-    for head in range(width // HEAD_DIM):
-        cols = slice(head * HEAD_DIM, (head + 1) * HEAD_DIM)
-        queries = proj[:, cols]
-        on_text = lax.dot_general(queries, text_k[:, cols], across, preferred_element_type=jnp.float32)
-        on_image = lax.dot_general(queries, image_k[:, cols], across, preferred_element_type=jnp.float32)
-        highest = jnp.maximum(
-            jnp.max(on_text, axis=-1, keepdims=True), jnp.max(on_image, axis=-1, keepdims=True)
-        )
-        on_text = jnp.exp((on_text - highest) * scale)
-        on_image = jnp.exp((on_image - highest) * scale)
-        total = jnp.sum(on_text, axis=-1, keepdims=True) + jnp.sum(on_image, axis=-1, keepdims=True)
+    heads = range(width // HEAD_DIM)
+    columns = [slice(head * HEAD_DIM, (head + 1) * HEAD_DIM) for head in heads]
+    for head in heads:
+        queries = proj[:, columns[head]]
+        for at, keys in enumerate((text_k, image_k)):
+            scores[head, :, at * tokens : (at + 1) * tokens] = lax.dot_general(
+                queries, keys[:, columns[head]], across, preferred_element_type=jnp.float32
+            )
+    for head in heads:
+        row = scores[head]
+        raised = jnp.exp((row - jnp.max(row, axis=-1, keepdims=True)) * scale)
+        total = jnp.sum(raised, axis=-1, keepdims=True)
+        raised = raised.astype(jnp.bfloat16)
         mixed = jnp.dot(
-            on_text.astype(jnp.bfloat16), text_v[:, cols], preferred_element_type=jnp.float32
-        ) + jnp.dot(on_image.astype(jnp.bfloat16), image_v[:, cols], preferred_element_type=jnp.float32)
-        attended[:, cols] = (mixed / total).astype(jnp.bfloat16)
+            raised[:, :tokens], text_v[:, columns[head]], preferred_element_type=jnp.float32
+        ) + jnp.dot(raised[:, tokens:], image_v[:, columns[head]], preferred_element_type=jnp.float32)
+        attended[:, columns[head]] = (mixed / total).astype(jnp.bfloat16)
 
 
 def weight_copies(pieces, weights, rows, blocks, sems):
@@ -211,7 +214,7 @@
     else:
         received, weights = rest[:2]
         keys, values, sent, *scratch = rest[2:]
-    hidden, image_k, image_v, txt_k, txt_v, proj, attended, cache_sem, back_sem, *weight_sem = scratch
+    hidden, image_k, image_v, txt_k, txt_v, proj, attended, scores, cache_sem, back_sem, *weight_sem = scratch
     width = hidden.shape[1]
     section = lax.axis_index("phase")
     picture, length, offset = batch_of(tick, section, sections, lengths)
@@ -273,7 +276,7 @@
     for back in backs:
         back.start()
 
-    attend(proj, image_k, image_v, txt_k, txt_v, attended)
+    attend(proj, image_k, image_v, txt_k, txt_v, attended, scores)
 
     summed = hidden[...].astype(jnp.float32) + jnp.dot(
         attended[...], weights[:, 3 * width :], preferred_element_type=jnp.float32
@@ -453,6 +456,7 @@
             *[pltpu.VMEM((tokens, width), jnp.bfloat16)] * 4,
             pltpu.VMEM((rows, 3 * width), jnp.bfloat16),
             pltpu.VMEM((rows, width), jnp.bfloat16),
+            pltpu.VMEM((width // HEAD_DIM, rows, 2 * tokens), jnp.float32),
             pltpu.SemaphoreType.DMA((4,)),
             pltpu.SemaphoreType.DMA((2,)),
         ]

time: 145 us -> 138 us (0.952)
  Pallas kernels: 36 us -> 29.5 us
    pallas_call x3, Pallas kernels: 26.3 us -> 19.8 us  [shards(): pl.pallas_call(functools.partial(tick_kernel, tick, sections, first, part...]
  transfers between devices with their start and end apart: 16 -> 16, of which waited for: 14 -> 14; matrix products, arithmetic and copies ran while one was open for 0% -> 0% of each run, Pallas kernels for 3% -> 4%
where the time goes in v4:
time: 138 us
  waiting for transfers between devices  93.5 us (68%)
  Pallas kernels  29.5 us (21%)
  starting transfers between devices  13.8 us (10%)
    ppermute x13, waiting for transfers between devices, moved(): return lax.ppermute(value, 'dp', pairs)  64.9 us
    ppermute x3, waiting for transfers between devices, shifted(): return lax.ppermute(value, 'phase', pairs)  28.6 us
    pallas_call x3, Pallas kernels, shards(): pl.pallas_call(functools.partial(tick_kernel, tick, sections, first, part...  19.8 us
    ppermute x13, starting transfers between devices, moved(): return lax.ppermute(value, 'dp', pairs)  11.7 us
    pallas_call x2, Pallas kernels, loaded(): pl.pallas_call(functools.partial(load_kernel, part, first, blocks, len(pi...  4.95 us
  transfers between devices with their start and end apart: 16, of which 14 were waited for; matrix products, arithmetic and copies ran while one was open for 0% of the time, Pallas kernels for 4%

profile of v4, /device:TPU:24, one launch (start us, length us, event | category | flops | bytes accessed | tf_op | source)
XLA Modules:
  0.0 137.7 jit_solution(2321620518431050257)
XLA Ops:
  0.6 1.3 own.1
  1.9 2.0 %collective-permute-start = (bf16[48,6144]{1,0:T(8,128)(2,1)S(1)}, bf16[48,6144]{1,0:T(8,128)(2,1)S(1)}, u32[]{:S(2)}, u32[]{:S(2)}) collective-permute-start(bf16[48,6144]{1,0:T(8,128)(2,1)S(1)} %get-tuple-element.32.refs_0_), channel_id=1, source_target_pairs={{0,2},{1,3},{2,4},{3,5},{4,6},{5,7},{6,0},{7,1},{8,10},{9,11},{10,... | collective-permute-start | bytes 1769480 | tf_op jit(solution)/shard_map/ppermute | solution.py:33
  4.0 1.5 %collective-permute-start.2 = (bf16[48,6144]{1,0:T(8,128)(2,1)S(1)}, bf16[48,6144]{1,0:T(8,128)(2,1)S(1)}, u32[]{:S(2)}, u32[]{:S(2)}) collective-permute-start(bf16[48,6144]{1,0:T(8,128)(2,1)S(1)} %get-tuple-element.32.refs_0_), channel_id=1, source_target_pairs={{0,8},{1,9},{2,10},{3,11},{4,12},{5,13},{6,14},{7,15},{8,0},{9,1},... | collective-permute-start | bytes 1769480 | tf_op jit(solution)/shard_map/ppermute | solution.py:33
  5.5 0.5 collective-permute-start.3
  6.1 11.0 %collective-permute-done.refs_2_ = bf16[48,6144]{1,0:T(8,128)(2,1)S(1)} collective-permute-done((bf16[48,6144]{1,0:T(8,128)(2,1)S(1)}, bf16[48,6144]{1,0:T(8,128)(2,1)S(1)}, u32[]{:S(2)}, u32[]{:S(2)}) %collective-permute-start) | collective-permute-done | bytes 589856 | tf_op jit(solution)/shard_map/ppermute | solution.py:33
  17.1 1.5 %collective-permute-start.4 = (bf16[48,6144]{1,0:T(8,128)(2,1)S(1)}, bf16[48,6144]{1,0:T(8,128)(2,1)S(1)}, u32[]{:S(2)}, u32[]{:S(2)}) collective-permute-start(bf16[48,6144]{1,0:T(8,128)(2,1)S(1)} %collective-permute-done.refs_2_), channel_id=1, source_target_pairs={{0,2},{1,3},{2,4},{3,5},{4,6},{5,7},{6,0},{7,1},{8,10},{9,11},{10,... | collective-permute-start | bytes 1769480 | tf_op jit(solution)/shard_map/ppermute | solution.py:33
  18.6 0.5 collective-permute-start.5
  19.1 1.2 collective-permute-done.2.refs_4_
  20.3 10.9 %collective-permute-done.3.refs_5_ = bf16[48,6144]{1,0:T(8,128)(2,1)S(1)} collective-permute-done((bf16[48,6144]{1,0:T(8,128)(2,1)S(1)}, bf16[48,6144]{1,0:T(8,128)(2,1)S(1)}, u32[]{:S(2)}, u32[]{:S(2)}) %collective-permute-start.3) | collective-permute-done | bytes 589856 | tf_op jit(solution)/shard_map/ppermute | solution.py:33
  31.3 1.2 collective-permute-done.5.refs_7_
  32.5 2.1 %stack.1 = (bf16[384,6144]{1,0:T(8,128)(2,1)S(1)}, bf16[144,6144]{1,0:T(8,128)(2,1)S(1)}, bf16[144,6144]{1,0:T(8,128)(2,1)S(1)}, bf16[96,6144]{1,0:T(8,128)(2,1)S(1)}) custom-call(bf16[48,6144]{1,0:T(8,128)(2,1)S(1)} %get-tuple-element.32.refs_0_, bf16[48,6144]{1,0:T(8,128)(2,1)S(1)} %get-tuple-element.33.refs_1_, ...), custom_call_target="tpu_custom_call" | custom-call | tf_op jit(solution)/shard_map/stack/pallas_call | solution.py:379
  34.6 0.1 collective-permute-start.6
  34.7 2.9 %collective-permute-start.7 = (bf16[96,6144]{1,0:T(8,128)(2,1)S(1)}, bf16[96,6144]{1,0:T(8,128)(2,1)S(1)}, u32[]{:S(2)}, u32[]{:S(2)}) collective-permute-start(bf16[96,6144]{1,0:T(8,128)(2,1)S(1)} %get-tuple-element.36), channel_id=1, source_target_pairs={{0,8},{1,9},{2,10},{3,11},{4,12},{5,13},{6,14},{7,15},{8,0},{9,1},... | collective-permute-start | bytes 3538952 | tf_op jit(solution)/shard_map/ppermute | solution.py:33
  37.5 0.3 collective-permute-start.8
  37.8 1.7 %collective-permute-start.9 = (bf16[144,6144]{1,0:T(8,128)(2,1)S(1)}, bf16[144,6144]{1,0:T(8,128)(2,1)S(1)}, u32[]{:S(2)}, u32[]{:S(2)}) collective-permute-start(bf16[144,6144]{1,0:T(8,128)(2,1)S(1)} %get-tuple-element.42), channel_id=1, source_target_pairs={{0,6},{1,7},{2,0},{3,1},{4,2},{5,3},{6,4},{7,5},{8,14},{9,15},{10,... | collective-permute-start | bytes 5308424 | tf_op jit(solution)/shard_map/ppermute | solution.py:33
  39.6 3.0 %collective-permute-done.6.refs_8_ = bf16[384,6144]{1,0:T(8,128)(2,1)S(1)} collective-permute-done((bf16[384,6144]{1,0:T(8,128)(2,1)S(1)}, bf16[384,6144]{1,0:T(8,128)(2,1)S(1)}, u32[]{:S(2)}, u32[]{:S(2)}) %collective-permute-start.6) | collective-permute-done | bytes 4718624 | tf_op jit(solution)/shard_map/ppermute | solution.py:33
  42.6 4.0 %near.1 = (bf16[1536,6144]{1,0:T(8,128)(2,1)S(1)}, bf16[2,256,1536]{2,1,0:T(8,128)(2,1)}, bf16[2,256,1536]{2,1,0:T(8,128)(2,1)}) custom-call(bf16[48,6144]{1,0:T(8,128)(2,1)S(1)} %get-tuple-element.32.refs_0_, bf16[48,6144]{1,0:T(8,128)(2,1)S(1)} %get-tuple-element.33.refs_1_, bf16[48,6144]{1,0:T(8,128)(2,1)S(1)} %collective-permute-done.refs_2_, ...), custom_call_target="tpu_custom_call" | custom-call | tf_op jit(solution)/shard_map/near/pallas_call | solution.py:397
  46.6 17.5 %collective-permute-done.7.refs_1_ = bf16[96,6144]{1,0:T(8,128)(2,1)S(1)} collective-permute-done((bf16[96,6144]{1,0:T(8,128)(2,1)S(1)}, bf16[96,6144]{1,0:T(8,128)(2,1)S(1)}, u32[]{:S(2)}, u32[]{:S(2)}) %collective-permute-start.7) | collective-permute-done | bytes 1179680 | tf_op jit(solution)/shard_map/ppermute | solution.py:33
  64.1 14.1 %collective-permute-done.8.refs_15_ = bf16[144,6144]{1,0:T(8,128)(2,1)S(1)} collective-permute-done((bf16[144,6144]{1,0:T(8,128)(2,1)S(1)}, bf16[144,6144]{1,0:T(8,128)(2,1)S(1)}, u32[]{:S(2)}, u32[]{:S(2)}) %collective-permute-start.8) | collective-permute-done | bytes 1769504 | tf_op jit(solution)/shard_map/ppermute | solution.py:33
  78.2 1.2 collective-permute-done.9.refs_16_
  79.4 0.5 collective-permute-start.12
  80.0 0.9 far.1
  81.0 2.2 %collective-permute-done.11.refs_17_ = bf16[144,6144]{1,0:T(8,128)(2,1)S(1)} collective-permute-done((bf16[144,6144]{1,0:T(8,128)(2,1)S(1)}, bf16[144,6144]{1,0:T(8,128)(2,1)S(1)}, u32[]{:S(2)}, u32[]{:S(2)}) %collective-permute-start.11) | collective-permute-done | bytes 1769504 | tf_op jit(solution)/shard_map/ppermute | solution.py:33
  83.1 2.5 %collective-permute-done.12.refs_18_ = bf16[144,6144]{1,0:T(8,128)(2,1)S(1)} collective-permute-done((bf16[144,6144]{1,0:T(8,128)(2,1)S(1)}, bf16[144,6144]{1,0:T(8,128)(2,1)S(1)}, u32[]{:S(2)}, u32[]{:S(2)}) %collective-permute-start.12) | collective-permute-done | bytes 1769504 | tf_op jit(solution)/shard_map/ppermute | solution.py:33
  85.7 7.5 %tick0.1 = (bf16[2,256,1536]{2,1,0:T(8,128)(2,1)}, bf16[2,256,1536]{2,1,0:T(8,128)(2,1)}, bf16[1536,6144]{1,0:T(8,128)(2,1)S(1)}, bf16[48,1664]{1,0:T(8,128)(2,1)S(1)}) custom-call(s32[2,8]{1,0:T(2,128)S(1)} %copy-done.7, s32[2]{0:T(128)S(1)} %copy-done.8, f32[5]{0:T(128)S(1)} %copy-done.9, ...), custom_call_target="tpu_custom_call", output_to_operand_aliasing={{0}: (10, {}), {1}: (11, {}), {2}: (14, {})} | custom-call | tf_op jit(solution)/shard_map/tick0/pallas_call | solution.py:465
  93.2 2.0 %collective-permute-start.13 = (bf16[48,1664]{1,0:T(8,128)(2,1)S(1)}, bf16[48,1664]{1,0:T(8,128)(2,1)S(1)}, u32[]{:S(2)}, u32[]{:S(2)}) collective-permute-start(bf16[48,1664]{1,0:T(8,128)(2,1)S(1)} %get-tuple-element.50), channel_id=1, source_target_pairs={{0,16},{16,32},{32,48},{48,64},{64,80},{80,96},{96,112},{112,128},... | collective-permute-start | bytes 479240 | tf_op jit(solution)/shard_map/ppermute | solution.py:39
  95.2 10.5 %collective-permute-done.13.refs_12_ = bf16[48,1664]{1,0:T(8,128)(2,1)S(1)} collective-permute-done((bf16[48,1664]{1,0:T(8,128)(2,1)S(1)}, bf16[48,1664]{1,0:T(8,128)(2,1)S(1)}, u32[]{:S(2)}, u32[]{:S(2)}) %collective-permute-start.13) | collective-permute-done | bytes 159776 | tf_op jit(solution)/shard_map/ppermute | solution.py:39
  105.7 6.0 %tick1.1 = (bf16[2,256,1536]{2,1,0:T(8,128)(2,1)}, bf16[2,256,1536]{2,1,0:T(8,128)(2,1)}, bf16[48,1664]{1,0:T(8,128)(2,1)S(1)}) custom-call(s32[2,8]{1,0:T(2,128)S(1)} %copy-done.7, s32[2]{0:T(128)S(1)} %copy-done.8, f32[5]{0:T(128)S(1)} %copy-done.9, f32[1,1536]{1,0:T(1,128)S(1)} %copy-done.6, ...), custom_call_target="tpu_custom_call", output_to_operand_aliasing={{0}: (10, {}), {1}: (11, {})} | custom-call | tf_op jit(solution)/shard_map/tick1/pallas_call | solution.py:465
  111.9 9.2 %collective-permute-done.14.refs_12_ = bf16[48,1664]{1,0:T(8,128)(2,1)S(1)} collective-permute-done((bf16[48,1664]{1,0:T(8,128)(2,1)S(1)}, bf16[48,1664]{1,0:T(8,128)(2,1)S(1)}, u32[]{:S(2)}, u32[]{:S(2)}) %collective-permute-start.14) | collective-permute-done | bytes 159776 | tf_op jit(solution)/shard_map/ppermute | solution.py:39
  121.1 6.2 %tick2.1 = (bf16[2,256,1536]{2,1,0:T(8,128)(2,1)}, bf16[2,256,1536]{2,1,0:T(8,128)(2,1)}, bf16[48,1664]{1,0:T(8,128)(2,1)S(1)}) custom-call(s32[2,8]{1,0:T(2,128)S(1)} %copy-done.7, s32[2]{0:T(128)S(1)} %copy-done.8, f32[5]{0:T(128)S(1)} %copy-done.9, f32[1,1536]{1,0:T(1,128)S(1)} %copy-done.6, ...), custom_call_target="tpu_custom_call", output_to_operand_aliasing={{0}: (10, {}), {1}: (11, {})} | custom-call | tf_op jit(solution)/shard_map/tick2/pallas_call | solution.py:465
  127.4 8.9 %collective-permute-done.15.received = bf16[48,1664]{1,0:T(8,128)(2,1)S(1)} collective-permute-done((bf16[48,1664]{1,0:T(8,128)(2,1)S(1)}, bf16[48,1664]{1,0:T(8,128)(2,1)S(1)}, u32[]{:S(2)}, u32[]{:S(2)}) %collective-permute-start.15) | collective-permute-done | bytes 159776 | tf_op jit(solution)/shard_map/ppermute | solution.py:39
  136.3 1.4 %final.1 = (bf16[48,1536]{1,0:T(8,128)(2,1)}, bf16[48,64]{1,0:T(8,128)(2,1)}) custom-call(s32[2,8]{1,0:T(2,128)S(1)} %copy-done.7, bf16[64,1536]{1,0:T(8,128)(2,1)S(1)} %copy-done.2, f32[1536]{0:T(1024)S(1)} %copy-done.5, bf16[48,1664]{1,0:T(8,128)(2,1)S(1)} %collective-permute-done.15.received), custom_call_target="tpu_custom_call" | custom-call | tf_op jit(solution)/shard_map/final/pallas_call | solution.py:481
  (30 shorter events, 0.4 us)
Async XLA Ops:
  1.9 15.1 %collective-permute-start = (bf16[48,6144]{1,0:T(8,128)(2,1)S(1)}, bf16[48,6144]{1,0:T(8,128)(2,1)S(1)}, u32[]{:S(2)}, u32[]{:S(2)}) collective-permute-start(bf16[48,6144]{1,0:T(8,128)(2,1)S(1)} %get-tuple-element.32.refs_0_), channel_id=1, source_target_pairs={{0,2},{1,3},{2,4},{3,5},{4,6},{5,7},{6,0},{7,1},{8,10},{9,11},{10,... | collective-permute-start | bytes 1769480 | tf_op jit(solution)/shard_map/ppermute | solution.py:33
  4.0 14.6 %collective-permute-start.1 = (bf16[48,6144]{1,0:T(8,128)(2,1)S(1)}, bf16[48,6144]{1,0:T(8,128)(2,1)S(1)}, u32[]{:S(2)}, u32[]{:S(2)}) collective-permute-start(bf16[48,6144]{1,0:T(8,128)(2,1)S(1)} %get-tuple-element.33.refs_1_), channel_id=1, source_target_pairs={{0,6},{1,7},{2,0},{3,1},{4,2},{5,3},{6,4},{7,5},{8,14},{9,15},{10,... | collective-permute-start | bytes 1769480 | tf_op jit(solution)/shard_map/ppermute | solution.py:33
  4.0 16.3 %collective-permute-start.2 = (bf16[48,6144]{1,0:T(8,128)(2,1)S(1)}, bf16[48,6144]{1,0:T(8,128)(2,1)S(1)}, u32[]{:S(2)}, u32[]{:S(2)}) collective-permute-start(bf16[48,6144]{1,0:T(8,128)(2,1)S(1)} %get-tuple-element.32.refs_0_), channel_id=1, source_target_pairs={{0,8},{1,9},{2,10},{3,11},{4,12},{5,13},{6,14},{7,15},{8,0},{9,1},... | collective-permute-start | bytes 1769480 | tf_op jit(solution)/shard_map/ppermute | solution.py:33
  5.5 25.7 %collective-permute-start.3 = (bf16[48,6144]{1,0:T(8,128)(2,1)S(1)}, bf16[48,6144]{1,0:T(8,128)(2,1)S(1)}, u32[]{:S(2)}, u32[]{:S(2)}) collective-permute-start(bf16[48,6144]{1,0:T(8,128)(2,1)S(1)} %get-tuple-element.33.refs_1_), channel_id=1, source_target_pairs={{0,8},{1,9},{2,10},{3,11},{4,12},{5,13},{6,14},{7,15},{8,0},{9,1},... | collective-permute-start | bytes 1769480 | tf_op jit(solution)/shard_map/ppermute | solution.py:33
  17.1 14.2 %collective-permute-start.4 = (bf16[48,6144]{1,0:T(8,128)(2,1)S(1)}, bf16[48,6144]{1,0:T(8,128)(2,1)S(1)}, u32[]{:S(2)}, u32[]{:S(2)}) collective-permute-start(bf16[48,6144]{1,0:T(8,128)(2,1)S(1)} %collective-permute-done.refs_2_), channel_id=1, source_target_pairs={{0,2},{1,3},{2,4},{3,5},{4,6},{5,7},{6,0},{7,1},{8,10},{9,11},{10,... | collective-permute-start | bytes 1769480 | tf_op jit(solution)/shard_map/ppermute | solution.py:33
  18.6 13.9 %collective-permute-start.5 = (bf16[48,6144]{1,0:T(8,128)(2,1)S(1)}, bf16[48,6144]{1,0:T(8,128)(2,1)S(1)}, u32[]{:S(2)}, u32[]{:S(2)}) collective-permute-start(bf16[48,6144]{1,0:T(8,128)(2,1)S(1)} %collective-permute-done.1.refs_3_), channel_id=1, source_target_pairs={{0,6},{1,7},{2,0},{3,1},{4,2},{5,3},{6,4},{7,5},{8,14},{9,15},{10,... | collective-permute-start | bytes 1769480 | tf_op jit(solution)/shard_map/ppermute | solution.py:33
  34.6 8.0 %collective-permute-start.6 = (bf16[384,6144]{1,0:T(8,128)(2,1)S(1)}, bf16[384,6144]{1,0:T(8,128)(2,1)S(1)}, u32[]{:S(2)}, u32[]{:S(2)}) collective-permute-start(bf16[384,6144]{1,0:T(8,128)(2,1)S(1)} %get-tuple-element.34), channel_id=1, source_target_pairs={{0,1},{1,0},{2,3},{3,2},{4,5},{5,4},{6,7},{7,6},{8,9},{9,8},{10,11... | collective-permute-start | bytes 14155784 | tf_op jit(solution)/shard_map/ppermute | solution.py:33
  34.7 29.4 %collective-permute-start.7 = (bf16[96,6144]{1,0:T(8,128)(2,1)S(1)}, bf16[96,6144]{1,0:T(8,128)(2,1)S(1)}, u32[]{:S(2)}, u32[]{:S(2)}) collective-permute-start(bf16[96,6144]{1,0:T(8,128)(2,1)S(1)} %get-tuple-element.36), channel_id=1, source_target_pairs={{0,8},{1,9},{2,10},{3,11},{4,12},{5,13},{6,14},{7,15},{8,0},{9,1},... | collective-permute-start | bytes 3538952 | tf_op jit(solution)/shard_map/ppermute | solution.py:33
  37.5 40.7 %collective-permute-start.8 = (bf16[144,6144]{1,0:T(8,128)(2,1)S(1)}, bf16[144,6144]{1,0:T(8,128)(2,1)S(1)}, u32[]{:S(2)}, u32[]{:S(2)}) collective-permute-start(bf16[144,6144]{1,0:T(8,128)(2,1)S(1)} %get-tuple-element.41), channel_id=1, source_target_pairs={{0,2},{1,3},{2,4},{3,5},{4,6},{5,7},{6,0},{7,1},{8,10},{9,11},{10,... | collective-permute-start | bytes 5308424 | tf_op jit(solution)/shard_map/ppermute | solution.py:33
  37.8 41.6 %collective-permute-start.9 = (bf16[144,6144]{1,0:T(8,128)(2,1)S(1)}, bf16[144,6144]{1,0:T(8,128)(2,1)S(1)}, u32[]{:S(2)}, u32[]{:S(2)}) collective-permute-start(bf16[144,6144]{1,0:T(8,128)(2,1)S(1)} %get-tuple-element.42), channel_id=1, source_target_pairs={{0,6},{1,7},{2,0},{3,1},{4,2},{5,3},{6,4},{7,5},{8,14},{9,15},{10,... | collective-permute-start | bytes 5308424 | tf_op jit(solution)/shard_map/ppermute | solution.py:33
  64.1 15.3 %collective-permute-start.10 = (bf16[96,6144]{1,0:T(8,128)(2,1)S(1)}, bf16[96,6144]{1,0:T(8,128)(2,1)S(1)}, u32[]{:S(2)}, u32[]{:S(2)}) collective-permute-start(bf16[96,6144]{1,0:T(8,128)(2,1)S(1)} %collective-permute-done.7.refs_1_), channel_id=1, source_target_pairs={{0,1},{1,0},{2,3},{3,2},{4,5},{5,4},{6,7},{7,6},{8,9},{9,8},{10,11... | collective-permute-start | bytes 3538952 | tf_op jit(solution)/shard_map/ppermute | solution.py:33
  79.4 3.7 %collective-permute-start.11 = (bf16[144,6144]{1,0:T(8,128)(2,1)S(1)}, bf16[144,6144]{1,0:T(8,128)(2,1)S(1)}, u32[]{:S(2)}, u32[]{:S(2)}) collective-permute-start(bf16[144,6144]{1,0:T(8,128)(2,1)S(1)} %collective-permute-done.8.refs_15_), channel_id=1, source_target_pairs={{0,1},{1,0},{2,3},{3,2},{4,5},{5,4},{6,7},{7,6},{8,9},{9,8},{10,11... | collective-permute-start | bytes 5308424 | tf_op jit(solution)/shard_map/ppermute | solution.py:33
  79.4 6.2 %collective-permute-start.12 = (bf16[144,6144]{1,0:T(8,128)(2,1)S(1)}, bf16[144,6144]{1,0:T(8,128)(2,1)S(1)}, u32[]{:S(2)}, u32[]{:S(2)}) collective-permute-start(bf16[144,6144]{1,0:T(8,128)(2,1)S(1)} %collective-permute-done.9.refs_16_), channel_id=1, source_target_pairs={{0,1},{1,0},{2,3},{3,2},{4,5},{5,4},{6,7},{7,6},{8,9},{9,8},{10,11... | collective-permute-start | bytes 5308424 | tf_op jit(solution)/shard_map/ppermute | solution.py:33
  79.9 5.7 %copy-start = (bf16[1,2,256,1536]{3,2,1,0:T(8,128)(2,1)S(1)}, bf16[1,2,256,1536]{3,2,1,0:T(8,128)(2,1)}, u32[]{:S(2)}) copy-start(bf16[1,2,256,1536]{3,2,1,0:T(8,128)(2,1)} %param.20) | copy-start | bytes 4718596
  79.9 5.7 %copy-start.1 = (bf16[1,2,256,1536]{3,2,1,0:T(8,128)(2,1)S(1)}, bf16[1,2,256,1536]{3,2,1,0:T(8,128)(2,1)}, u32[]{:S(2)}) copy-start(bf16[1,2,256,1536]{3,2,1,0:T(8,128)(2,1)} %param.21) | copy-start | bytes 4718596
  79.9 5.7 %copy-start.2 = (bf16[64,1536]{1,0:T(8,128)(2,1)S(1)}, bf16[64,1536]{1,0:T(8,128)(2,1)}, u32[]{:S(2)}) copy-start(bf16[64,1536]{1,0:T(8,128)(2,1)} %embed_w.1) | copy-start | bytes 589828
  79.9 5.7 %copy-start.3 = (bf16[1536,64]{0,1:T(8,128)(2,1)S(1)}, bf16[1536,64]{0,1:T(8,128)(2,1)}, u32[]{:S(2)}) copy-start(bf16[1536,64]{0,1:T(8,128)(2,1)} %param.27) | copy-start | bytes 589828
  79.9 5.7 %copy-start.4 = (bf16[1,1,48,1536]{3,2,1,0:T(8,128)(2,1)S(1)}, bf16[1,1,48,1536]{3,2,1,0:T(8,128)(2,1)}, u32[]{:S(2)}) copy-start(bf16[1,1,48,1536]{3,2,1,0:T(8,128)(2,1)} %param.16) | copy-start | bytes 442372
  80.0 5.7 %copy-start.5 = (f32[1536]{0:T(1024)S(1)}, f32[1536]{0:T(1024)}, u32[]{:S(2)}) copy-start(f32[1536]{0:T(1024)} %embed_b.1) | copy-start | bytes 18436
  80.0 5.7 %copy-start.6 = (f32[1,1536]{1,0:T(1,128)S(1)}, f32[1,1536]{1,0:T(1,128)}, u32[]{:S(2)}) copy-start(f32[1,1536]{1,0:T(1,128)} %refs_3_.5) | copy-start | bytes 18436
  80.0 5.7 %copy-start.7 = (s32[2,8]{1,0:T(2,128)S(1)}, s32[2,8]{1,0:T(2,128)}, u32[]{:S(2)}) copy-start(s32[2,8]{1,0:T(2,128)} %lengths.1) | copy-start | bytes 196
  80.0 5.7 %copy-start.8 = (s32[2]{0:T(128)S(1)}, s32[2]{0:T(128)}, u32[]{:S(2)}) copy-start(s32[2]{0:T(128)} %refs_1_.5) | copy-start | bytes 28
  80.0 5.7 %copy-start.9 = (f32[5]{0:T(128)S(1)}, f32[5]{0:T(128)}, u32[]{:S(2)}) copy-start(f32[5]{0:T(128)} %refs_2_.5) | copy-start | bytes 64
  80.0 5.7 %copy-start.10 = (f32[64]{0:T(128)S(1)}, f32[64]{0:T(128)}, u32[]{:S(2)}) copy-start(f32[64]{0:T(128)} %refs_7_.5) | copy-start | bytes 772
  93.2 12.5 %collective-permute-start.13 = (bf16[48,1664]{1,0:T(8,128)(2,1)S(1)}, bf16[48,1664]{1,0:T(8,128)(2,1)S(1)}, u32[]{:S(2)}, u32[]{:S(2)}) collective-permute-start(bf16[48,1664]{1,0:T(8,128)(2,1)S(1)} %get-tuple-element.50), channel_id=1, source_target_pairs={{0,16},{16,32},{32,48},{48,64},{64,80},{80,96},{96,112},{112,128},... | collective-permute-start | bytes 479240 | tf_op jit(solution)/shard_map/ppermute | solution.py:39
  111.8 9.3 %collective-permute-start.14 = (bf16[48,1664]{1,0:T(8,128)(2,1)S(1)}, bf16[48,1664]{1,0:T(8,128)(2,1)S(1)}, u32[]{:S(2)}, u32[]{:S(2)}) collective-permute-start(bf16[48,1664]{1,0:T(8,128)(2,1)S(1)} %get-tuple-element.54), channel_id=1, source_target_pairs={{0,16},{16,32},{32,48},{48,64},{64,80},{80,96},{96,112},{112,128},... | collective-permute-start | bytes 479240 | tf_op jit(solution)/shard_map/ppermute | solution.py:39
  127.4 9.0 %collective-permute-start.15 = (bf16[48,1664]{1,0:T(8,128)(2,1)S(1)}, bf16[48,1664]{1,0:T(8,128)(2,1)S(1)}, u32[]{:S(2)}, u32[]{:S(2)}) collective-permute-start(bf16[48,1664]{1,0:T(8,128)(2,1)S(1)} %get-tuple-element.55), channel_id=1, source_target_pairs={{0,16},{16,32},{32,48},{48,64},{64,80},{80,96},{96,112},{112,128},... | collective-permute-start | bytes 479240 | tf_op jit(solution)/shard_map/ppermute | solution.py:39

commit v5 on v4

--- a/solution.py
+++ b/solution.py
@@ -43,26 +43,25 @@
     return lax.optimization_barrier(values)
 
 
-LOW, HIGH = 0, 1
 NEAR = [
-    [(0, 0, 0, LOW)],
-    [(0, 0, 0, HIGH)],
-    [(0, -1, 0, LOW)],
-    [(0, 1, 0, HIGH)],
-    [(1, 0, 0, LOW)],
-    [(1, 0, 0, HIGH)],
-    [(0, 2, 0, LOW)],
-    [(0, 2, 0, HIGH)],
+    [(0, 0, 0, 0, 3)],
+    [(0, 0, 0, 3, 3)],
+    [(0, -1, 0, 0, 3)],
+    [(0, 1, 0, 3, 3)],
+    [(1, 0, 0, 0, 3)],
+    [(1, 0, 0, 3, 3)],
+    [(0, 2, 0, 0, 3)],
+    [(0, 2, 0, 3, 3)],
 ]
-FAR = [[(1, 2, 0, LOW), (1, 2, 0, HIGH)]]
+FAR = [[(1, 2, 0, 0, 3), (1, 2, 0, 3, 3)], [(1, -1, 0, 0, 1), (1, 1, 0, 5, 1)]]
 LAST = [
-    [(0, -1, 0, HIGH), (1, -1, 0, LOW), (1, -1, 0, HIGH)],
-    [(0, 1, 0, LOW), (1, 1, 0, LOW), (1, 1, 0, HIGH)],
+    [(0, -1, 0, 3, 3), (1, -1, 0, 1, 5)],
+    [(0, 1, 0, 0, 3), (1, 1, 0, 0, 5)],
 ]
 
 
 def paired(pieces):
-    return [[(dx, dy, 1, half) for dx, dy, _, half in piece] for piece in pieces]
+    return [[(dx, dy, 1, first, tiles) for dx, dy, _, first, tiles in piece] for piece in pieces]
 
 
 def in_hbm(array):
@@ -74,12 +73,12 @@
 
 
 def place(rows, block):
-    dx, dy, dc, half = block
+    dx, dy, dc, first, _ = block
     device = lax.axis_index("dp")
     core = lax.rem(device % C + dc, C)
     y = lax.rem((device // C) % Y + dy + Y, Y)
     x = lax.rem(device // (C * Y) + dx, X)
-    return pl.multiple_of(((x * Y + y) * C + core) * rows + half * (rows // 2), TILE)
+    return pl.multiple_of(((x * Y + y) * C + core) * rows + first * TILE, TILE)
 
 
 def normalize(widened):
@@ -129,17 +128,19 @@
 
 
 def weight_copies(pieces, weights, rows, blocks, sems):
-    size = rows // 2
     found = []
     for piece, held in zip(pieces, blocks):
-        for at, block in enumerate(held):
+        start = 0
+        for block in held:
+            size = block[-1] * TILE
             found.append(
                 pltpu.make_async_copy(
-                    piece.at[pl.ds(at * size, size), :],
+                    piece.at[pl.ds(start, size), :],
                     weights.at[pl.ds(place(rows, block), size), :],
                     sems.at[len(found)],
                 )
             )
+            start += size
     return found
 
 
@@ -166,15 +167,18 @@
 
 def stack_kernel(stacks, count, *refs):
     pieces, targets, sems = refs[:count], refs[count:-1], refs[-1]
-    size = pieces[0].shape[0]
     copies = []
     for target, held in zip(targets, stacks):
-        for at, piece in enumerate(held):
+        start = 0
+        for piece, first, tiles in held:
             copies.append(
                 pltpu.make_async_copy(
-                    pieces[piece], target.at[pl.ds(at * size, size), :], sems.at[len(copies)]
+                    pieces[piece].at[pl.ds(first * TILE, tiles * TILE), :],
+                    target.at[pl.ds(start, tiles * TILE), :],
+                    sems.at[len(copies)],
                 )
             )
+            start += tiles * TILE
     run_copies(copies)
 
 
@@ -379,7 +383,8 @@
         return pl.pallas_call(
             functools.partial(stack_kernel, stacks, len(pieces)),
             out_shape=[
-                jax.ShapeDtypeStruct((len(held) * (part // 2), total), jnp.bfloat16) for held in stacks
+                jax.ShapeDtypeStruct((sum(tiles for *_, tiles in held) * TILE, total), jnp.bfloat16)
+                for held in stacks
             ],
             in_specs=[hbm] * len(pieces),
             out_specs=[hbm] * len(stacks),
@@ -413,9 +418,19 @@
     across_low, across_high = moved(low, 1, 0, 0), moved(high, 1, 0, 0)
     far_low, far_high = moved(below_low, 0, 1, 0), moved(above_high, 0, -1, 0)
     near = [low, high, below_low, above_high, across_low, across_high, far_low, far_high]
-    near_pair, up, down, far = stacked(near, [list(range(8)), [1, 4, 5], [0, 4, 5], [6, 7]])
+    near_pair, up, down, far, side = stacked(
+        near,
+        [
+            [(piece, 0, 3) for piece in range(len(near))],
+            [(1, 0, 3), (4, 1, 2), (5, 0, 3)],
+            [(0, 0, 3), (4, 0, 3), (5, 0, 2)],
+            [(6, 0, 3), (7, 0, 3)],
+            [(2, 0, 1), (3, 2, 1)],
+        ],
+    )
     near_pair = pair(near_pair)
-    up, down, far = moved(up, 0, 1, 0), moved(down, 0, -1, 0), moved(far, 1, 0, 0)
+    up, down = moved(up, 0, 1, 0), moved(down, 0, -1, 0)
+    far, side = moved(far, 1, 0, 0), moved(side, 1, 0, 0)
     weights, keys, values = loaded(
         "near",
         None,
@@ -423,10 +438,10 @@
         NEAR + [[block for piece in paired(NEAR) for block in piece]],
         [keys, values],
     )
-    keys, far = joined(keys, far)
-    far_pair = pair(far)
-    up, down, far_pair = joined(up, down, far_pair)
-    weights, latents = loaded("far", weights, [far, far_pair], FAR + paired(FAR), [latents])
+    keys, far, side = joined(keys, far, side)
+    far_pair, side_pair = pair(far), pair(side)
+    up, down, far_pair, side_pair = joined(up, down, far_pair, side_pair)
+    weights, latents = loaded("far", weights, [far, side, far_pair, side_pair], FAR + paired(FAR), [latents])
     last = [up, down]
     last += [pair(piece) for piece in last]
 

time: 138 us -> 135 us (0.978)
  waiting for transfers between devices: 93.5 us -> 88.4 us
  Pallas kernels: 29.5 us -> 31.1 us
    ppermute x13 -> x15, waiting for transfers between devices: 64.9 us -> 59.5 us  [moved(): return lax.ppermute(value, 'dp', pairs)]
    ppermute x13 -> x15, starting transfers between devices: 11.7 us -> 12.3 us  [moved(): return lax.ppermute(value, 'dp', pairs)]
  transfers between devices with their start and end apart: 16 -> 18, of which waited for: 14 -> 15; matrix products, arithmetic and copies ran while one was open for 0% -> 0% of each run, Pallas kernels for 4% -> 4%
where the time goes in v5:
time: 135 us
  waiting for transfers between devices  88.4 us (65%)
  Pallas kernels  31.1 us (23%)
  starting transfers between devices  14.7 us (11%)
    ppermute x15, waiting for transfers between devices, moved(): return lax.ppermute(value, 'dp', pairs)  59.5 us
    ppermute x3, waiting for transfers between devices, shifted(): return lax.ppermute(value, 'phase', pairs)  28.9 us
    pallas_call x3, Pallas kernels, shards(): pl.pallas_call(functools.partial(tick_kernel, tick, sections, first, part...  20 us
    ppermute x15, starting transfers between devices, moved(): return lax.ppermute(value, 'dp', pairs)  12.3 us
    pallas_call x2, Pallas kernels, loaded(): pl.pallas_call(functools.partial(load_kernel, part, first, blocks, len(pi...  5.69 us
    pallas_call x1, Pallas kernels, stacked(): pl.pallas_call(functools.partial(stack_kernel, stacks, len(pieces)), out_...  2.74 us
  transfers between devices with their start and end apart: 18, of which 15 were waited for; matrix products, arithmetic and copies ran while one was open for 0% of the time, Pallas kernels for 4%

profile of v5, /device:TPU:24, one launch (start us, length us, event | category | flops | bytes accessed | tf_op | source)
XLA Modules:
  0.0 135.1 jit_solution(4557470579996720447)
XLA Ops:
  0.6 1.3 own.1
  1.9 2.0 %collective-permute-start = (bf16[48,6144]{1,0:T(8,128)(2,1)S(1)}, bf16[48,6144]{1,0:T(8,128)(2,1)S(1)}, u32[]{:S(2)}, u32[]{:S(2)}) collective-permute-start(bf16[48,6144]{1,0:T(8,128)(2,1)S(1)} %get-tuple-element.35.refs_0_), channel_id=1, source_target_pairs={{0,2},{1,3},{2,4},{3,5},{4,6},{5,7},{6,0},{7,1},{8,10},{9,11},{10,... | collective-permute-start | bytes 1769480 | tf_op jit(solution)/shard_map/ppermute | solution.py:33
  4.0 1.5 %collective-permute-start.2 = (bf16[48,6144]{1,0:T(8,128)(2,1)S(1)}, bf16[48,6144]{1,0:T(8,128)(2,1)S(1)}, u32[]{:S(2)}, u32[]{:S(2)}) collective-permute-start(bf16[48,6144]{1,0:T(8,128)(2,1)S(1)} %get-tuple-element.35.refs_0_), channel_id=1, source_target_pairs={{0,8},{1,9},{2,10},{3,11},{4,12},{5,13},{6,14},{7,15},{8,0},{9,1},... | collective-permute-start | bytes 1769480 | tf_op jit(solution)/shard_map/ppermute | solution.py:33
  5.5 0.5 collective-permute-start.3
  6.1 11.0 %collective-permute-done.refs_2_ = bf16[48,6144]{1,0:T(8,128)(2,1)S(1)} collective-permute-done((bf16[48,6144]{1,0:T(8,128)(2,1)S(1)}, bf16[48,6144]{1,0:T(8,128)(2,1)S(1)}, u32[]{:S(2)}, u32[]{:S(2)}) %collective-permute-start) | collective-permute-done | bytes 589856 | tf_op jit(solution)/shard_map/ppermute | solution.py:33
  17.1 1.5 %collective-permute-start.4 = (bf16[48,6144]{1,0:T(8,128)(2,1)S(1)}, bf16[48,6144]{1,0:T(8,128)(2,1)S(1)}, u32[]{:S(2)}, u32[]{:S(2)}) collective-permute-start(bf16[48,6144]{1,0:T(8,128)(2,1)S(1)} %collective-permute-done.refs_2_), channel_id=1, source_target_pairs={{0,2},{1,3},{2,4},{3,5},{4,6},{5,7},{6,0},{7,1},{8,10},{9,11},{10,... | collective-permute-start | bytes 1769480 | tf_op jit(solution)/shard_map/ppermute | solution.py:33
  18.6 0.5 collective-permute-start.5
  19.1 1.2 collective-permute-done.2.refs_4_
  20.3 10.9 %collective-permute-done.3.refs_5_ = bf16[48,6144]{1,0:T(8,128)(2,1)S(1)} collective-permute-done((bf16[48,6144]{1,0:T(8,128)(2,1)S(1)}, bf16[48,6144]{1,0:T(8,128)(2,1)S(1)}, u32[]{:S(2)}, u32[]{:S(2)}) %collective-permute-start.3) | collective-permute-done | bytes 589856 | tf_op jit(solution)/shard_map/ppermute | solution.py:33
  31.3 1.2 collective-permute-done.5.refs_7_
  32.5 2.7 %stack.1 = (bf16[384,6144]{1,0:T(8,128)(2,1)S(1)}, bf16[128,6144]{1,0:T(8,128)(2,1)S(1)}, bf16[128,6144]{1,0:T(8,128)(2,1)S(1)}, bf16[96,6144]{1,0:T(8,128)(2,1)S(1)}, bf16[32,6144]{1,0:T(8,128)(2,1)S(1)}) custom-call(bf16[48,6144]{1,0:T(8,128)(2,1)S(1)} %get-tuple-element.35.refs_0_, bf16[48,6144]{1,0:T(8,128)(2,1)S(1)} %get-tuple-element.36.refs_1_, ...), custom_call_target="tpu_custom_call" | custom-call | tf_op jit(solution)/shard_map/stack/pallas_call | solution.py:383
  35.3 2.9 %collective-permute-start.7 = (bf16[96,6144]{1,0:T(8,128)(2,1)S(1)}, bf16[96,6144]{1,0:T(8,128)(2,1)S(1)}, u32[]{:S(2)}, u32[]{:S(2)}) collective-permute-start(bf16[96,6144]{1,0:T(8,128)(2,1)S(1)} %get-tuple-element.39), channel_id=1, source_target_pairs={{0,8},{1,9},{2,10},{3,11},{4,12},{5,13},{6,14},{7,15},{8,0},{9,1},... | collective-permute-start | bytes 3538952 | tf_op jit(solution)/shard_map/ppermute | solution.py:33
  38.6 1.7 %collective-permute-start.10 = (bf16[128,6144]{1,0:T(8,128)(2,1)S(1)}, bf16[128,6144]{1,0:T(8,128)(2,1)S(1)}, u32[]{:S(2)}, u32[]{:S(2)}) collective-permute-start(bf16[128,6144]{1,0:T(8,128)(2,1)S(1)} %get-tuple-element.47), channel_id=1, source_target_pairs={{0,6},{1,7},{2,0},{3,1},{4,2},{5,3},{6,4},{7,5},{8,14},{9,15},{10,... | collective-permute-start | bytes 4718600 | tf_op jit(solution)/shard_map/ppermute | solution.py:33
  40.3 2.9 %collective-permute-done.6.refs_8_ = bf16[384,6144]{1,0:T(8,128)(2,1)S(1)} collective-permute-done((bf16[384,6144]{1,0:T(8,128)(2,1)S(1)}, bf16[384,6144]{1,0:T(8,128)(2,1)S(1)}, u32[]{:S(2)}, u32[]{:S(2)}) %collective-permute-start.6) | collective-permute-done | bytes 4718624 | tf_op jit(solution)/shard_map/ppermute | solution.py:33
  43.2 4.0 %near.1 = (bf16[1536,6144]{1,0:T(8,128)(2,1)S(1)}, bf16[2,256,1536]{2,1,0:T(8,128)(2,1)}, bf16[2,256,1536]{2,1,0:T(8,128)(2,1)}) custom-call(bf16[48,6144]{1,0:T(8,128)(2,1)S(1)} %get-tuple-element.35.refs_0_, bf16[48,6144]{1,0:T(8,128)(2,1)S(1)} %get-tuple-element.36.refs_1_, bf16[48,6144]{1,0:T(8,128)(2,1)S(1)} %collective-permute-done.refs_2_, ...), custom_call_target="tpu_custom_call" | custom-call | tf_op jit(solution)/shard_map/near/pallas_call | solution.py:402
  47.3 25.9 %collective-permute-done.8.refs_2_ = bf16[32,6144]{1,0:T(8,128)(2,1)S(1)} collective-permute-done((bf16[32,6144]{1,0:T(8,128)(2,1)S(1)}, bf16[32,6144]{1,0:T(8,128)(2,1)S(1)}, u32[]{:S(2)}, u32[]{:S(2)}) %collective-permute-start.8) | collective-permute-done | bytes 393248 | tf_op jit(solution)/shard_map/ppermute | solution.py:33
  73.2 0.5 collective-permute-start.12
  73.7 1.0 collective-permute-done.9.refs_15_
  74.7 1.2 collective-permute-done.10.refs_16_
  75.9 0.7 collective-permute-done.12.refs_4_
  76.7 0.4 collective-permute-start.14
  77.2 1.7 %far.1 = (bf16[1536,6144]{1,0:T(8,128)(2,1)S(1)}, bf16[48,64]{1,0:T(8,128)(2,1)S(1)}) custom-call(bf16[1536,6144]{1,0:T(8,128)(2,1)S(1)} %get-tuple-element.43.refs_0_, bf16[96,6144]{1,0:T(8,128)(2,1)S(1)} %collective-permute-done.7.refs_1_, bf16[32,6144]{1,0:T(8,128)(2,1)S(1)} %collective-permute-done.8.refs_2_, ...), custom_call_target="tpu_custom_call", output_to_operand_aliasing={{0}: (0, {})} | custom-call | tf_op jit(solution)/shard_map/far/pallas_call | solution.py:402
  78.9 1.1 collective-permute-done.13.refs_17_
  80.0 2.2 %collective-permute-done.14.refs_18_ = bf16[128,6144]{1,0:T(8,128)(2,1)S(1)} collective-permute-done((bf16[128,6144]{1,0:T(8,128)(2,1)S(1)}, bf16[128,6144]{1,0:T(8,128)(2,1)S(1)}, u32[]{:S(2)}, u32[]{:S(2)}) %collective-permute-start.14) | collective-permute-done | bytes 1572896 | tf_op jit(solution)/shard_map/ppermute | solution.py:33
  82.3 7.7 %tick0.1 = (bf16[2,256,1536]{2,1,0:T(8,128)(2,1)}, bf16[2,256,1536]{2,1,0:T(8,128)(2,1)}, bf16[1536,6144]{1,0:T(8,128)(2,1)S(1)}, bf16[48,1664]{1,0:T(8,128)(2,1)S(1)}) custom-call(s32[2,8]{1,0:T(2,128)S(1)} %copy-done.7, s32[2]{0:T(128)S(1)} %copy-done.8, f32[5]{0:T(128)S(1)} %copy-done.9, ...), custom_call_target="tpu_custom_call", output_to_operand_aliasing={{0}: (10, {}), {1}: (11, {}), {2}: (14, {})} | custom-call | tf_op jit(solution)/shard_map/tick0/pallas_call | solution.py:480
  90.0 2.3 %collective-permute-start.15 = (bf16[48,1664]{1,0:T(8,128)(2,1)S(1)}, bf16[48,1664]{1,0:T(8,128)(2,1)S(1)}, u32[]{:S(2)}, u32[]{:S(2)}) collective-permute-start(bf16[48,1664]{1,0:T(8,128)(2,1)S(1)} %get-tuple-element.56), channel_id=1, source_target_pairs={{0,16},{16,32},{32,48},{48,64},{64,80},{80,96},{96,112},{112,128},... | collective-permute-start | bytes 479240 | tf_op jit(solution)/shard_map/ppermute | solution.py:39
  92.3 10.8 %collective-permute-done.15.refs_12_ = bf16[48,1664]{1,0:T(8,128)(2,1)S(1)} collective-permute-done((bf16[48,1664]{1,0:T(8,128)(2,1)S(1)}, bf16[48,1664]{1,0:T(8,128)(2,1)S(1)}, u32[]{:S(2)}, u32[]{:S(2)}) %collective-permute-start.15) | collective-permute-done | bytes 159776 | tf_op jit(solution)/shard_map/ppermute | solution.py:39
  103.1 6.0 %tick1.1 = (bf16[2,256,1536]{2,1,0:T(8,128)(2,1)}, bf16[2,256,1536]{2,1,0:T(8,128)(2,1)}, bf16[48,1664]{1,0:T(8,128)(2,1)S(1)}) custom-call(s32[2,8]{1,0:T(2,128)S(1)} %copy-done.7, s32[2]{0:T(128)S(1)} %copy-done.8, f32[5]{0:T(128)S(1)} %copy-done.9, f32[1,1536]{1,0:T(1,128)S(1)} %copy-done.6, ...), custom_call_target="tpu_custom_call", output_to_operand_aliasing={{0}: (10, {}), {1}: (11, {})} | custom-call | tf_op jit(solution)/shard_map/tick1/pallas_call | solution.py:480
  109.3 9.2 %collective-permute-done.16.refs_12_ = bf16[48,1664]{1,0:T(8,128)(2,1)S(1)} collective-permute-done((bf16[48,1664]{1,0:T(8,128)(2,1)S(1)}, bf16[48,1664]{1,0:T(8,128)(2,1)S(1)}, u32[]{:S(2)}, u32[]{:S(2)}) %collective-permute-start.16) | collective-permute-done | bytes 159776 | tf_op jit(solution)/shard_map/ppermute | solution.py:39
  118.5 6.2 %tick2.1 = (bf16[2,256,1536]{2,1,0:T(8,128)(2,1)}, bf16[2,256,1536]{2,1,0:T(8,128)(2,1)}, bf16[48,1664]{1,0:T(8,128)(2,1)S(1)}) custom-call(s32[2,8]{1,0:T(2,128)S(1)} %copy-done.7, s32[2]{0:T(128)S(1)} %copy-done.8, f32[5]{0:T(128)S(1)} %copy-done.9, f32[1,1536]{1,0:T(1,128)S(1)} %copy-done.6, ...), custom_call_target="tpu_custom_call", output_to_operand_aliasing={{0}: (10, {}), {1}: (11, {})} | custom-call | tf_op jit(solution)/shard_map/tick2/pallas_call | solution.py:480
  124.8 8.9 %collective-permute-done.17.received = bf16[48,1664]{1,0:T(8,128)(2,1)S(1)} collective-permute-done((bf16[48,1664]{1,0:T(8,128)(2,1)S(1)}, bf16[48,1664]{1,0:T(8,128)(2,1)S(1)}, u32[]{:S(2)}, u32[]{:S(2)}) %collective-permute-start.17) | collective-permute-done | bytes 159776 | tf_op jit(solution)/shard_map/ppermute | solution.py:39
  133.7 1.4 %final.1 = (bf16[48,1536]{1,0:T(8,128)(2,1)}, bf16[48,64]{1,0:T(8,128)(2,1)}) custom-call(s32[2,8]{1,0:T(2,128)S(1)} %copy-done.7, bf16[64,1536]{1,0:T(8,128)(2,1)S(1)} %copy-done.2, f32[1536]{0:T(1024)S(1)} %copy-done.5, bf16[48,1664]{1,0:T(8,128)(2,1)S(1)} %collective-permute-done.17.received), custom_call_target="tpu_custom_call" | custom-call | tf_op jit(solution)/shard_map/final/pallas_call | solution.py:496
  (34 shorter events, 1.0 us)
Async XLA Ops:
  1.9 15.1 %collective-permute-start = (bf16[48,6144]{1,0:T(8,128)(2,1)S(1)}, bf16[48,6144]{1,0:T(8,128)(2,1)S(1)}, u32[]{:S(2)}, u32[]{:S(2)}) collective-permute-start(bf16[48,6144]{1,0:T(8,128)(2,1)S(1)} %get-tuple-element.35.refs_0_), channel_id=1, source_target_pairs={{0,2},{1,3},{2,4},{3,5},{4,6},{5,7},{6,0},{7,1},{8,10},{9,11},{10,... | collective-permute-start | bytes 1769480 | tf_op jit(solution)/shard_map/ppermute | solution.py:33
  4.0 14.6 %collective-permute-start.1 = (bf16[48,6144]{1,0:T(8,128)(2,1)S(1)}, bf16[48,6144]{1,0:T(8,128)(2,1)S(1)}, u32[]{:S(2)}, u32[]{:S(2)}) collective-permute-start(bf16[48,6144]{1,0:T(8,128)(2,1)S(1)} %get-tuple-element.36.refs_1_), channel_id=1, source_target_pairs={{0,6},{1,7},{2,0},{3,1},{4,2},{5,3},{6,4},{7,5},{8,14},{9,15},{10,... | collective-permute-start | bytes 1769480 | tf_op jit(solution)/shard_map/ppermute | solution.py:33
  4.0 16.3 %collective-permute-start.2 = (bf16[48,6144]{1,0:T(8,128)(2,1)S(1)}, bf16[48,6144]{1,0:T(8,128)(2,1)S(1)}, u32[]{:S(2)}, u32[]{:S(2)}) collective-permute-start(bf16[48,6144]{1,0:T(8,128)(2,1)S(1)} %get-tuple-element.35.refs_0_), channel_id=1, source_target_pairs={{0,8},{1,9},{2,10},{3,11},{4,12},{5,13},{6,14},{7,15},{8,0},{9,1},... | collective-permute-start | bytes 1769480 | tf_op jit(solution)/shard_map/ppermute | solution.py:33
  5.5 25.7 %collective-permute-start.3 = (bf16[48,6144]{1,0:T(8,128)(2,1)S(1)}, bf16[48,6144]{1,0:T(8,128)(2,1)S(1)}, u32[]{:S(2)}, u32[]{:S(2)}) collective-permute-start(bf16[48,6144]{1,0:T(8,128)(2,1)S(1)} %get-tuple-element.36.refs_1_), channel_id=1, source_target_pairs={{0,8},{1,9},{2,10},{3,11},{4,12},{5,13},{6,14},{7,15},{8,0},{9,1},... | collective-permute-start | bytes 1769480 | tf_op jit(solution)/shard_map/ppermute | solution.py:33
  17.1 14.2 %collective-permute-start.4 = (bf16[48,6144]{1,0:T(8,128)(2,1)S(1)}, bf16[48,6144]{1,0:T(8,128)(2,1)S(1)}, u32[]{:S(2)}, u32[]{:S(2)}) collective-permute-start(bf16[48,6144]{1,0:T(8,128)(2,1)S(1)} %collective-permute-done.refs_2_), channel_id=1, source_target_pairs={{0,2},{1,3},{2,4},{3,5},{4,6},{5,7},{6,0},{7,1},{8,10},{9,11},{10,... | collective-permute-start | bytes 1769480 | tf_op jit(solution)/shard_map/ppermute | solution.py:33
  18.6 13.9 %collective-permute-start.5 = (bf16[48,6144]{1,0:T(8,128)(2,1)S(1)}, bf16[48,6144]{1,0:T(8,128)(2,1)S(1)}, u32[]{:S(2)}, u32[]{:S(2)}) collective-permute-start(bf16[48,6144]{1,0:T(8,128)(2,1)S(1)} %collective-permute-done.1.refs_3_), channel_id=1, source_target_pairs={{0,6},{1,7},{2,0},{3,1},{4,2},{5,3},{6,4},{7,5},{8,14},{9,15},{10,... | collective-permute-start | bytes 1769480 | tf_op jit(solution)/shard_map/ppermute | solution.py:33
  35.2 8.0 %collective-permute-start.6 = (bf16[384,6144]{1,0:T(8,128)(2,1)S(1)}, bf16[384,6144]{1,0:T(8,128)(2,1)S(1)}, u32[]{:S(2)}, u32[]{:S(2)}) collective-permute-start(bf16[384,6144]{1,0:T(8,128)(2,1)S(1)} %get-tuple-element.37), channel_id=1, source_target_pairs={{0,1},{1,0},{2,3},{3,2},{4,5},{5,4},{6,7},{7,6},{8,9},{9,8},{10,11... | collective-permute-start | bytes 14155784 | tf_op jit(solution)/shard_map/ppermute | solution.py:33
  35.3 37.8 %collective-permute-start.7 = (bf16[96,6144]{1,0:T(8,128)(2,1)S(1)}, bf16[96,6144]{1,0:T(8,128)(2,1)S(1)}, u32[]{:S(2)}, u32[]{:S(2)}) collective-permute-start(bf16[96,6144]{1,0:T(8,128)(2,1)S(1)} %get-tuple-element.39), channel_id=1, source_target_pairs={{0,8},{1,9},{2,10},{3,11},{4,12},{5,13},{6,14},{7,15},{8,0},{9,1},... | collective-permute-start | bytes 3538952 | tf_op jit(solution)/shard_map/ppermute | solution.py:33
  38.2 35.0 %collective-permute-start.8 = (bf16[32,6144]{1,0:T(8,128)(2,1)S(1)}, bf16[32,6144]{1,0:T(8,128)(2,1)S(1)}, u32[]{:S(2)}, u32[]{:S(2)}) collective-permute-start(bf16[32,6144]{1,0:T(8,128)(2,1)S(1)} %get-tuple-element.40), channel_id=1, source_target_pairs={{0,8},{1,9},{2,10},{3,11},{4,12},{5,13},{6,14},{7,15},{8,0},{9,1},... | collective-permute-start | bytes 1179656 | tf_op jit(solution)/shard_map/ppermute | solution.py:33
  38.3 36.4 %collective-permute-start.9 = (bf16[128,6144]{1,0:T(8,128)(2,1)S(1)}, bf16[128,6144]{1,0:T(8,128)(2,1)S(1)}, u32[]{:S(2)}, u32[]{:S(2)}) collective-permute-start(bf16[128,6144]{1,0:T(8,128)(2,1)S(1)} %get-tuple-element.46), channel_id=1, source_target_pairs={{0,2},{1,3},{2,4},{3,5},{4,6},{5,7},{6,0},{7,1},{8,10},{9,11},{10,... | collective-permute-start | bytes 4718600 | tf_op jit(solution)/shard_map/ppermute | solution.py:33
  38.6 37.3 %collective-permute-start.10 = (bf16[128,6144]{1,0:T(8,128)(2,1)S(1)}, bf16[128,6144]{1,0:T(8,128)(2,1)S(1)}, u32[]{:S(2)}, u32[]{:S(2)}) collective-permute-start(bf16[128,6144]{1,0:T(8,128)(2,1)S(1)} %get-tuple-element.47), channel_id=1, source_target_pairs={{0,6},{1,7},{2,0},{3,1},{4,2},{5,3},{6,4},{7,5},{8,14},{9,15},{10,... | collective-permute-start | bytes 4718600 | tf_op jit(solution)/shard_map/ppermute | solution.py:33
  73.2 3.4 %collective-permute-start.11 = (bf16[96,6144]{1,0:T(8,128)(2,1)S(1)}, bf16[96,6144]{1,0:T(8,128)(2,1)S(1)}, u32[]{:S(2)}, u32[]{:S(2)}) collective-permute-start(bf16[96,6144]{1,0:T(8,128)(2,1)S(1)} %collective-permute-done.7.refs_1_), channel_id=1, source_target_pairs={{0,1},{1,0},{2,3},{3,2},{4,5},{5,4},{6,7},{7,6},{8,9},{9,8},{10,11... | collective-permute-start | bytes 3538952 | tf_op jit(solution)/shard_map/ppermute | solution.py:33
  73.2 3.4 %collective-permute-start.12 = (bf16[32,6144]{1,0:T(8,128)(2,1)S(1)}, bf16[32,6144]{1,0:T(8,128)(2,1)S(1)}, u32[]{:S(2)}, u32[]{:S(2)}) collective-permute-start(bf16[32,6144]{1,0:T(8,128)(2,1)S(1)} %collective-permute-done.8.refs_2_), channel_id=1, source_target_pairs={{0,1},{1,0},{2,3},{3,2},{4,5},{5,4},{6,7},{7,6},{8,9},{9,8},{10,11... | collective-permute-start | bytes 1179656 | tf_op jit(solution)/shard_map/ppermute | solution.py:33
  76.6 3.4 %collective-permute-start.13 = (bf16[128,6144]{1,0:T(8,128)(2,1)S(1)}, bf16[128,6144]{1,0:T(8,128)(2,1)S(1)}, u32[]{:S(2)}, u32[]{:S(2)}) collective-permute-start(bf16[128,6144]{1,0:T(8,128)(2,1)S(1)} %collective-permute-done.9.refs_15_), channel_id=1, source_target_pairs={{0,1},{1,0},{2,3},{3,2},{4,5},{5,4},{6,7},{7,6},{8,9},{9,8},{10,11... | collective-permute-start | bytes 4718600 | tf_op jit(solution)/shard_map/ppermute | solution.py:33
  76.7 5.5 %collective-permute-start.14 = (bf16[128,6144]{1,0:T(8,128)(2,1)S(1)}, bf16[128,6144]{1,0:T(8,128)(2,1)S(1)}, u32[]{:S(2)}, u32[]{:S(2)}) collective-permute-start(bf16[128,6144]{1,0:T(8,128)(2,1)S(1)} %collective-permute-done.10.refs_16_), channel_id=1, source_target_pairs={{0,1},{1,0},{2,3},{3,2},{4,5},{5,4},{6,7},{7,6},{8,9},{9,8},{10,11... | collective-permute-start | bytes 4718600 | tf_op jit(solution)/shard_map/ppermute | solution.py:33
  77.1 5.2 %copy-start = (bf16[1,2,256,1536]{3,2,1,0:T(8,128)(2,1)S(1)}, bf16[1,2,256,1536]{3,2,1,0:T(8,128)(2,1)}, u32[]{:S(2)}) copy-start(bf16[1,2,256,1536]{3,2,1,0:T(8,128)(2,1)} %param.20) | copy-start | bytes 4718596
  77.1 5.2 %copy-start.1 = (bf16[1,2,256,1536]{3,2,1,0:T(8,128)(2,1)S(1)}, bf16[1,2,256,1536]{3,2,1,0:T(8,128)(2,1)}, u32[]{:S(2)}) copy-start(bf16[1,2,256,1536]{3,2,1,0:T(8,128)(2,1)} %param.21) | copy-start | bytes 4718596
  77.1 5.2 %copy-start.2 = (bf16[64,1536]{1,0:T(8,128)(2,1)S(1)}, bf16[64,1536]{1,0:T(8,128)(2,1)}, u32[]{:S(2)}) copy-start(bf16[64,1536]{1,0:T(8,128)(2,1)} %embed_w.1) | copy-start | bytes 589828
  77.1 5.2 %copy-start.3 = (bf16[1536,64]{0,1:T(8,128)(2,1)S(1)}, bf16[1536,64]{0,1:T(8,128)(2,1)}, u32[]{:S(2)}) copy-start(bf16[1536,64]{0,1:T(8,128)(2,1)} %param.27) | copy-start | bytes 589828
  77.1 5.2 %copy-start.4 = (bf16[1,1,48,1536]{3,2,1,0:T(8,128)(2,1)S(1)}, bf16[1,1,48,1536]{3,2,1,0:T(8,128)(2,1)}, u32[]{:S(2)}) copy-start(bf16[1,1,48,1536]{3,2,1,0:T(8,128)(2,1)} %param.16) | copy-start | bytes 442372
  77.1 5.2 %copy-start.5 = (f32[1536]{0:T(1024)S(1)}, f32[1536]{0:T(1024)}, u32[]{:S(2)}) copy-start(f32[1536]{0:T(1024)} %embed_b.1) | copy-start | bytes 18436
  77.1 5.2 %copy-start.6 = (f32[1,1536]{1,0:T(1,128)S(1)}, f32[1,1536]{1,0:T(1,128)}, u32[]{:S(2)}) copy-start(f32[1,1536]{1,0:T(1,128)} %refs_3_.5) | copy-start | bytes 18436
  77.1 5.2 %copy-start.7 = (s32[2,8]{1,0:T(2,128)S(1)}, s32[2,8]{1,0:T(2,128)}, u32[]{:S(2)}) copy-start(s32[2,8]{1,0:T(2,128)} %lengths.1) | copy-start | bytes 196
  77.2 5.2 %copy-start.8 = (s32[2]{0:T(128)S(1)}, s32[2]{0:T(128)}, u32[]{:S(2)}) copy-start(s32[2]{0:T(128)} %refs_1_.5) | copy-start | bytes 28
  77.2 5.2 %copy-start.9 = (f32[5]{0:T(128)S(1)}, f32[5]{0:T(128)}, u32[]{:S(2)}) copy-start(f32[5]{0:T(128)} %refs_2_.5) | copy-start | bytes 64
  77.2 5.1 %copy-start.10 = (f32[64]{0:T(128)S(1)}, f32[64]{0:T(128)}, u32[]{:S(2)}) copy-start(f32[64]{0:T(128)} %refs_7_.5) | copy-start | bytes 772
  90.0 13.1 %collective-permute-start.15 = (bf16[48,1664]{1,0:T(8,128)(2,1)S(1)}, bf16[48,1664]{1,0:T(8,128)(2,1)S(1)}, u32[]{:S(2)}, u32[]{:S(2)}) collective-permute-start(bf16[48,1664]{1,0:T(8,128)(2,1)S(1)} %get-tuple-element.56), channel_id=1, source_target_pairs={{0,16},{16,32},{32,48},{48,64},{64,80},{80,96},{96,112},{112,128},... | collective-permute-start | bytes 479240 | tf_op jit(solution)/shard_map/ppermute | solution.py:39
  109.2 9.3 %collective-permute-start.16 = (bf16[48,1664]{1,0:T(8,128)(2,1)S(1)}, bf16[48,1664]{1,0:T(8,128)(2,1)S(1)}, u32[]{:S(2)}, u32[]{:S(2)}) collective-permute-start(bf16[48,1664]{1,0:T(8,128)(2,1)S(1)} %get-tuple-element.60), channel_id=1, source_target_pairs={{0,16},{16,32},{32,48},{48,64},{64,80},{80,96},{96,112},{112,128},... | collective-permute-start | bytes 479240 | tf_op jit(solution)/shard_map/ppermute | solution.py:39
  124.7 9.0 %collective-permute-start.17 = (bf16[48,1664]{1,0:T(8,128)(2,1)S(1)}, bf16[48,1664]{1,0:T(8,128)(2,1)S(1)}, u32[]{:S(2)}, u32[]{:S(2)}) collective-permute-start(bf16[48,1664]{1,0:T(8,128)(2,1)S(1)} %get-tuple-element.61), channel_id=1, source_target_pairs={{0,16},{16,32},{32,48},{48,64},{64,80},{80,96},{96,112},{112,128},... | collective-permute-start | bytes 479240 | tf_op jit(solution)/shard_map/ppermute | solution.py:39
